TPU v7x, 128 devices: a whole 4x4x4 slice. The times are simulated.
128 devices in a mesh: lon: 32 (over y, z, x_lo), lat: 4 (over x_hi, core).
Axes of the slice: x: 4 (x_hi: 2, x_lo: 2; x = x_hi * 2 + x_lo), y: 4, z: 4, core: 2. Of those that a mesh axis runs over, the one named last changes fastest.
Arguments:
- adjoint_final: float32 [75, 32, 8192], P(None, 'lat', 'lon'), may hold values from -6 to 6
- vert_inverse: bfloat16 [75, 75, 32, 8192], P(None, None, 'lat', 'lon'), may hold values from -0.36 to 1
- speed_east: bfloat16 [75, 32, 8192], P(None, 'lat', 'lon'), may hold values from -0.3984375 to 0.3984375
- mixing_east: bfloat16 [75, 32, 8192], P(None, 'lat', 'lon'), may hold values from 0.019897461 to 0.119628906
- speed_north: bfloat16 [75, 32, 8192], P(None, 'lat', 'lon'), may hold values from -0.3984375 to 0.3984375
- mixing_north: bfloat16 [75, 32, 8192], P(None, 'lat', 'lon'), may hold values from 0.019897461 to 0.119628906
- depth_levels: int32 [32, 8192], P('lat', 'lon'), may hold values from 0 to 75
- fold_block: int32 [32], replicated, may hold values from 0 to 31, as said below
Outputs:
- adjoint_initial: float32 [75, 32, 8192], P(None, 'lat', 'lon')
Inputs may be any that keep to these rules, and one draw needn't show every extreme that they name: fold_block pairs the longitude blocks: fold_block[fold_block[b]] = b and fold_block[b] != b.
All inputs are finite; a program needn't handle non-finite values.
Results may differ from a plain program's by a relative error of at most 0.0005.
Values may be sent and summed in bfloat16 or wider, within the bound.
No kernel may reach another device: no remote copies, remote signals or barrier semaphores. Data moves between devices by JAX's collectives and lax.ppermute only.
A program may use at most 128 MiB of HBM per device.

v0:
```python
import jax
import jax.numpy as jnp
from jax import lax
from jax.sharding import PartitionSpec as P

STEPS = 2


def extended_2(block, sides, width, periodic):
    for axis, dim in sides:
        count = lax.axis_size(axis)
        forward = [(i, i + 1) for i in range(count - 1)]
        if periodic:
            forward.append((count - 1, 0))
        backward = [(target, source) for source, target in forward]
        low = lax.ppermute(
            lax.slice_in_dim(block, block.shape[dim] - width, None, axis=dim), axis, forward
        )
        high = lax.ppermute(lax.slice_in_dim(block, 0, width, axis=dim), axis, backward)
        block = jnp.concatenate([low, block, high], axis=dim)
    return block


def passed_along(block, axis, distance):
    devices = range(lax.axis_size(axis))
    route = [((i - distance) % len(devices), i) for i in devices]
    return lax.ppermute(block, axis, route)


def from_behind(block, axis, distance):
    devices = range(lax.axis_size(axis))
    route = [(i - distance, i) for i in devices if i - distance in devices]
    return lax.ppermute(block, axis, route)


def face_flux(strip_cells, speed_face, mixing, flux_axis):
    cell_count = strip_cells.shape[flux_axis]
    far_low = lax.slice_in_dim(strip_cells, 0, cell_count - 3, axis=flux_axis)
    near_low = lax.slice_in_dim(strip_cells, 1, cell_count - 2, axis=flux_axis)
    near_high = lax.slice_in_dim(strip_cells, 2, cell_count - 1, axis=flux_axis)
    far_high = lax.slice_in_dim(strip_cells, 3, cell_count, axis=flux_axis)
    return speed_face * (7.0 * (near_low + near_high) - far_low - far_high) / 12.0 - mixing * (
        near_high - near_low
    )


def local_horizontal(extended, wet_mask, speed_x, mixing_x, speed_y, mixing_y):
    flux_x = face_flux(extended[:, 2:-2, :], speed_x, mixing_x, 2)
    flux_y = face_flux(extended[:, :, 2:-2], speed_y, mixing_y, 1)
    centre = extended[:, 2:-2, 2:-2]
    return wet_mask * (
        centre - (flux_x[:, :, 1:] - flux_x[:, :, :-1]) - (flux_y[:, 1:, :] - flux_y[:, :-1, :])
    )


def vertical_adjoint(inverse, weighted):
    return jnp.sum(inverse.astype(jnp.float32) * weighted[:, None], axis=0)


def carry_vertical(inverse, wet_mask, core_part, extras):
    return vertical_adjoint(inverse, wet_mask * (core_part + extras))


def adjoint_parts(projected, pullback, partner, is_top):
    cotangent_ext = pullback(projected)[0]
    row_count = cotangent_ext.shape[1] - 4
    col_count = cotangent_ext.shape[2] - 4
    core_part = cotangent_ext[:, 2:-2, 2:-2]
    side_rims = jnp.concatenate([cotangent_ext[:, :, :2], cotangent_ext[:, :, -2:]], axis=2)
    arrived_cols = extended_2(side_rims, (("lon", 2),), 2, True)
    column_add = jnp.pad(arrived_cols[:, :, :2], ((0, 0), (0, 0), (0, col_count - 2)))
    column_add = column_add + jnp.pad(arrived_cols[:, :, -2:], ((0, 0), (0, 0), (col_count - 2, 0)))
    south_rows = cotangent_ext[:, :2, 2:-2] + column_add[:, :2]
    north_rows = cotangent_ext[:, -2:, 2:-2] + column_add[:, -2:]
    edge_rows = jnp.concatenate([south_rows, north_rows * (1.0 - is_top)], axis=1)
    got_rows = extended_2(edge_rows.astype(jnp.bfloat16), (("lat", 1),), 2, False).astype(
        edge_rows.dtype
    )
    row_add = jnp.pad(got_rows[:, :2], ((0, 0), (0, row_count - 2), (0, 0)))
    row_add = row_add + jnp.pad(got_rows[:, -2:], ((0, 0), (row_count - 2, 0), (0, 0)))
    folded = north_rows * is_top
    shard_piece = lax.all_gather(folded.astype(jnp.bfloat16), "lon", axis=2, tiled=True).astype(
        jnp.float32
    )
    piece_width = shard_piece.shape[2]
    column_index = lax.iota(jnp.int32, col_count) + partner * col_count
    inside_mask = (column_index >= 0) & (column_index < piece_width)
    picked = jnp.take(shard_piece, jnp.clip(column_index, 0, piece_width - 1), axis=2)
    received = jnp.zeros(folded.shape, jnp.float32) + jnp.where(
        inside_mask[None, None, :], picked, 0.0
    )
    mirrored = jnp.flip(received, axis=2)
    fold_add = jnp.pad(
        jnp.stack([mirrored[:, 1], mirrored[:, 0]], axis=1), ((0, 0), (row_count - 3, 1), (0, 0))
    )
    extras = column_add[:, 2:-2] + row_add + fold_add
    return (core_part, extras)


def per_device(
    adjoint_final,
    vert_inverse,
    speed_east,
    mixing_east,
    speed_north,
    mixing_north,
    depth_levels,
    fold_block,
):
    levels = adjoint_final.shape[0]
    row_count = adjoint_final.shape[1]
    col_count = adjoint_final.shape[2]
    wet_mask = (lax.iota(jnp.int32, levels)[:, None, None] < depth_levels[None]).astype(jnp.float32)
    west_coef = passed_along(jnp.stack([speed_east[:, :, -1], mixing_east[:, :, -1]]), "lon", 1)
    south_coef = from_behind(jnp.stack([speed_north[:, -1, :], mixing_north[:, -1, :]]), "lat", 1)
    speed_x = jnp.concatenate([west_coef[0][:, :, None], speed_east], axis=2).astype(jnp.float32)
    mixing_x = jnp.concatenate([west_coef[1][:, :, None], mixing_east], axis=2).astype(jnp.float32)
    speed_y = jnp.concatenate([south_coef[0][:, None, :], speed_north], axis=1).astype(jnp.float32)
    mixing_y = jnp.concatenate([south_coef[1][:, None, :], mixing_north], axis=1).astype(
        jnp.float32
    )
    partner = fold_block[lax.axis_index("lon")]
    is_top = (lax.axis_index("lat") == lax.axis_size("lat") - 1).astype(jnp.float32)

    def operator(extended):
        return local_horizontal(extended, wet_mask, speed_x, mixing_x, speed_y, mixing_y)

    primal_out, pullback = jax.vjp(
        operator, jnp.zeros((levels, row_count + 4, col_count + 4), jnp.float32)
    )
    core_part = adjoint_final
    extras = jnp.zeros_like(adjoint_final)
    for turn_index in range(STEPS):
        if turn_index == 0:
            projected = vertical_adjoint(vert_inverse, wet_mask * adjoint_final)
        else:
            projected = carry_vertical(vert_inverse, wet_mask, core_part, extras)
        core_part, extras = adjoint_parts(projected, pullback, partner, is_top)
    return wet_mask * (core_part + extras)


def solution(mesh):
    return jax.shard_map(
        per_device,
        mesh=mesh,
        in_specs=(
            P(None, "lat", "lon"),
            P(None, None, "lat", "lon"),
            P(None, "lat", "lon"),
            P(None, "lat", "lon"),
            P(None, "lat", "lon"),
            P(None, "lat", "lon"),
            P("lat", "lon"),
            P(),
        ),
        out_specs=P(None, "lat", "lon"),
        check_vma=False,
    )
```

profile of v0, /device:TPU:0, one launch (start us, length us, event | category | flops | bytes accessed | tf_op | source)
XLA Modules:
  0.0 410.9 jit_solution(10976875660218082199)
XLA Ops:
  16.5 9.6 %fusion = f32[75,8,256]{2,1,0:T(8,128)S(1)} fusion(bf16[75,75,8,256]{3,2,1,0:T(8,128)(2,1)} %param.11, f32[75,8,256]{2,1,0:T(8,128)S(1)} %copy.89), kind=kLoop, calls=%fused_computation.4 | loop fusion | flops 34406400 | bytes 24268800 | tf_op jit(solution)/shard_map/reduce_sum | solution.py:57
  29.1 2.2 copy.94
  31.3 2.2 copy.96
  40.5 1.9 collective-permute-start.2
  42.4 4.4 %collective-permute-start.3 = (f32[75,12,2]{0,1,2:T(8,128)}, f32[75,12,2]{0,1,2:T(8,128)}, u32[]{:S(2)}, u32[]{:S(2)}) collective-permute-start(f32[75,12,2]{0,1,2:T(8,128)} %get-tuple-element.18), channel_id=1, source_target_pairs={{4,0},{8,4},{12,8},{16,12},{20,16},{24,20},{28,24},{32,28},{36,32}... | collective-permute-start | bytes 21608 | tf_op jit(solution)/shard_map/ppermute | solution.py:19
  46.8 1.9 collective-permute-done.2
  48.8 1.7 multiply_convert_fusion.3
  51.2 1.7 copy.101
  56.0 4.0 collective-permute-start.4
  61.7 3.3 pad_add_fusion.1
  65.9 125.1 %all-gather.3.cloned.1.call-done = bf16[75,2,8192]{2,1,0:T(2,128)(2,1)} async-done(((bf16[75,2,256]{2,1,0:T(2,128)(2,1)}), bf16[75,2,8192]{2,1,0:T(2,128)(2,1)}) %all-gather.3.cloned.1.call-update) | async-done | bytes 2457616 | tf_op jit(solution)/shard_map/all_gather | solution.py:82
  191.0 14.4 %copy.102 = f32[75,2,8192]{0,1,2:T(2,128)} copy(bf16[75,2,8192]{2,1,0:T(2,128)(2,1)} %all-gather.3.cloned.1.call-done) | data formatting | bytes 7372800 | tf_op jit(solution)/shard_map/convert_element_type | solution.py:82
  205.4 4.5 %gather_fusion = f32[256,75,2]{1,2,0:T(2,128)S(1)} fusion(f32[75,2,8192]{0,1,2:T(2,128)} %copy.102, s32[1024]{0:T(1024)} %pad_clamp_fusion), kind=kCustom, calls=%fused_computation.clone | custom fusion | bytes 308224 | tf_op jit(solution)/shard_map/jit(_take)/gather | solution.py:88
  211.7 3.0 fusion.6
  215.2 9.6 %fusion.1 = f32[75,8,256]{2,1,0:T(8,128)S(1)} fusion(bf16[75,75,8,256]{3,2,1,0:T(8,128)(2,1)} %param.11, f32[75,8,256]{2,1,0:T(8,128)S(1)} %copy.103), kind=kLoop, calls=%fused_computation.5 | loop fusion | flops 34406400 | bytes 24268800 | tf_op jit(solution)/shard_map/reduce_sum | solution.py:57
  230.1 5.7 %collective-permute-start.7 = (f32[75,12,2]{0,1,2:T(8,128)S(1)}, f32[75,12,2]{0,1,2:T(8,128)S(1)}, u32[]{:S(2)}, u32[]{:S(2)}) collective-permute-start(f32[75,12,2]{0,1,2:T(8,128)S(1)} %get-tuple-element.16), channel_id=1, source_target_pairs={{4,0},{8,4},{12,8},{16,12},{20,16},{24,20},{28,24},{32,28},{36,32}... | collective-permute-start | bytes 21608 | tf_op jit(solution)/shard_map/ppermute | solution.py:19
  235.8 1.7 collective-permute-done.6
  238.9 1.7 copy.105
  243.5 3.3 pad_add_fusion
  246.7 1.8 collective-permute-done.9
  249.5 129.5 %all-gather.5.cloned.1.call-done = bf16[75,2,8192]{2,1,0:T(2,128)(2,1)} async-done(((bf16[75,2,256]{2,1,0:T(2,128)(2,1)}), bf16[75,2,8192]{2,1,0:T(2,128)(2,1)}) %all-gather.5.cloned.1.call-update) | async-done | bytes 2457616 | tf_op jit(solution)/shard_map/all_gather | solution.py:82
  379.0 14.4 %copy.106 = f32[75,2,8192]{0,1,2:T(2,128)} copy(bf16[75,2,8192]{2,1,0:T(2,128)(2,1)} %all-gather.5.cloned.1.call-done) | data formatting | bytes 7372800 | tf_op jit(solution)/shard_map/convert_element_type | solution.py:82
  393.4 4.5 %gather_fusion.1 = f32[256,75,2]{1,2,0:T(2,128)S(1)} fusion(f32[75,2,8192]{0,1,2:T(2,128)} %copy.106, s32[1024]{0:T(1024)} %pad_clamp_fusion), kind=kCustom, calls=%fused_computation.1.clone | custom fusion | bytes 308224 | tf_op jit(solution)/shard_map/jit(_take)/gather | solution.py:88
  399.7 3.1 fusion.11
  (140 shorter events, 40.9 us)
Async XLA Ops:
  6.5 184.5 %all-gather.3.cloned.1.call-start = ((), (), s32[]{:S(2)}) async-start(), calls=%async_computation | async-start | bytes 2534400 | tf_op jit(solution)/shard_map/all_gather | solution.py:82
  9.7 23.8 %collective-permute-start.1 = (bf16[2,75,8]{1,2,0:T(8,128)(2,1)S(1)}, bf16[2,75,8]{1,2,0:T(8,128)(2,1)S(1)}, u32[]{:S(2)}, u32[]{:S(2)}) collective-permute-start(bf16[2,75,8]{1,2,0:T(8,128)(2,1)S(1)} %pad_maximum_fusion.5), channel_id=1, source_target_pairs={{124,0},{0,4},{4,8},{8,12},{12,16},{16,20},{20,24},{24,28},{28,32}... | collective-permute-start | bytes 7208 | tf_op jit(solution)/shard_map/ppermute | solution.py:27
  13.5 21.9 %collective-permute-start = (bf16[2,75,256]{2,1,0:T(8,128)(2,1)S(1)}, bf16[2,75,256]{2,1,0:T(8,128)(2,1)S(1)}, u32[]{:S(2)}, u32[]{:S(2)}) collective-permute-start(bf16[2,75,256]{2,1,0:T(8,128)(2,1)S(1)} %pad_maximum_fusion.4), channel_id=1, source_target_pairs={{0,1},{1,2},{2,3},{4,5},{5,6},{6,7},{8,9},{9,10},{10,11},{12,13},{... | collective-permute-start | bytes 230408 | tf_op jit(solution)/shard_map/ppermute | solution.py:33
  40.5 8.2 %collective-permute-start.2 = (f32[75,12,2]{0,1,2:T(8,128)}, f32[75,12,2]{0,1,2:T(8,128)S(1)}, u32[]{:S(2)}, u32[]{:S(2)}) collective-permute-start(f32[75,12,2]{0,1,2:T(8,128)} %get-tuple-element.19), channel_id=1, source_target_pairs={{0,4},{4,8},{8,12},{12,16},{16,20},{20,24},{24,28},{28,32},{32,36}... | collective-permute-start | bytes 21608 | tf_op jit(solution)/shard_map/ppermute | solution.py:16
  42.4 6.3 %collective-permute-start.3 = (f32[75,12,2]{0,1,2:T(8,128)}, f32[75,12,2]{0,1,2:T(8,128)}, u32[]{:S(2)}, u32[]{:S(2)}) collective-permute-start(f32[75,12,2]{0,1,2:T(8,128)} %get-tuple-element.18), channel_id=1, source_target_pairs={{4,0},{8,4},{12,8},{16,12},{20,16},{24,20},{28,24},{32,28},{36,32}... | collective-permute-start | bytes 21608 | tf_op jit(solution)/shard_map/ppermute | solution.py:19
  53.0 326.1 %all-gather.5.cloned.1.call-start = ((), (), s32[]{:S(2)}) async-start(), calls=%async_computation.1 | async-start | bytes 2534400 | tf_op jit(solution)/shard_map/all_gather | solution.py:82
  56.0 8.9 %collective-permute-start.4 = (bf16[75,2,256]{0,1,2:T(2,128)(2,1)}, bf16[75,2,256]{0,1,2:T(2,128)(2,1)S(1)}, u32[]{:S(2)}, u32[]{:S(2)}) collective-permute-start(bf16[75,2,256]{0,1,2:T(2,128)(2,1)} %get-tuple-element.10), channel_id=1, source_target_pairs={{0,1},{1,2},{2,3},{4,5},{5,6},{6,7},{8,9},{9,10},{10,11},{12,13},{... | collective-permute-start | bytes 230408 | tf_op jit(solution)/shard_map/ppermute | solution.py:16
  60.0 4.9 %collective-permute-start.5 = (bf16[75,2,256]{0,1,2:T(2,128)(2,1)}, bf16[75,2,256]{0,1,2:T(2,128)(2,1)S(1)}, u32[]{:S(2)}, u32[]{:S(2)}) collective-permute-start(bf16[75,2,256]{0,1,2:T(2,128)(2,1)} %get-tuple-element.15), channel_id=1, source_target_pairs={{1,0},{2,1},{3,2},{5,4},{6,5},{7,6},{9,8},{10,9},{11,10},{13,12},{... | collective-permute-start | bytes 230408 | tf_op jit(solution)/shard_map/ppermute | solution.py:19
  65.8 144.1 %copy-start.30 = (pred[256]{0:T(512)(128)(4,1)S(1)}, pred[256]{0:T(512)(128)(4,1)}, u32[]{:S(2)}) copy-start(pred[256]{0:T(512)(128)(4,1)} %get-tuple-element.44) | copy-start | bytes 772
  65.9 145.8 %copy-start.11 = (bf16[75,2,256]{0,1,2:T(2,128)(2,1)S(1)}, bf16[75,2,256]{0,1,2:T(2,128)(2,1)}, u32[]{:S(2)}) copy-start(bf16[75,2,256]{0,1,2:T(2,128)(2,1)} %get-tuple-element.10) | copy-start | bytes 230404
  65.9 145.8 %copy-start.13 = (bf16[75,2,256]{0,1,2:T(2,128)(2,1)S(1)}, bf16[75,2,256]{0,1,2:T(2,128)(2,1)}, u32[]{:S(2)}) copy-start(bf16[75,2,256]{0,1,2:T(2,128)(2,1)} %get-tuple-element.15) | copy-start | bytes 230404
  65.9 145.8 %copy-start.18 = (bf16[75,2,256]{0,1,2:T(2,128)(2,1)S(1)}, bf16[75,2,256]{0,1,2:T(2,128)(2,1)}, u32[]{:S(2)}) copy-start(bf16[75,2,256]{0,1,2:T(2,128)(2,1)} %copy-done.17) | copy-start | bytes 230404
  65.9 145.8 %copy-start.22 = (bf16[75,2,256]{0,1,2:T(2,128)(2,1)S(1)}, bf16[75,2,256]{0,1,2:T(2,128)(2,1)}, u32[]{:S(2)}) copy-start(bf16[75,2,256]{0,1,2:T(2,128)(2,1)} %copy-done.21) | copy-start | bytes 230404
  65.9 145.8 %copy-start.34 = (pred[8]{0:T(512)(128)(4,1)S(1)}, pred[8]{0:T(512)(128)(4,1)}, u32[]{:S(2)}) copy-start(pred[8]{0:T(512)(128)(4,1)} %constant.45.clone.1) | copy-start | bytes 28
  229.5 8.0 %collective-permute-start.6 = (f32[75,12,2]{0,1,2:T(8,128)S(1)}, f32[75,12,2]{0,1,2:T(8,128)S(1)}, u32[]{:S(2)}, u32[]{:S(2)}) collective-permute-start(f32[75,12,2]{0,1,2:T(8,128)S(1)} %get-tuple-element.17), channel_id=1, source_target_pairs={{0,4},{4,8},{8,12},{12,16},{16,20},{20,24},{24,28},{28,32},{32,36}... | collective-permute-start | bytes 21608 | tf_op jit(solution)/shard_map/ppermute | solution.py:16
  230.1 7.4 %collective-permute-start.7 = (f32[75,12,2]{0,1,2:T(8,128)S(1)}, f32[75,12,2]{0,1,2:T(8,128)S(1)}, u32[]{:S(2)}, u32[]{:S(2)}) collective-permute-start(f32[75,12,2]{0,1,2:T(8,128)S(1)} %get-tuple-element.16), channel_id=1, source_target_pairs={{4,0},{8,4},{12,8},{16,12},{20,16},{24,20},{28,24},{32,28},{36,32}... | collective-permute-start | bytes 21608 | tf_op jit(solution)/shard_map/ppermute | solution.py:19
  240.6 6.1 %collective-permute-start.8 = (bf16[75,2,256]{0,1,2:T(2,128)(2,1)S(1)}, bf16[75,2,256]{0,1,2:T(2,128)(2,1)S(1)}, u32[]{:S(2)}, u32[]{:S(2)}) collective-permute-start(bf16[75,2,256]{0,1,2:T(2,128)(2,1)S(1)} %get-tuple-element.6), channel_id=1, source_target_pairs={{0,1},{1,2},{2,3},{4,5},{5,6},{6,7},{8,9},{9,10},{10,11},{12,13},{... | collective-permute-start | bytes 230408 | tf_op jit(solution)/shard_map/ppermute | solution.py:16
  241.9 6.6 %collective-permute-start.9 = (bf16[75,2,256]{0,1,2:T(2,128)(2,1)S(1)}, bf16[75,2,256]{0,1,2:T(2,128)(2,1)S(1)}, u32[]{:S(2)}, u32[]{:S(2)}) collective-permute-start(bf16[75,2,256]{0,1,2:T(2,128)(2,1)S(1)} %get-tuple-element.14), channel_id=1, source_target_pairs={{1,0},{2,1},{3,2},{5,4},{6,5},{7,6},{9,8},{10,9},{11,10},{13,12},{... | collective-permute-start | bytes 230408 | tf_op jit(solution)/shard_map/ppermute | solution.py:19
  249.4 148.5 %copy-start.31 = (pred[256]{0:T(512)(128)(4,1)S(1)}, pred[256]{0:T(512)(128)(4,1)}, u32[]{:S(2)}) copy-start(pred[256]{0:T(512)(128)(4,1)} %get-tuple-element.44) | copy-start | bytes 772
  249.4 148.5 %copy-start.33 = (pred[256]{0:T(512)(128)(4,1)S(1)}, pred[256]{0:T(512)(128)(4,1)}, u32[]{:S(2)}) copy-start(pred[256]{0:T(512)(128)(4,1)} %get-tuple-element.45) | copy-start | bytes 772
  249.4 150.2 %copy-start.16 = (bf16[75,2,256]{0,1,2:T(2,128)(2,1)S(1)}, bf16[75,2,256]{0,1,2:T(2,128)(2,1)}, u32[]{:S(2)}) copy-start(bf16[75,2,256]{0,1,2:T(2,128)(2,1)} %copy-done.15) | copy-start | bytes 230404
  249.5 150.2 %copy-start.20 = (bf16[75,2,256]{0,1,2:T(2,128)(2,1)S(1)}, bf16[75,2,256]{0,1,2:T(2,128)(2,1)}, u32[]{:S(2)}) copy-start(bf16[75,2,256]{0,1,2:T(2,128)(2,1)} %copy-done.19) | copy-start | bytes 230404
  249.5 150.2 %copy-start.24 = (f32[75,12,2]{0,1,2:T(8,128)S(1)}, f32[75,12,2]{0,1,2:T(8,128)}, u32[]{:S(2)}) copy-start(f32[75,12,2]{0,1,2:T(8,128)} %copy-done.23) | copy-start | bytes 21604
  249.5 150.2 %copy-start.35 = (pred[8]{0:T(512)(128)(4,1)S(1)}, pred[8]{0:T(512)(128)(4,1)}, u32[]{:S(2)}) copy-start(pred[8]{0:T(512)(128)(4,1)} %constant.45.clone.1) | copy-start | bytes 28
  (24 other events, 250.0 us)
Sparse Core Ops, SparseCore 0:
  53.1 137.8 all-gather.2
  240.8 138.2 all-gather.4
where the time goes:
time: 413 us; the launch traced here: 411 us
  waiting for transfers between devices  260 us (63%)
  local copies, waits for them, and re-layouts  60.5 us (15%)
  other arithmetic  51.3 us (12%)
  starting transfers between devices  24.2 us (6%)
  between operations  14.8 us (4%)
    all_gather x2, waiting for transfers between devices, adjoint_parts(): lax.all_gather(folded.astype(jnp.bfloat16), 'lon', axis=2, tiled=True)  255 us
    convert_element_type x2, local copies, waits for them, and re-layouts, adjoint_parts(): lax.all_gather(folded.astype(jnp.bfloat16), 'lon', axis=2, tiled=True)  28.8 us
    reduce_sum x2, other arithmetic, vertical_adjoint(): return jnp.sum(inverse.astype(jnp.float32) * weighted[:, None], axis=0)  19.1 us
    ppermute x4, starting transfers between devices, extended_2(): lax.ppermute(lax.slice_in_dim(block, 0, width, axis=dim), axis, backward)  13.3 us
    unnamed x78, local copies, waits for them, and re-layouts  9.07 us
    gather x2, local copies, waits for them, and re-layouts, adjoint_parts(): jnp.take(shard_piece, jnp.clip(column_index, 0, piece_width - 1), axis=2)  9.02 us
  transfers between devices with their start and end apart: 12, of which 5 were waited for; matrix products, arithmetic and copies ran while one was open for 8% of the time, Pallas kernels for 0%

commit v1 on v0

v1 whole, which is shorter than its diff:
```python
import jax
import jax.numpy as jnp
from jax import lax
from jax.experimental import pallas as pl
from jax.experimental.pallas import tpu as pltpu
from jax.sharding import PartitionSpec as P

F32 = jnp.float32
BF16 = jnp.bfloat16
LEV = 75
ROWS = 8
COLS = 256
HALF = 128
JB = 5
QUADS = 19
FULL_QUADS = 18
TAIL = LEV - 4 * FULL_QUADS
MIX_LANE = 22


def lane_ids():
    return lax.broadcasted_iota(jnp.int32, (ROWS, HALF), 1)


def row_ids():
    return lax.broadcasted_iota(jnp.int32, (ROWS, HALF), 0)


def turn(tile, shift, axis):
    size = tile.shape[axis]
    if isinstance(shift, int):
        shift = shift % size
        if shift == 0:
            return tile
    return pltpu.roll(tile, shift, axis)


def halves(value):
    return [value[:, :HALF], value[:, HALF:]]


def for_quads(body):
    def step(quad, carry):
        body(quad, 4)
        return carry

    lax.fori_loop(0, FULL_QUADS, step, 0)
    body(FULL_QUADS, TAIL)


def vertical_block(inverse_ref, weighted_ref, depth, first_level, g_ref):
    group = 15

    def some_levels(step, sums):
        sums = list(sums)
        for offset in range(group):
            k = step * group + offset
            weight = weighted_ref[k]
            for jj in range(JB):
                sums[jj] = sums[jj] + inverse_ref[k, jj].astype(F32) * weight
        return tuple(sums)

    zero = jnp.zeros((ROWS, COLS), F32)
    sums = lax.fori_loop(0, LEV // group, some_levels, (zero,) * JB)
    for jj in range(JB):
        j = first_level + jj
        g_ref[j] = jnp.where(depth > j, sums[jj], 0.0)


def place_lanes(acc_ref, side, j, tile, from_lane):
    spot = lax.rem(j, 64)
    which = j // 64
    rolled = pltpu.roll(tile, lax.rem(2 * spot + (2 * HALF - from_lane), HALF), 1)
    keep = (lane_ids() // 2) == spot
    acc_ref[side, which] = jnp.where(keep, rolled, acc_ref[side, which])


def place_mix(acc_ref, side, j, tile):
    lane = MIX_LANE + j
    rolled = pltpu.roll(tile, lax.rem(lane + 1, HALF), 1)
    acc_ref[side, 1] = jnp.where(lane_ids() == lane, rolled, acc_ref[side, 1])


def pack_rims(g_ref, sn_ref, mn_ref, se_ref, me_ref, slots_ref, north_ref, south_ref, lonc_ref,
              fold_scr, lon_scr, lonc_scr, with_coefs):
    row = row_ids()
    lon_scr[...] = jnp.zeros_like(lon_scr)
    if with_coefs:
        lonc_scr[...] = jnp.zeros_like(lonc_scr)
    fold_scr[...] = jnp.zeros_like(fold_scr)

    def quad_body(quad, count):
        zero = jnp.zeros((ROWS, HALF), F32)
        north = [zero, zero]
        south = [zero, zero]
        fold = [zero, zero]
        s_north = [zero, zero]
        m_north = [zero, zero]
        s_south = [zero, zero]
        for l in range(count):
            j = quad * 4 + l
            mine = (row // 2) == l
            g = halves(g_ref[j])
            s = halves(sn_ref[j].astype(F32))
            m = halves(mn_ref[j].astype(F32))
            for c in range(2):
                north[c] = jnp.where(mine, turn(g[c], 2 * l - 6, 0), north[c])
                south[c] = jnp.where(mine, turn(g[c], 2 * l, 0), south[c])
                slope = s[c] * (1.0 / 12.0)
                direct = g[c] * (m[c] - 7.0 * slope)
                inner = (g[c] - turn(g[c], -1, 0)) * slope
                both = jnp.where(row == 7, direct + turn(inner, 1, 0), turn(slope * g[c], -1, 0))
                fold[c] = jnp.where(mine, turn(both, 2 * l - 6, 0), fold[c])
                if with_coefs:
                    s_north[c] = jnp.where(mine, turn(s[c], 2 * l - 6, 0), s_north[c])
                    m_north[c] = jnp.where(mine, turn(m[c], 2 * l - 6, 0), m_north[c])
                    s_south[c] = jnp.where(mine, turn(s[c], 2 * l, 0), s_south[c])
            place_lanes(lon_scr, 0, j, g[1], 126)
            place_lanes(lon_scr, 1, j, g[0], 0)
            if with_coefs:
                se = halves(se_ref[j].astype(F32))
                me = halves(me_ref[j].astype(F32))
                place_lanes(lonc_scr, 0, j, se[1], 126)
                place_lanes(lonc_scr, 1, j, se[0], 0)
                place_mix(lonc_scr, 0, j, me[1])
        for c in range(2):
            cols = slice(c * HALF, (c + 1) * HALF)
            north_ref[0, quad, :, cols] = north[c].astype(BF16)
            south_ref[0, quad, :, cols] = south[c].astype(BF16)
            fold_scr[quad, :, cols] = fold[c]
            if with_coefs:
                north_ref[1, quad, :, cols] = s_north[c].astype(BF16)
                north_ref[2, quad, :, cols] = m_north[c].astype(BF16)
                south_ref[1, quad, :, cols] = s_south[c].astype(BF16)

    for_quads(quad_body)
    r = lax.broadcasted_iota(jnp.int32, (COLS, COLS), 0)
    q = lax.broadcasted_iota(jnp.int32, (COLS, COLS), 1)
    mirror = (r + q == COLS - 1).astype(F32).astype(BF16)
    flat = fold_scr[...].reshape(20 * ROWS, COLS).astype(BF16)
    flipped = jnp.dot(flat, mirror, preferred_element_type=F32).reshape(20, ROWS, COLS)
    count = lax.axis_size("lon")
    me_lon = lax.axis_index("lon")
    east = lax.rem(me_lon + 1, count)
    west = lax.rem(me_lon + count - 1, count)
    to_east = jnp.concatenate([lon_scr[0, 0], lon_scr[0, 1]], axis=1)
    to_west = jnp.concatenate([lon_scr[1, 0], lon_scr[1, 1]], axis=1)
    zero = jnp.zeros((ROWS, COLS), F32)
    for i in range(slots_ref.shape[0]):
        piece = flipped[i] if i < QUADS else zero
        rim = jnp.where(i == east, to_east, jnp.where(i == west, to_west, zero))
        slots_ref[i] = jnp.concatenate([piece, rim], axis=0).astype(BF16)
    if with_coefs:
        for side in range(2):
            lonc_ref[side] = jnp.concatenate([lonc_scr[side, 0], lonc_scr[side, 1]], axis=1).astype(BF16)


def transposed_h(g_ref, se_ref, me_ref, sn_ref, mn_ref, depth_ref, slots_ref, coef_slots_ref,
                 fold_slots_ref, north_ref, south_ref, north_c_ref, south_c_ref, out_ref):
    row = row_ids()
    lane = lane_ids()
    count = lax.axis_size("lon")
    me_lon = lax.axis_index("lon")
    east = lax.rem(me_lon + 1, count)
    west = lax.rem(me_lon + count - 1, count)
    lat = lax.axis_index("lat")
    has_south = (lat > 0).astype(F32)
    has_north = (lat < lax.axis_size("lat") - 1).astype(F32)
    is_top = 1.0 - has_north
    lon_w = slots_ref.at[west]
    lon_e = slots_ref.at[east]
    lonc_w = coef_slots_ref.at[west]
    lonc_e = coef_slots_ref.at[east]

    def pick(ref):
        value = ref[...].astype(F32)[ROWS:]
        return halves(value)

    gw, ge, cw, ce = pick(lon_w), pick(lon_e), pick(lonc_w), pick(lonc_e)

    def quad_body(quad, levels):
        g_n = halves(north_ref[0, quad].astype(F32) * has_south)
        s_n = halves(north_c_ref[1, quad].astype(F32) * has_south)
        m_n = halves(north_c_ref[2, quad].astype(F32) * has_south)
        g_s = halves(south_ref[0, quad].astype(F32) * has_north)
        s_s = halves(south_c_ref[1, quad].astype(F32) * has_north)
        fold = halves(fold_slots_ref[quad].astype(F32)[:ROWS] * is_top)
        for l in range(levels):
            j = quad * 4 + l
            depth = halves(depth_ref[...])
            g = halves(g_ref[j])
            se = halves(se_ref[j].astype(F32))
            me = halves(me_ref[j].astype(F32))
            sn = halves(sn_ref[j].astype(F32))
            mn = halves(mn_ref[j].astype(F32))
            first = j < 64
            at = 2 * lax.rem(j, 64)
            back = lax.rem(HALF - at, HALF)
            fore = lax.rem(2 * HALF - 2 - at, HALF)
            g_rim = jnp.where(
                lane < 64,
                pltpu.roll(jnp.where(first, ge[0], ge[1]), back, 1),
                pltpu.roll(jnp.where(first, gw[0], gw[1]), fore, 1),
            )
            s_rim = jnp.where(
                lane < 64,
                pltpu.roll(jnp.where(first, ce[0], ce[1]), back, 1),
                pltpu.roll(jnp.where(first, cw[0], cw[1]), fore, 1),
            )
            m_rim = pltpu.roll(cw[1], lax.rem(2 * HALF - 1 - MIX_LANE - j, HALF), 1)
            tiles = [g[0], g[1], g_rim]
            ahead = [turn(jnp.where(lane == 0, tiles[(c + 1) % 3], tiles[c]), -1, 1) for c in range(3)]
            jump = [ahead[c] - tiles[c] for c in range(3)]
            slope = [x * (1.0 / 12.0) for x in (se[0], se[1], s_rim)]
            mixes = [me[0], me[1], m_rim]
            far = [-slope[c] * jump[c] for c in range(3)]
            high = [(7.0 * slope[c] - mixes[c]) * jump[c] for c in range(3)]
            total = []
            for c in range(2):
                before = (c + 2) % 3
                after = c + 1
                value = g[c] + (7.0 * slope[c] + mixes[c]) * jump[c]
                value = value + turn(jnp.where(lane == 127, high[before], high[c]), 1, 1)
                value = value + turn(jnp.where(lane == 0, far[after], far[c]), -1, 1)
                value = value + turn(jnp.where(lane >= 126, far[before], far[c]), 2, 1)
                total.append(value)
            for c in range(2):
                rim = jnp.where(row < 4, turn(g_s[c], -2 * l, 0), turn(g_n[c], 6 - 2 * l, 0))
                s_r = jnp.where(row < 4, turn(s_s[c], -2 * l, 0), turn(s_n[c], 6 - 2 * l, 0)) * (1.0 / 12.0)
                m_r = turn(m_n[c], 6 - 2 * l, 0)
                d = turn(jnp.where(row == 0, rim, g[c]), -1, 0) - g[c]
                d_r = turn(jnp.where(row == 0, g[c], rim), -1, 0) - rim
                sl = sn[c] * (1.0 / 12.0)
                hi = (7.0 * sl - mn[c]) * d
                hi_r = (7.0 * s_r - m_r) * d_r
                fa = -sl * d
                fa_r = -s_r * d_r
                value = total[c] + (7.0 * sl + mn[c]) * d
                value = value + turn(jnp.where(row == 7, hi_r, hi), 1, 0)
                value = value + turn(jnp.where(row == 0, fa_r, fa), -1, 0)
                value = value + turn(jnp.where(row >= 6, fa_r, fa), 2, 0)
                over = turn(fold[c], 5 - 2 * l, 0)
                value = value + jnp.where((row == 5) | (row == 6), over, 0.0)
                out_ref[j, :, c * HALF:(c + 1) * HALF] = jnp.where(depth[c] > j, value, 0.0)

    for_quads(quad_body)


def first_kernel(lam_ref, inv_ref, se_ref, me_ref, sn_ref, mn_ref, depth_ref,
                 g_ref, slots_ref, north_ref, south_ref, lonc_ref,
                 weighted, fold_scr, lon_scr, lonc_scr):
    step = pl.program_id(0)
    depth = depth_ref[...]

    @pl.when(step == 0)
    def _():
        def mask(k, carry):
            weighted[k] = jnp.where(depth > k, lam_ref[k], 0.0)
            return carry

        lax.fori_loop(0, LEV, mask, 0, unroll=5)

    vertical_block(inv_ref, weighted, depth, step * JB, g_ref)

    @pl.when(step == pl.num_programs(0) - 1)
    def _():
        pack_rims(g_ref, sn_ref, mn_ref, se_ref, me_ref, slots_ref, north_ref, south_ref, lonc_ref,
                  fold_scr, lon_scr, lonc_scr, True)


def second_kernel(g1_ref, inv_ref, se_ref, me_ref, sn_ref, mn_ref, depth_ref,
                  in_slots_ref, coef_slots_ref, in_north_ref, in_south_ref,
                  g_ref, slots_ref, north_ref, south_ref, weighted, fold_scr, lon_scr):
    step = pl.program_id(0)

    @pl.when(step == 0)
    def _():
        transposed_h(g1_ref, se_ref, me_ref, sn_ref, mn_ref, depth_ref, in_slots_ref, coef_slots_ref,
                     coef_slots_ref, in_north_ref, in_south_ref, in_north_ref, in_south_ref, weighted)

    vertical_block(inv_ref, weighted, depth_ref[...], step * JB, g_ref)

    @pl.when(step == pl.num_programs(0) - 1)
    def _():
        pack_rims(g_ref, sn_ref, mn_ref, se_ref, me_ref, slots_ref, north_ref, south_ref, None,
                  fold_scr, lon_scr, None, False)


def relay_kernel(fold_ref, in_ref, lonc_ref, out_ref):
    count = out_ref.shape[0]
    me_lon = lax.axis_index("lon")
    east = lax.rem(me_lon + 1, count)
    west = lax.rem(me_lon + count - 1, count)
    for d in range(count):
        piece = in_ref[fold_ref[d]]
        if lonc_ref is None:
            out_ref[d] = piece
        else:
            rim = jnp.where(d == east, lonc_ref[0].astype(F32), lonc_ref[1].astype(F32))
            out_ref[d] = jnp.concatenate([piece.astype(F32)[:ROWS], rim], axis=0).astype(BF16)


def plain_relay(fold_ref, in_ref, out_ref):
    relay_kernel(fold_ref, in_ref, None, out_ref)


def third_kernel(g_ref, se_ref, me_ref, sn_ref, mn_ref, depth_ref, slots_ref, coef_slots_ref,
                 fold_slots_ref, north_ref, south_ref, north_c_ref, south_c_ref, out_ref):
    transposed_h(g_ref, se_ref, me_ref, sn_ref, mn_ref, depth_ref, slots_ref, coef_slots_ref,
                 fold_slots_ref, north_ref, south_ref, north_c_ref, south_c_ref, out_ref)


def whole(shape):
    zeros = (0,) * len(shape)
    return pl.BlockSpec(shape, lambda *_: zeros)


def shaped(shape, dtype):
    return jax.ShapeDtypeStruct(shape, dtype)


def per_device(lam, inverse, se, me, sn, mn, depth, fold_block):
    field = (LEV, ROWS, COLS)
    count = lax.axis_size("lon")
    lats = lax.axis_size("lat")
    slot_shape = (count, 2 * ROWS, COLS)
    params = pltpu.CompilerParams(vmem_limit_bytes=40 * 1024 * 1024)
    vspec = pl.BlockSpec((LEV, JB, ROWS, COLS), lambda b: (0, b, 0, 0))
    grid = (LEV // JB,)
    coefs = [se, me, sn, mn]
    cost = pl.CostEstimate(flops=2 * LEV * LEV * ROWS * COLS, bytes_accessed=LEV * LEV * ROWS * COLS * 2,
                           transcendentals=0)
    north_shape = (3, QUADS, ROWS, COLS)
    south_shape = (2, QUADS, ROWS, COLS)
    one_shape = (1, QUADS, ROWS, COLS)
    lon_scr = pltpu.VMEM((2, 2, ROWS, HALF), F32)
    fold_scr = pltpu.VMEM((20, ROWS, COLS), F32)

    g1, slots1, north1, south1, lonc = pl.pallas_call(
        first_kernel,
        grid=grid,
        in_specs=[whole(field), vspec] + [whole(field)] * 4 + [whole((ROWS, COLS))],
        out_specs=[whole(field), whole(slot_shape), whole(north_shape), whole(south_shape),
                   whole((2, ROWS, COLS))],
        out_shape=[shaped(field, F32), shaped(slot_shape, BF16), shaped(north_shape, BF16),
                   shaped(south_shape, BF16), shaped((2, ROWS, COLS), BF16)],
        scratch_shapes=[pltpu.VMEM(field, F32), fold_scr, lon_scr, lon_scr],
        compiler_params=params,
        cost_estimate=cost,
        name="vertical_first",
    )(lam, inverse, *coefs, depth)

    up = [(i, (i + 1) % lats) for i in range(lats)]
    down = [(i, (i - 1) % lats) for i in range(lats)]

    def exchange(north, south, slots):
        return (lax.ppermute(north, "lat", up), lax.ppermute(south, "lat", down),
                lax.all_to_all(slots, "lon", 0, 0, tiled=True))

    smem = pl.BlockSpec(memory_space=pltpu.SMEM)
    in_north1, in_south1, in_slots1 = exchange(north1, south1, slots1)
    relayed1 = pl.pallas_call(
        relay_kernel,
        in_specs=[smem, whole(slot_shape), whole((2, ROWS, COLS))],
        out_specs=whole(slot_shape),
        out_shape=shaped(slot_shape, BF16),
        name="relay_first",
    )(fold_block, in_slots1, lonc)
    fold1 = lax.all_to_all(relayed1, "lon", 0, 0, tiled=True)

    g2, slots2, north2, south2 = pl.pallas_call(
        second_kernel,
        grid=grid,
        in_specs=[whole(field), vspec] + [whole(field)] * 4
        + [whole((ROWS, COLS)), whole(slot_shape), whole(slot_shape), whole(north_shape), whole(south_shape)],
        out_specs=[whole(field), whole(slot_shape), whole(one_shape), whole(one_shape)],
        out_shape=[shaped(field, F32), shaped(slot_shape, BF16), shaped(one_shape, BF16),
                   shaped(one_shape, BF16)],
        scratch_shapes=[pltpu.VMEM(field, F32), fold_scr, lon_scr],
        compiler_params=params,
        cost_estimate=cost,
        name="horizontal_vertical",
    )(g1, inverse, *coefs, depth, in_slots1, fold1, in_north1, in_south1)

    in_north2, in_south2, in_slots2 = exchange(north2, south2, slots2)
    relayed2 = pl.pallas_call(
        plain_relay,
        in_specs=[smem, whole(slot_shape)],
        out_specs=whole(slot_shape),
        out_shape=shaped(slot_shape, BF16),
        name="relay_second",
    )(fold_block, in_slots2)
    fold2 = lax.all_to_all(relayed2, "lon", 0, 0, tiled=True)

    return pl.pallas_call(
        third_kernel,
        in_specs=[whole(field)] * 5
        + [whole((ROWS, COLS)), whole(slot_shape), whole(slot_shape), whole(slot_shape), whole(one_shape),
           whole(one_shape), whole(north_shape), whole(south_shape)],
        out_specs=whole(field),
        out_shape=shaped(field, F32),
        compiler_params=params,
        name="horizontal_last",
    )(g2, *coefs, depth, in_slots2, fold1, fold2, in_north2, in_south2, in_north1, in_south1)


def solution(mesh):
    return jax.shard_map(
        per_device,
        mesh=mesh,
        in_specs=(
            P(None, "lat", "lon"),
            P(None, None, "lat", "lon"),
            P(None, "lat", "lon"),
            P(None, "lat", "lon"),
            P(None, "lat", "lon"),
            P(None, "lat", "lon"),
            P("lat", "lon"),
            P(),
        ),
        out_specs=P(None, "lat", "lon"),
        check_vma=False,
    )
```

time: 413 us -> 120 us (0.29)
  waiting for transfers between devices: 260 us -> 12.7 us
  local copies, waits for them, and re-layouts: 60.5 us -> 7.55 us
  other arithmetic: 51.3 us -> 0 us
  Pallas kernels: 0 us -> 47.4 us
  blocking collectives: 0 us -> 36.2 us
  between operations: 14.8 us -> 0.11 us
  starting transfers between devices: 24.2 us -> 14.4 us
    all_gather x2 -> x0, waiting for transfers between devices: 255 us -> none  [adjoint_parts(): lax.all_gather(folded.astype(jnp.bfloat16), 'lon', axis=2, tiled=True)]
    pallas_call x0 -> x5, Pallas kernels: none -> 47.4 us  [the longest x1 21.4 us: per_device(): pl.pallas_call(second_kernel, grid=grid, in_specs=[whole(field), vspec] +...]
    all_to_all x0 -> x2, blocking collectives: none -> 36.2 us  [exchange(): lax.all_to_all(slots, 'lon', 0, 0, tiled=True)]
    convert_element_type x4 -> x0, local copies, waits for them, and re-layouts: 32.2 us -> none  [the longest x2 28.8 us: adjoint_parts(): lax.all_gather(folded.astype(jnp.bfloat16), 'lon', axis=2, tiled=True)]
    reduce_sum x2 -> x0, other arithmetic: 19.1 us -> none  [vertical_adjoint(): return jnp.sum(inverse.astype(jnp.float32) * weighted[:, None], axis=0)]
    ppermute x10 -> x4, starting transfers between devices: 24.1 us -> 6.62 us  [the longest x2 6.47 us: exchange(): lax.ppermute(south, 'lat', down)]
    add_any x10 -> x0, other arithmetic: 14.5 us -> none  [the longest x2 6.56 us: local_horizontal(): flux_x = face_flux(extended[:, 2:-2, :], speed_x, mixing_x, 2)]
    gather x2 -> x0, local copies, waits for them, and re-layouts: 9.02 us -> none  [adjoint_parts(): jnp.take(shard_piece, jnp.clip(column_index, 0, piece_width - 1), axis=2)]
  transfers between devices with their start and end apart: 12 -> 6, of which waited for: 5 -> 5; matrix products, arithmetic and copies ran while one was open for 8% -> 0% of each run, Pallas kernels for 0% -> 0%
where the time goes in v1:
time: 120 us; the launch traced here: 118 us
  Pallas kernels  47.4 us (40%)
  blocking collectives  36.2 us (30%)
  starting transfers between devices  14.4 us (12%)
  waiting for transfers between devices  12.7 us (11%)
  local copies, waits for them, and re-layouts  7.55 us (6%)
    all_to_all x2, blocking collectives, exchange(): lax.all_to_all(slots, 'lon', 0, 0, tiled=True)  36.2 us
    pallas_call x1, Pallas kernels, per_device(): pl.pallas_call(second_kernel, grid=grid, in_specs=[whole(field), vspec] +...  21.4 us
    pallas_call x1, Pallas kernels, per_device(): pl.pallas_call(first_kernel, grid=grid, in_specs=[whole(field), vspec] +...  17 us
    unnamed x28, local copies, waits for them, and re-layouts  7.55 us
    ppermute x2, starting transfers between devices, exchange(): lax.ppermute(south, 'lat', down)  6.47 us
    pallas_call x1, Pallas kernels, per_device(): pl.pallas_call(third_kernel, in_specs=[whole(field)] * 5 + [whole((ROWS,...  5.64 us
    ppermute x2, waiting for transfers between devices, exchange(): lax.ppermute(south, 'lat', down)  4.16 us
    all_to_all x1, waiting for transfers between devices, per_device(): fold2 = lax.all_to_all(relayed2, 'lon', 0, 0, tiled=True)  3.87 us
  transfers between devices with their start and end apart: 6, of which 5 were waited for; matrix products, arithmetic and copies ran while one was open for 0% of the time, Pallas kernels for 0%

profile of v1, /device:TPU:0, one launch (start us, length us, event | category | flops | bytes accessed | tf_op | source)
XLA Modules:
  0.0 118.3 jit_solution(11916301764674768981)
XLA Ops:
  0.0 1.0 copy-done
  1.0 1.0 copy-done.2
  1.9 1.0 copy-done.4
  2.9 1.0 copy-done.6
  3.9 1.1 copy-done.10
  4.9 0.7 copy-done.11
  5.7 17.0 %vertical_first.1 = (f32[75,8,256]{2,1,0:T(8,128)S(1)}, bf16[32,16,256]{2,1,0:T(8,128)(2,1)S(1)}, bf16[3,19,8,256]{3,2,1,0:T(8,128)(2,1)S(1)}, bf16[2,19,8,256]{3,2,1,0:T(8,128)(2,1)S(1)}, bf16[2,8,256]{2,1,0:T(8,128)(2,1)S(1)}) custom-call(f32[75,8,256]{2,1,0:T(8,128)S(1)} %copy-done.10, bf16[75,75,8,256]{3,2,1,0:T(8,128)(2,1)} %inv_ref.3, ...), custom_call_target="tpu_custom_call" | custom-call | flops 23040000 | bytes 23040000 | tf_op jit(solution)/shard_map/vertical_first/pallas_call | solution.py:339
  22.7 18.7 %all_to_all.20.in_ref.in_slots_ref = bf16[32,16,256]{2,1,0:T(8,128)(2,1)} all-to-all(bf16[32,16,256]{2,1,0:T(8,128)(2,1)S(1)} %get-tuple-element.15), channel_id=1, replica_groups=mesh['lon'=32,'lat'=4] {'lon'}, dimensions={0} | all-to-all | bytes 524288 | tf_op jit(solution)/shard_map/all_to_all | solution.py:358
  41.4 1.7 %relay_first.1 = bf16[32,16,256]{2,1,0:T(8,128)(2,1)} custom-call(s32[32]{0:T(128)} %fold_ref.3, bf16[32,16,256]{2,1,0:T(8,128)(2,1)} %all_to_all.20.in_ref.in_slots_ref, bf16[2,8,256]{2,1,0:T(8,128)(2,1)} %copy-done.13), custom_call_target="tpu_custom_call" | custom-call | tf_op jit(solution)/shard_map/relay_first/pallas_call | solution.py:362
  43.1 3.9 %all-to-all-start.1 = ((bf16[32,16,256]{2,1,0:T(8,128)(2,1)}), bf16[32,16,256]{2,1,0:T(8,128)(2,1)S(1)}, u32[]{:S(2)}, u32[]{:S(2)}) async-start(bf16[32,16,256]{2,1,0:T(8,128)(2,1)} %relay_first.1), calls=%async_computation.1 | async-start | bytes 524288 | tf_op jit(solution)/shard_map/all_to_all | solution.py:369
  47.1 3.2 %collective-permute-start.1 = (bf16[2,19,8,256]{3,2,1,0:T(8,128)(2,1)S(1)}, bf16[2,19,8,256]{3,2,1,0:T(8,128)(2,1)S(1)}, u32[]{:S(2)}, u32[]{:S(2)}) collective-permute-start(bf16[2,19,8,256]{3,2,1,0:T(8,128)(2,1)S(1)} %get-tuple-element.18), channel_id=1, source_target_pairs={{0,3},{1,0},{2,1},{3,2},{4,7},{5,4},{6,5},{7,6},{8,11},{9,8},{10,9... | collective-permute-start | bytes 466952 | tf_op jit(solution)/shard_map/ppermute | solution.py:357
  50.3 4.2 %collective-permute-done.1.in_south_ref.south_c_ref = bf16[2,19,8,256]{3,2,1,0:T(8,128)(2,1)S(1)} collective-permute-done((bf16[2,19,8,256]{3,2,1,0:T(8,128)(2,1)S(1)}, bf16[2,19,8,256]{3,2,1,0:T(8,128)(2,1)S(1)}, u32[]{:S(2)}, u32[]{:S(2)}) %collective-permute-start.1) | collective-permute-done | bytes 155680 | tf_op jit(solution)/shard_map/ppermute | solution.py:357
  54.5 1.1 collective-permute-done.in_north_ref.north_c_ref
  55.6 0.8 all-to-all-done.1.coef_slots_ref
  56.5 0.9 copy-done.8
  57.4 21.4 %horizontal_vertical.1 = (f32[75,8,256]{2,1,0:T(8,128)S(1)}, bf16[32,16,256]{2,1,0:T(8,128)(2,1)S(1)}, bf16[1,19,8,256]{3,2,1,0:T(8,128)(2,1)S(1)}, bf16[1,19,8,256]{3,2,1,0:T(8,128)(2,1)S(1)}) custom-call(f32[75,8,256]{2,1,0:T(8,128)S(1)} %get-tuple-element.14.g1_ref, bf16[75,75,8,256]{3,2,1,0:T(8,128)(2,1)} %inv_ref.3, bf16[75,8,256]{2,1,0:T(8,128)(2,1)S(1)} %copy-done.1, ...), custom_call_target="tpu_custom_call" | custom-call | flops 23040000 | bytes 23040000 | tf_op jit(solution)/shard_map/horizontal_vertical/pallas_call | solution.py:371
  78.8 17.5 %all_to_all.21.in_ref.slots_ref = bf16[32,16,256]{2,1,0:T(8,128)(2,1)} all-to-all(bf16[32,16,256]{2,1,0:T(8,128)(2,1)S(1)} %get-tuple-element.20), channel_id=1, replica_groups=mesh['lon'=32,'lat'=4] {'lon'}, dimensions={0} | all-to-all | bytes 524288 | tf_op jit(solution)/shard_map/all_to_all | solution.py:358
  96.3 1.7 %relay_second.1 = bf16[32,16,256]{2,1,0:T(8,128)(2,1)} custom-call(s32[32]{0:T(128)} %fold_ref.3, bf16[32,16,256]{2,1,0:T(8,128)(2,1)} %all_to_all.21.in_ref.slots_ref), custom_call_target="tpu_custom_call" | custom-call | tf_op jit(solution)/shard_map/relay_second/pallas_call | solution.py:386
  98.0 3.9 %all-to-all-start.3 = ((bf16[32,16,256]{2,1,0:T(8,128)(2,1)}), bf16[32,16,256]{2,1,0:T(8,128)(2,1)S(1)}, u32[]{:S(2)}, u32[]{:S(2)}) async-start(bf16[32,16,256]{2,1,0:T(8,128)(2,1)} %relay_second.1), calls=%async_computation.3 | async-start | bytes 524288 | tf_op jit(solution)/shard_map/all_to_all | solution.py:393
  101.9 3.2 %collective-permute-start.3 = (bf16[1,19,8,256]{3,2,1,0:T(8,128)(2,1)S(1)}, bf16[1,19,8,256]{3,2,1,0:T(8,128)(2,1)S(1)}, u32[]{:S(2)}, u32[]{:S(2)}) collective-permute-start(bf16[1,19,8,256]{3,2,1,0:T(8,128)(2,1)S(1)} %get-tuple-element.22), channel_id=1, source_target_pairs={{0,3},{1,0},{2,1},{3,2},{4,7},{5,4},{6,5},{7,6},{8,11},{9,8},{10,9... | collective-permute-start | bytes 233480 | tf_op jit(solution)/shard_map/ppermute | solution.py:357
  105.2 2.7 %collective-permute-done.2.north_ref = bf16[1,19,8,256]{3,2,1,0:T(8,128)(2,1)S(1)} collective-permute-done((bf16[1,19,8,256]{3,2,1,0:T(8,128)(2,1)S(1)}, bf16[1,19,8,256]{3,2,1,0:T(8,128)(2,1)S(1)}, u32[]{:S(2)}, u32[]{:S(2)}) %collective-permute-start.2) | collective-permute-done | bytes 77856 | tf_op jit(solution)/shard_map/ppermute | solution.py:357
  107.9 3.9 %all-to-all-done.3.fold_slots_ref = bf16[32,16,256]{2,1,0:T(8,128)(2,1)S(1)} async-done(((bf16[32,16,256]{2,1,0:T(8,128)(2,1)}), bf16[32,16,256]{2,1,0:T(8,128)(2,1)S(1)}, u32[]{:S(2)}, u32[]{:S(2)}) %all-to-all-start.3) | async-done | bytes 262176 | tf_op jit(solution)/shard_map/all_to_all | solution.py:393
  111.8 0.9 copy-done.9
  112.7 5.6 %horizontal_last.1 = f32[75,8,256]{2,1,0:T(8,128)} custom-call(f32[75,8,256]{2,1,0:T(8,128)S(1)} %get-tuple-element.19.g_ref, bf16[75,8,256]{2,1,0:T(8,128)(2,1)S(1)} %copy-done.1, bf16[75,8,256]{2,1,0:T(8,128)(2,1)S(1)} %copy-done.3, bf16[75,8,256]{2,1,0:T(8,128)(2,1)S(1)} %copy-done.5, bf16[75,8,256]{2,1,0:T(8,128)(2,1)S(1)} %copy-done.7, ...), custom_call_target="tpu_custom_call" | custom-call | tf_op jit(solution)/shard_map/horizontal_last/pallas_call | solution.py:395
  (23 shorter events, 0.2 us)
Async XLA Ops:
  0.0 1.0 copy-start
  1.0 1.0 copy-start.2
  1.9 1.0 copy-start.4
  2.9 1.0 copy-start.6
  3.9 1.1 copy-start.10
  4.9 0.7 copy-start.11
  5.6 50.8 %copy-start.1 = (bf16[75,8,256]{2,1,0:T(8,128)(2,1)S(1)}, bf16[75,8,256]{2,1,0:T(8,128)(2,1)}, u32[]{:S(2)}) copy-start(bf16[75,8,256]{2,1,0:T(8,128)(2,1)} %se_ref.5) | copy-start | bytes 921604
  5.6 50.8 %copy-start.3 = (bf16[75,8,256]{2,1,0:T(8,128)(2,1)S(1)}, bf16[75,8,256]{2,1,0:T(8,128)(2,1)}, u32[]{:S(2)}) copy-start(bf16[75,8,256]{2,1,0:T(8,128)(2,1)} %me_ref.5) | copy-start | bytes 921604
  5.6 50.8 %copy-start.5 = (bf16[75,8,256]{2,1,0:T(8,128)(2,1)S(1)}, bf16[75,8,256]{2,1,0:T(8,128)(2,1)}, u32[]{:S(2)}) copy-start(bf16[75,8,256]{2,1,0:T(8,128)(2,1)} %sn_ref.5) | copy-start | bytes 921604
  5.6 50.8 %copy-start.7 = (bf16[75,8,256]{2,1,0:T(8,128)(2,1)S(1)}, bf16[75,8,256]{2,1,0:T(8,128)(2,1)}, u32[]{:S(2)}) copy-start(bf16[75,8,256]{2,1,0:T(8,128)(2,1)} %mn_ref.5) | copy-start | bytes 921604
  5.6 50.8 %copy-start.12 = (s32[8,256]{1,0:T(8,128)S(1)}, s32[8,256]{1,0:T(8,128)}, u32[]{:S(2)}) copy-start(s32[8,256]{1,0:T(8,128)} %depth_ref.5) | copy-start | bytes 24580
  22.7 18.7 %copy-start.13 = (bf16[2,8,256]{2,1,0:T(8,128)(2,1)}, bf16[2,8,256]{2,1,0:T(8,128)(2,1)S(1)}, u32[]{:S(2)}) copy-start(bf16[2,8,256]{2,1,0:T(8,128)(2,1)S(1)} %get-tuple-element.16.lonc_ref) | copy-start | bytes 24580
  43.1 13.3 %all-to-all-start.1 = ((bf16[32,16,256]{2,1,0:T(8,128)(2,1)}), bf16[32,16,256]{2,1,0:T(8,128)(2,1)S(1)}, u32[]{:S(2)}, u32[]{:S(2)}) async-start(bf16[32,16,256]{2,1,0:T(8,128)(2,1)} %relay_first.1), calls=%async_computation.1 | async-start | bytes 524288 | tf_op jit(solution)/shard_map/all_to_all | solution.py:369
  47.0 8.6 %collective-permute-start = (bf16[3,19,8,256]{3,2,1,0:T(8,128)(2,1)S(1)}, bf16[3,19,8,256]{3,2,1,0:T(8,128)(2,1)S(1)}, u32[]{:S(2)}, u32[]{:S(2)}) collective-permute-start(bf16[3,19,8,256]{3,2,1,0:T(8,128)(2,1)S(1)} %get-tuple-element.17), channel_id=1, source_target_pairs={{0,1},{1,2},{2,3},{3,0},{4,5},{5,6},{6,7},{7,4},{8,9},{9,10},{10,1... | collective-permute-start | bytes 700424 | tf_op jit(solution)/shard_map/ppermute | solution.py:357
  47.1 7.4 %collective-permute-start.1 = (bf16[2,19,8,256]{3,2,1,0:T(8,128)(2,1)S(1)}, bf16[2,19,8,256]{3,2,1,0:T(8,128)(2,1)S(1)}, u32[]{:S(2)}, u32[]{:S(2)}) collective-permute-start(bf16[2,19,8,256]{3,2,1,0:T(8,128)(2,1)S(1)} %get-tuple-element.18), channel_id=1, source_target_pairs={{0,3},{1,0},{2,1},{3,2},{4,7},{5,4},{6,5},{7,6},{8,11},{9,8},{10,9... | collective-permute-start | bytes 466952 | tf_op jit(solution)/shard_map/ppermute | solution.py:357
  56.5 1.0 copy-start.8
  98.0 13.8 %all-to-all-start.3 = ((bf16[32,16,256]{2,1,0:T(8,128)(2,1)}), bf16[32,16,256]{2,1,0:T(8,128)(2,1)S(1)}, u32[]{:S(2)}, u32[]{:S(2)}) async-start(bf16[32,16,256]{2,1,0:T(8,128)(2,1)} %relay_second.1), calls=%async_computation.3 | async-start | bytes 524288 | tf_op jit(solution)/shard_map/all_to_all | solution.py:393
  101.9 6.0 %collective-permute-start.2 = (bf16[1,19,8,256]{3,2,1,0:T(8,128)(2,1)S(1)}, bf16[1,19,8,256]{3,2,1,0:T(8,128)(2,1)S(1)}, u32[]{:S(2)}, u32[]{:S(2)}) collective-permute-start(bf16[1,19,8,256]{3,2,1,0:T(8,128)(2,1)S(1)} %get-tuple-element.21), channel_id=1, source_target_pairs={{0,1},{1,2},{2,3},{3,0},{4,5},{5,6},{6,7},{7,4},{8,9},{9,10},{10,1... | collective-permute-start | bytes 233480 | tf_op jit(solution)/shard_map/ppermute | solution.py:357
  101.9 6.0 %collective-permute-start.3 = (bf16[1,19,8,256]{3,2,1,0:T(8,128)(2,1)S(1)}, bf16[1,19,8,256]{3,2,1,0:T(8,128)(2,1)S(1)}, u32[]{:S(2)}, u32[]{:S(2)}) collective-permute-start(bf16[1,19,8,256]{3,2,1,0:T(8,128)(2,1)S(1)} %get-tuple-element.22), channel_id=1, source_target_pairs={{0,3},{1,0},{2,1},{3,2},{4,7},{5,4},{6,5},{7,6},{8,11},{9,8},{10,9... | collective-permute-start | bytes 233480 | tf_op jit(solution)/shard_map/ppermute | solution.py:357
  111.8 1.0 copy-start.9

commit v2 on v1

v2 whole, which is shorter than its diff:
```python
import jax
import jax.numpy as jnp
from jax import lax
from jax.experimental import pallas as pl
from jax.experimental.pallas import tpu as pltpu
from jax.sharding import PartitionSpec as P

F32 = jnp.float32
BF16 = jnp.bfloat16
LEV = 75
ROWS = 8
COLS = 256
HALF = 128
QUADS = 19
FULL_QUADS = 18
AHEAD = 4
HELD = 0
TAIL = LEV - 4 * FULL_QUADS
MIX_LANE = 22


def lane_ids():
    return lax.broadcasted_iota(jnp.int32, (ROWS, HALF), 1)


def row_ids():
    return lax.broadcasted_iota(jnp.int32, (ROWS, HALF), 0)


def turn(tile, shift, axis):
    size = tile.shape[axis]
    if isinstance(shift, int):
        shift = shift % size
        if shift == 0:
            return tile
    return pltpu.roll(tile, shift, axis)


def halves(value):
    return [value[:, :HALF], value[:, HALF:]]


def for_quads(body):
    def step(quad, carry):
        body(quad, 4)
        return carry

    lax.fori_loop(0, FULL_QUADS, step, 0)
    body(FULL_QUADS, TAIL)


def vertical_sums(inverse_ref, weighted_ref, first_level, count):
    group = 15

    def some_levels(step, sums):
        sums = list(sums)
        for offset in range(group):
            k = step * group + offset
            weight = weighted_ref[k]
            for jj in range(count):
                sums[jj] = sums[jj] + inverse_ref[k, first_level + jj].astype(F32) * weight
        return tuple(sums)

    zero = jnp.zeros((ROWS, COLS), F32)
    return lax.fori_loop(0, LEV // group, some_levels, (zero,) * count)


def place_lanes(acc_ref, side, j, tile, from_lane):
    spot = lax.rem(j, 64)
    which = j // 64
    rolled = pltpu.roll(tile, lax.rem(2 * spot + (2 * HALF - from_lane), HALF), 1)
    keep = (lane_ids() // 2) == spot
    acc_ref[side, which] = jnp.where(keep, rolled, acc_ref[side, which])


def place_mix(acc_ref, side, j, tile):
    lane = MIX_LANE + j
    rolled = pltpu.roll(tile, lax.rem(lane + 1, HALF), 1)
    acc_ref[side, 1] = jnp.where(lane_ids() == lane, rolled, acc_ref[side, 1])


def pack_quad(quad, gs, sn_ref, mn_ref, se_ref, me_ref, north_ref, south_ref,
              fold_scr, lon_scr, lonc_scr, with_coefs):
    row = row_ids()
    count = len(gs)
    is_top = lax.axis_index("lat") == lax.axis_size("lat") - 1

    def gathered(tiles_of, shift):
        for c in range(2):
            value = jnp.zeros((ROWS, HALF), F32)
            for l in range(count):
                moved = turn(tiles_of(l)[c], 2 * l - shift, 0)
                value = jnp.where((row // 2) == l, moved, value)
            yield slice(c * HALF, (c + 1) * HALF), value

    def level_of(ref):
        return lambda l: halves(ref[quad * 4 + l].astype(F32))

    for cols, value in gathered(lambda l: halves(gs[l]), 0):
        south_ref[0, quad, :, cols] = value.astype(BF16)
    if with_coefs:
        for cols, value in gathered(level_of(sn_ref), 0):
            south_ref[1, quad, :, cols] = value.astype(BF16)

    @pl.when(jnp.logical_not(is_top))
    def _():
        for cols, value in gathered(lambda l: halves(gs[l]), 6):
            north_ref[0, quad, :, cols] = value.astype(BF16)
        if with_coefs:
            for cols, value in gathered(level_of(sn_ref), 6):
                north_ref[1, quad, :, cols] = value.astype(BF16)
            for cols, value in gathered(level_of(mn_ref), 6):
                north_ref[2, quad, :, cols] = value.astype(BF16)

    @pl.when(is_top)
    def _():
        def ghosts(l):
            g = halves(gs[l])
            s = level_of(sn_ref)(l)
            m = level_of(mn_ref)(l)
            result = []
            for c in range(2):
                slope = s[c] * (1.0 / 12.0)
                direct = g[c] * (m[c] - 7.0 * slope)
                inner = (g[c] - turn(g[c], -1, 0)) * slope
                result.append(jnp.where(row == 7, direct + turn(inner, 1, 0), turn(slope * g[c], -1, 0)))
            return result

        for cols, value in gathered(ghosts, 6):
            fold_scr[quad, :, cols] = value

    for l in range(count):
        j = quad * 4 + l
        g = halves(gs[l])
        place_lanes(lon_scr, 0, j, g[1], 126)
        place_lanes(lon_scr, 1, j, g[0], 0)
        if with_coefs:
            se = level_of(se_ref)(l)
            me = level_of(me_ref)(l)
            place_lanes(lonc_scr, 0, j, se[1], 126)
            place_lanes(lonc_scr, 1, j, se[0], 0)
            place_mix(lonc_scr, 0, j, me[1])


def fill_slots(slots_ref, fold_scr, lon_scr, lonc_scr, with_coefs):
    is_top = lax.axis_index("lat") == lax.axis_size("lat") - 1

    @pl.when(is_top)
    def _():
        r = lax.broadcasted_iota(jnp.int32, (COLS, COLS), 0)
        q = lax.broadcasted_iota(jnp.int32, (COLS, COLS), 1)
        mirror = (r + q == COLS - 1).astype(F32).astype(BF16)
        flat = fold_scr[...].reshape(20 * ROWS, COLS).astype(BF16)
        fold_scr[...] = jnp.dot(flat, mirror, preferred_element_type=F32).reshape(20, ROWS, COLS)

    count = lax.axis_size("lon")
    me_lon = lax.axis_index("lon")
    east = lax.rem(me_lon + 1, count)
    west = lax.rem(me_lon + count - 1, count)

    def wide(ref, side):
        return jnp.concatenate([ref[side, 0], ref[side, 1]], axis=1)

    to_east = wide(lon_scr, 0)
    to_west = wide(lon_scr, 1)
    if with_coefs:
        to_east = jnp.concatenate([to_east, wide(lonc_scr, 0)], axis=0)
        to_west = jnp.concatenate([to_west, wide(lonc_scr, 1)], axis=0)
    for i in range(count):
        rim = jnp.where(i == east, to_east, to_west)
        slots_ref[i] = jnp.concatenate([fold_scr[min(i, QUADS)], rim], axis=0).astype(BF16)


def transposed_h(g_ref, se_ref, me_ref, sn_ref, mn_ref, depth_ref, slots_ref, coef_slots_ref,
                 north_ref, south_ref, north_c_ref, south_c_ref, out_ref):
    row = row_ids()
    lane = lane_ids()
    count = lax.axis_size("lon")
    me_lon = lax.axis_index("lon")
    east = lax.rem(me_lon + 1, count)
    west = lax.rem(me_lon + count - 1, count)
    lat = lax.axis_index("lat")
    has_south = lat > 0
    has_north = lat < lax.axis_size("lat") - 1

    def pick(ref, which, part):
        return halves(ref[which].astype(F32)[part * ROWS:(part + 1) * ROWS])

    def kept(value, condition):
        return halves(jnp.where(condition, value.astype(F32), 0.0))

    gw, ge = pick(slots_ref, west, 1), pick(slots_ref, east, 1)
    cw, ce = pick(coef_slots_ref, west, 2), pick(coef_slots_ref, east, 2)

    def quad_body(quad, levels):
        g_n = kept(north_ref[0, quad], has_south)
        s_n = kept(north_c_ref[1, quad], has_south)
        m_n = kept(north_c_ref[2, quad], has_south)
        g_s = kept(south_ref[0, quad], has_north)
        s_s = kept(south_c_ref[1, quad], has_north)
        for l in range(levels):
            j = quad * 4 + l
            depth = halves(depth_ref[...])
            g = halves(g_ref[j])
            se = halves(se_ref[j].astype(F32))
            me = halves(me_ref[j].astype(F32))
            sn = halves(sn_ref[j].astype(F32))
            mn = halves(mn_ref[j].astype(F32))
            first = j < 64
            at = 2 * lax.rem(j, 64)
            back = lax.rem(HALF - at, HALF)
            fore = lax.rem(2 * HALF - 2 - at, HALF)
            g_rim = jnp.where(
                lane < 64,
                pltpu.roll(jnp.where(first, ge[0], ge[1]), back, 1),
                pltpu.roll(jnp.where(first, gw[0], gw[1]), fore, 1),
            )
            s_rim = jnp.where(
                lane < 64,
                pltpu.roll(jnp.where(first, ce[0], ce[1]), back, 1),
                pltpu.roll(jnp.where(first, cw[0], cw[1]), fore, 1),
            )
            m_rim = pltpu.roll(cw[1], lax.rem(2 * HALF - 1 - MIX_LANE - j, HALF), 1)
            tiles = [g[0], g[1], g_rim]
            ahead = [turn(jnp.where(lane == 0, tiles[(c + 1) % 3], tiles[c]), -1, 1) for c in range(3)]
            jump = [ahead[c] - tiles[c] for c in range(3)]
            slope = [x * (1.0 / 12.0) for x in (se[0], se[1], s_rim)]
            mixes = [me[0], me[1], m_rim]
            far = [-slope[c] * jump[c] for c in range(3)]
            high = [(7.0 * slope[c] - mixes[c]) * jump[c] for c in range(3)]
            total = []
            for c in range(2):
                before = (c + 2) % 3
                after = c + 1
                value = g[c] + (7.0 * slope[c] + mixes[c]) * jump[c]
                value = value + turn(jnp.where(lane == 127, high[before], high[c]), 1, 1)
                value = value + turn(jnp.where(lane == 0, far[after], far[c]), -1, 1)
                value = value + turn(jnp.where(lane >= 126, far[before], far[c]), 2, 1)
                total.append(value)
            for c in range(2):
                rim = jnp.where(row < 4, turn(g_s[c], -2 * l, 0), turn(g_n[c], 6 - 2 * l, 0))
                s_r = jnp.where(row < 4, turn(s_s[c], -2 * l, 0), turn(s_n[c], 6 - 2 * l, 0)) * (1.0 / 12.0)
                m_r = turn(m_n[c], 6 - 2 * l, 0)
                d = turn(jnp.where(row == 0, rim, g[c]), -1, 0) - g[c]
                d_r = turn(jnp.where(row == 0, g[c], rim), -1, 0) - rim
                sl = sn[c] * (1.0 / 12.0)
                hi = (7.0 * sl - mn[c]) * d
                hi_r = (7.0 * s_r - m_r) * d_r
                fa = -sl * d
                fa_r = -s_r * d_r
                value = total[c] + (7.0 * sl + mn[c]) * d
                value = value + turn(jnp.where(row == 7, hi_r, hi), 1, 0)
                value = value + turn(jnp.where(row == 0, fa_r, fa), -1, 0)
                value = value + turn(jnp.where(row >= 6, fa_r, fa), 2, 0)
                out_ref[j, :, c * HALF:(c + 1) * HALF] = jnp.where(depth[c] > j, value, 0.0)

    for_quads(quad_body)


def add_fold(pre_ref, fold_ref, depth_ref, put):
    row = row_ids()
    depth = halves(depth_ref[...])
    on_top = lax.axis_index("lat") == lax.axis_size("lat") - 1

    def quad_body(quad, levels):
        fold = halves(fold_ref[quad].astype(F32))
        for l in range(levels):
            j = quad * 4 + l
            for c in range(2):
                cols = slice(c * HALF, (c + 1) * HALF)
                use = ((row == 5) | (row == 6)) & (depth[c] > j) & on_top
                put(j, cols, pre_ref[j, :, cols] + jnp.where(use, turn(fold[c], 5 - 2 * l, 0), 0.0))

    for_quads(quad_body)


def first_kernel(lam_hbm, inv_hbm, se_hbm, me_hbm, sn_hbm, mn_hbm, depth_hbm,
                 g_ref, slots_ref, north_ref, south_ref,
                 lam, inverse, se, me, sn, mn, depth_ref, fold_scr, lon_scr, lonc_scr, small_sem, sem):
    small = [pltpu.make_async_copy(src, dst, small_sem.at[i])
             for i, (src, dst) in enumerate([(depth_hbm, depth_ref), (lam_hbm, lam), (sn_hbm, sn),
                                             (mn_hbm, mn), (se_hbm, se), (me_hbm, me)])]

    def levels_copy(quad, count):
        part = pl.ds(quad * 4, count)
        return pltpu.make_async_copy(inv_hbm.at[:, part], inverse.at[:, part], sem.at[quad])

    small[0].start()
    small[1].start()
    levels_copy(0, 4).start()
    levels_copy(1, 4).start()
    for copy in small[2:]:
        copy.start()
    for quad in range(2, AHEAD):
        levels_copy(quad, 4).start()
    small[0].wait()
    small[1].wait()
    depth = depth_ref[...]

    def mask(k, carry):
        lam[k] = jnp.where(depth > k, lam[k], 0.0)
        return carry

    lax.fori_loop(0, LEV, mask, 0, unroll=5)
    for copy in small[2:]:
        copy.wait()

    def quad_body(quad, count):
        if count == 4:
            @pl.when(quad + AHEAD < FULL_QUADS)
            def _():
                levels_copy(quad + AHEAD, 4).start()

            @pl.when(quad + AHEAD == FULL_QUADS)
            def _():
                levels_copy(FULL_QUADS, TAIL).start()

        levels_copy(quad, count).wait()
        sums = vertical_sums(inverse, lam, quad * 4, count)
        gs = [jnp.where(depth > quad * 4 + l, sums[l], 0.0) for l in range(count)]
        for l in range(count):
            g_ref[quad * 4 + l] = gs[l]
        pack_quad(quad, gs, sn, mn, se, me, north_ref, south_ref, fold_scr, lon_scr, lonc_scr, True)

    for_quads(quad_body)
    fill_slots(slots_ref, fold_scr, lon_scr, lonc_scr, True)


def second_kernel(pre_ref, fold_ref, inv_hbm, sn_ref, mn_ref, depth_ref,
                  g_ref, slots_ref, north_ref, south_ref, lam, rest, fold_scr, lon_scr, sem):
    def levels_copy(quad, count):
        return pltpu.make_async_copy(inv_hbm.at[:, pl.ds(quad * 4, count)],
                                     rest.at[:, pl.ds((quad - HELD) * 4, count)], sem.at[quad - HELD])

    for quad in range(HELD, HELD + AHEAD):
        levels_copy(quad, 4).start()

    def put(j, cols, value):
        lam[j, :, cols] = value

    add_fold(pre_ref, fold_ref, depth_ref, put)
    depth = depth_ref[...]

    def quad_body(quad, count, source_ref, first_level):
        sums = vertical_sums(source_ref, lam, first_level, count)
        gs = [jnp.where(depth > quad * 4 + l, sums[l], 0.0) for l in range(count)]
        for l in range(count):
            g_ref[quad * 4 + l] = gs[l]
        pack_quad(quad, gs, sn_ref, mn_ref, None, None, north_ref, south_ref, fold_scr, lon_scr, None, False)

    def rest_quad(quad, carry):
        @pl.when(quad + AHEAD < FULL_QUADS)
        def _():
            levels_copy(quad + AHEAD, 4).start()

        @pl.when(quad + AHEAD == FULL_QUADS)
        def _():
            levels_copy(FULL_QUADS, TAIL).start()

        levels_copy(quad, 4).wait()
        quad_body(quad, 4, rest, (quad - HELD) * 4)
        return carry

    lax.fori_loop(HELD, FULL_QUADS, rest_quad, 0)
    levels_copy(FULL_QUADS, TAIL).wait()
    quad_body(FULL_QUADS, TAIL, rest, (FULL_QUADS - HELD) * 4)
    fill_slots(slots_ref, fold_scr, lon_scr, None, False)


def last_kernel(pre_ref, fold_ref, depth_ref, out_hbm, total, sem):
    def put(j, cols, value):
        total[j, :, cols] = value

    add_fold(pre_ref, fold_ref, depth_ref, put)
    copy = pltpu.make_async_copy(total, out_hbm, sem)
    copy.start()
    copy.wait()


def relay_kernel(fold_ref, in_ref, *rest):
    out_ref = rest[-1]
    for d in range(out_ref.shape[0]):
        out_ref[d] = in_ref[fold_ref[d]].astype(F32)[:ROWS].astype(BF16)


def shaped(shape, dtype):
    return jax.ShapeDtypeStruct(shape, dtype)


def per_device(lam, inverse, se, me, sn, mn, depth, fold_block):
    field = (LEV, ROWS, COLS)
    count = lax.axis_size("lon")
    lats = lax.axis_size("lat")
    vmem = pl.BlockSpec(memory_space=pltpu.VMEM)
    hbm = pl.BlockSpec(memory_space=pltpu.HBM)
    smem = pl.BlockSpec(memory_space=pltpu.SMEM)
    anywhere = pl.BlockSpec(memory_space=pl.ANY)
    coefs = [se, me, sn, mn]
    lon_scr = pltpu.VMEM((2, 2, ROWS, HALF), F32)
    fold_scr = pltpu.VMEM((20, ROWS, COLS), F32)
    bf_field = pltpu.VMEM(field, BF16)
    work = 2 * LEV * LEV * ROWS * COLS
    mib = 1024 * 1024
    beside = pl.CostEstimate(flops=work, bytes_accessed=2 * LEV * LEV * ROWS * COLS, transcendentals=0)

    def rims(north, south, rows):
        return [shaped((count, rows, COLS), BF16), shaped((north, QUADS, ROWS, COLS), BF16),
                shaped((south, QUADS, ROWS, COLS), BF16)]

    g1, slots1, north1, south1 = pl.pallas_call(
        first_kernel,
        in_specs=[hbm] * 7,
        out_specs=[vmem] * 4,
        out_shape=[shaped(field, F32)] + rims(3, 2, 3 * ROWS),
        scratch_shapes=[pltpu.VMEM(field, F32), pltpu.VMEM((LEV,) + field, BF16)] + [bf_field] * 4
        + [pltpu.VMEM((ROWS, COLS), jnp.int32), fold_scr, lon_scr, lon_scr,
           pltpu.SemaphoreType.DMA((6,)), pltpu.SemaphoreType.DMA((QUADS,))],
        compiler_params=pltpu.CompilerParams(vmem_limit_bytes=62 * mib),
        cost_estimate=pl.CostEstimate(flops=work, bytes_accessed=2 * LEV * LEV * ROWS * COLS, transcendentals=0),
        name="vertical_first",
    )(lam, inverse, *coefs, depth)

    up = [(i, (i + 1) % lats) for i in range(lats)]
    down = [(i, (i - 1) % lats) for i in range(lats)]

    def fold_route(slots, north, south, order):
        north = lax.ppermute(north, "lat", up)
        south = lax.ppermute(south, "lat", down)
        slots = lax.all_to_all(slots, "lon", 0, 0, tiled=True)
        relayed = pl.pallas_call(
            relay_kernel,
            in_specs=[smem, vmem] + [anywhere] * (2 * order),
            out_specs=vmem,
            out_shape=shaped((count, ROWS, COLS), BF16),
            compiler_params=pltpu.CompilerParams(vmem_limit_bytes=4 * mib),
            cost_estimate=beside,
            name="relay",
        )(fold_block, slots, *((north, south) if order else ()))
        return slots, north, south, lax.all_to_all(relayed, "lon", 0, 0, tiled=True)

    params = pltpu.CompilerParams(vmem_limit_bytes=4 * mib)
    slots1, north1, south1, fold1 = fold_route(slots1, north1, south1, False)
    pre1 = pl.pallas_call(
        transposed_h,
        in_specs=[vmem] * 12,
        out_specs=vmem,
        out_shape=shaped(field, F32),
        compiler_params=params,
        cost_estimate=beside,
        name="horizontal_first",
    )(g1, *coefs, depth, slots1, slots1, north1, south1, north1, south1)

    g2, slots2, north2, south2 = pl.pallas_call(
        second_kernel,
        in_specs=[vmem] * 2 + [hbm] + [vmem] * 3,
        out_specs=[vmem] * 4,
        out_shape=[shaped(field, F32)] + rims(1, 1, 2 * ROWS),
        scratch_shapes=[pltpu.VMEM(field, F32), pltpu.VMEM((LEV, LEV - 4 * HELD, ROWS, COLS), BF16), fold_scr, lon_scr,
                        pltpu.SemaphoreType.DMA((QUADS - HELD,))],
        compiler_params=pltpu.CompilerParams(vmem_limit_bytes=44 * mib),
        cost_estimate=pl.CostEstimate(flops=work, bytes_accessed=8 * LEV * ROWS * COLS, transcendentals=0),
        name="vertical_second",
    )(pre1, fold1, inverse, sn, mn, depth)

    slots2, north2, south2, fold2 = fold_route(slots2, north2, south2, True)
    pre2 = pl.pallas_call(
        transposed_h,
        in_specs=[vmem] * 12,
        out_specs=vmem,
        out_shape=shaped(field, F32),
        compiler_params=params,
        cost_estimate=beside,
        name="horizontal_second",
    )(g2, *coefs, depth, slots2, slots1, north2, south2, north1, south1)

    return pl.pallas_call(
        last_kernel,
        in_specs=[vmem] * 3,
        out_specs=hbm,
        out_shape=shaped(field, F32),
        scratch_shapes=[pltpu.VMEM(field, F32), pltpu.SemaphoreType.DMA],
        compiler_params=pltpu.CompilerParams(vmem_limit_bytes=4 * mib),
        name="add_fold",
    )(pre2, fold2, depth)


def solution(mesh):
    return jax.shard_map(
        per_device,
        mesh=mesh,
        in_specs=(
            P(None, "lat", "lon"),
            P(None, None, "lat", "lon"),
            P(None, "lat", "lon"),
            P(None, "lat", "lon"),
            P(None, "lat", "lon"),
            P(None, "lat", "lon"),
            P("lat", "lon"),
            P(),
        ),
        out_specs=P(None, "lat", "lon"),
        check_vma=False,
    )
```

time: 120 us -> 90.1 us (0.75)
  the two profiles are of different devices: /device:TPU:0 before, /device:TPU:1 now
where the time goes in v2:
time: 90.1 us; the launch traced here: 89.5 us
  starting transfers between devices  36.6 us (41%)
  Pallas kernels  34.3 us (38%)
  waiting for transfers between devices  14.8 us (16%)
  local copies, waits for them, and re-layouts  3.56 us (4%)
    all_to_all x2, starting transfers between devices, fold_route(): slots = lax.all_to_all(slots, 'lon', 0, 0, tiled=True)  15.9 us
    pallas_call x1, Pallas kernels, per_device(): pl.pallas_call(first_kernel, in_specs=[hbm] * 7, out_specs=[vmem] * 4, ou...  11.6 us
    all_to_all x2, starting transfers between devices, fold_route(): lax.all_to_all(relayed, 'lon', 0, 0, tiled=True)  11.1 us
    ppermute x2, starting transfers between devices, fold_route(): north = lax.ppermute(north, 'lat', up)  9.61 us
    pallas_call x2, Pallas kernels, per_device(): pl.pallas_call(transposed_h, in_specs=[vmem] * 12, out_specs=vmem, out_sh...  9.57 us
    pallas_call x1, Pallas kernels, per_device(): pl.pallas_call(second_kernel, in_specs=[vmem] * 2 + [hbm] + [vmem] * 3, o...  8.75 us
    all_to_all x2, waiting for transfers between devices, fold_route(): slots = lax.all_to_all(slots, 'lon', 0, 0, tiled=True)  6.54 us
    ppermute x2, waiting for transfers between devices, fold_route(): south = lax.ppermute(south, 'lat', down)  4.17 us
  transfers between devices with their start and end apart: 8, of which 5 were waited for; matrix products, arithmetic and copies ran while one was open for 0% of the time, Pallas kernels for 12%

profile of v2, /device:TPU:1, one launch (start us, length us, event | category | flops | bytes accessed | tf_op | source)
XLA Modules:
  0.0 89.5 jit_solution(11870532351999460363)
XLA Ops:
  0.0 11.6 %vertical_first.1 = (f32[75,8,256]{2,1,0:T(8,128)}, bf16[32,24,256]{2,1,0:T(8,128)(2,1)}, bf16[3,19,8,256]{3,2,1,0:T(8,128)(2,1)}, bf16[2,19,8,256]{3,2,1,0:T(8,128)(2,1)}) custom-call(f32[75,8,256]{2,1,0:T(8,128)} %lam_hbm.1, bf16[75,75,8,256]{3,2,1,0:T(8,128)(2,1)} %inv_hbm.3, bf16[75,8,256]{2,1,0:T(8,128)(2,1)} %se_ref.3, bf16[75,8,256]{2,1,0:T(8,128)(2,1)} %me_ref.3, ...), custom_call_target="tpu_custom_call" | custom-call | flops 23040000 | bytes 23040000 | tf_op jit(solution)/shard_map/vertical_first/pallas_call | solution.py:410
  11.7 9.8 %all-to-all-start = ((bf16[32,24,256]{2,1,0:T(8,128)(2,1)}), bf16[32,24,256]{2,1,0:T(8,128)(2,1)S(1)}, u32[]{:S(2)}, u32[]{:S(2)}) async-start(bf16[32,24,256]{2,1,0:T(8,128)(2,1)} %get-tuple-element.14), calls=%async_computation | async-start | bytes 786432 | tf_op jit(solution)/shard_map/all_to_all | solution.py:429
  21.5 3.4 %collective-permute-start = (bf16[3,19,8,256]{3,2,1,0:T(8,128)(2,1)}, bf16[3,19,8,256]{3,2,1,0:T(8,128)(2,1)S(1)}, u32[]{:S(2)}, u32[]{:S(2)}) collective-permute-start(bf16[3,19,8,256]{3,2,1,0:T(8,128)(2,1)} %get-tuple-element.15), channel_id=1, source_target_pairs={{0,1},{1,2},{2,3},{3,0},{4,5},{5,6},{6,7},{7,4},{8,9},{9,10},{10,1... | collective-permute-start | bytes 700424 | tf_op jit(solution)/shard_map/ppermute | solution.py:427
  24.9 6.5 %all-to-all-done.slots_ref.coef_slots_ref.in_ref = bf16[32,24,256]{2,1,0:T(8,128)(2,1)S(1)} async-done(((bf16[32,24,256]{2,1,0:T(8,128)(2,1)}), bf16[32,24,256]{2,1,0:T(8,128)(2,1)S(1)}, u32[]{:S(2)}, u32[]{:S(2)}) %all-to-all-start) | async-done | bytes 393248 | tf_op jit(solution)/shard_map/all_to_all | solution.py:429
  31.4 1.2 %relay.2 = bf16[32,8,256]{2,1,0:T(8,128)(2,1)} custom-call(s32[32]{0:T(128)S(1)} %copy-done.11, bf16[32,24,256]{2,1,0:T(8,128)(2,1)S(1)} %all-to-all-done.slots_ref.coef_slots_ref.in_ref), custom_call_target="tpu_custom_call" | custom-call | flops 23040000 | bytes 23040000 | tf_op jit(solution)/shard_map/relay/pallas_call | solution.py:430
  32.6 3.9 %all-to-all-start.1 = ((bf16[32,8,256]{2,1,0:T(8,128)(2,1)}), bf16[32,8,256]{2,1,0:T(8,128)(2,1)S(1)}, u32[]{:S(2)}, u32[]{:S(2)}) async-start(bf16[32,8,256]{2,1,0:T(8,128)(2,1)} %relay.2), calls=%async_computation.1 | async-start | bytes 262144 | tf_op jit(solution)/shard_map/all_to_all | solution.py:439
  36.6 0.0 copy-start.4
  36.6 1.1 %copy-done.4 = f32[75,8,256]{2,1,0:T(8,128)S(1)} copy-done((f32[75,8,256]{2,1,0:T(8,128)S(1)}, f32[75,8,256]{2,1,0:T(8,128)}, u32[]{:S(2)}) %copy-start.4) | copy-done | bytes 614424
  37.6 4.8 %horizontal_first.1.pre_ref = f32[75,8,256]{2,1,0:T(8,128)S(1)} custom-call(f32[75,8,256]{2,1,0:T(8,128)S(1)} %copy-done.4, bf16[75,8,256]{2,1,0:T(8,128)(2,1)S(1)} %copy-done.2, bf16[75,8,256]{2,1,0:T(8,128)(2,1)S(1)} %copy-done.3, bf16[75,8,256]{2,1,0:T(8,128)(2,1)S(1)} %copy-done, bf16[75,8,256]{2,1,0:T(8,128)(2,1)S(1)} %copy-done.1, ...), custom_call_target="tpu_custom_call" | custom-call | flops 23040000 | bytes 23040000 | tf_op jit(solution)/shard_map/horizontal_first/pallas_call | solution.py:443
  42.4 1.6 %all-to-all-done.1.fold_ref = bf16[32,8,256]{2,1,0:T(8,128)(2,1)S(1)} async-done(((bf16[32,8,256]{2,1,0:T(8,128)(2,1)}), bf16[32,8,256]{2,1,0:T(8,128)(2,1)S(1)}, u32[]{:S(2)}, u32[]{:S(2)}) %all-to-all-start.1) | async-done | bytes 131104 | tf_op jit(solution)/shard_map/all_to_all | solution.py:439
  44.1 8.7 %vertical_second.1 = (f32[75,8,256]{2,1,0:T(8,128)S(1)}, bf16[32,16,256]{2,1,0:T(8,128)(2,1)S(1)}, bf16[1,19,8,256]{3,2,1,0:T(8,128)(2,1)S(1)}, bf16[1,19,8,256]{3,2,1,0:T(8,128)(2,1)S(1)}) custom-call(f32[75,8,256]{2,1,0:T(8,128)S(1)} %horizontal_first.1.pre_ref, bf16[32,8,256]{2,1,0:T(8,128)(2,1)S(1)} %all-to-all-done.1.fold_ref, ...), custom_call_target="tpu_custom_call" | custom-call | flops 23040000 | bytes 1228800 | tf_op jit(solution)/shard_map/vertical_second/pallas_call | solution.py:453
  52.8 0.0 copy-start.9
  52.9 0.7 copy-done.9
  53.5 6.1 %all-to-all-start.2 = ((bf16[32,16,256]{2,1,0:T(8,128)(2,1)}), bf16[32,16,256]{2,1,0:T(8,128)(2,1)S(1)}, u32[]{:S(2)}, u32[]{:S(2)}) async-start(bf16[32,16,256]{2,1,0:T(8,128)(2,1)} %copy-done.9), calls=%async_computation.2 | async-start | bytes 524288 | tf_op jit(solution)/shard_map/all_to_all | solution.py:429
  59.7 6.3 %collective-permute-start.2 = (bf16[1,19,8,256]{3,2,1,0:T(8,128)(2,1)S(1)}, bf16[1,19,8,256]{3,2,1,0:T(8,128)(2,1)S(1)}, u32[]{:S(2)}, u32[]{:S(2)}) collective-permute-start(bf16[1,19,8,256]{3,2,1,0:T(8,128)(2,1)S(1)} %get-tuple-element.19), channel_id=1, source_target_pairs={{0,1},{1,2},{2,3},{3,0},{4,5},{5,6},{6,7},{7,4},{8,9},{9,10},{10,1... | collective-permute-start | bytes 233480 | tf_op jit(solution)/shard_map/ppermute | solution.py:427
  65.9 1.4 %collective-permute-done.2.north_ref.rest_0_ = bf16[1,19,8,256]{3,2,1,0:T(8,128)(2,1)S(1)} collective-permute-done((bf16[1,19,8,256]{3,2,1,0:T(8,128)(2,1)S(1)}, bf16[1,19,8,256]{3,2,1,0:T(8,128)(2,1)S(1)}, u32[]{:S(2)}, u32[]{:S(2)}) %collective-permute-start.2) | collective-permute-done | bytes 77856 | tf_op jit(solution)/shard_map/ppermute | solution.py:427
  67.4 4.2 %collective-permute-done.3.south_ref.rest_1_ = bf16[1,19,8,256]{3,2,1,0:T(8,128)(2,1)S(1)} collective-permute-done((bf16[1,19,8,256]{3,2,1,0:T(8,128)(2,1)S(1)}, bf16[1,19,8,256]{3,2,1,0:T(8,128)(2,1)S(1)}, u32[]{:S(2)}, u32[]{:S(2)}) %collective-permute-start.3) | collective-permute-done | bytes 77856 | tf_op jit(solution)/shard_map/ppermute | solution.py:428
  71.5 1.2 %relay.3 = bf16[32,8,256]{2,1,0:T(8,128)(2,1)} custom-call(s32[32]{0:T(128)S(1)} %copy-done.11, bf16[32,16,256]{2,1,0:T(8,128)(2,1)S(1)} %all-to-all-done.2.slots_ref.in_ref, bf16[1,19,8,256]{3,2,1,0:T(8,128)(2,1)S(1)} %collective-permute-done.2.north_ref.rest_0_, bf16[1,19,8,256]{3,2,1,0:T(8,128)(2,1)S(1)} %collective-permute-done.3.south_ref.rest_1_), custom_call_target="tpu_custom_call" | custom-call | flops 23040000 | bytes 23040000 | tf_op jit(solution)/shard_map/relay/pallas_call | solution.py:430
  72.8 7.2 %all-to-all-start.3 = ((bf16[32,8,256]{2,1,0:T(8,128)(2,1)}), bf16[32,8,256]{2,1,0:T(8,128)(2,1)}, u32[]{:S(2)}, u32[]{:S(2)}) async-start(bf16[32,8,256]{2,1,0:T(8,128)(2,1)} %relay.3), calls=%async_computation.3 | async-start | bytes 262144 | tf_op jit(solution)/shard_map/all_to_all | solution.py:439
  80.0 0.9 copy-done.6
  80.9 0.9 copy-done.8
  81.8 4.8 %horizontal_second.1.pre_ref = f32[75,8,256]{2,1,0:T(8,128)S(1)} custom-call(f32[75,8,256]{2,1,0:T(8,128)S(1)} %get-tuple-element.17.g_ref, bf16[75,8,256]{2,1,0:T(8,128)(2,1)S(1)} %copy-done.2, bf16[75,8,256]{2,1,0:T(8,128)(2,1)S(1)} %copy-done.3, bf16[75,8,256]{2,1,0:T(8,128)(2,1)S(1)} %copy-done, bf16[75,8,256]{2,1,0:T(8,128)(2,1)S(1)} %copy-done.1, ...), custom_call_target="tpu_custom_call" | custom-call | flops 23040000 | bytes 23040000 | tf_op jit(solution)/shard_map/horizontal_second/pallas_call | solution.py:466
  86.6 1.0 %all-to-all-done.3.fold_ref = bf16[32,8,256]{2,1,0:T(8,128)(2,1)} async-done(((bf16[32,8,256]{2,1,0:T(8,128)(2,1)}), bf16[32,8,256]{2,1,0:T(8,128)(2,1)}, u32[]{:S(2)}, u32[]{:S(2)}) %all-to-all-start.3) | async-done | bytes 131104 | tf_op jit(solution)/shard_map/all_to_all | solution.py:439
  87.6 1.9 %add_fold.1 = f32[75,8,256]{2,1,0:T(8,128)} custom-call(f32[75,8,256]{2,1,0:T(8,128)S(1)} %horizontal_second.1.pre_ref, bf16[32,8,256]{2,1,0:T(8,128)(2,1)} %all-to-all-done.3.fold_ref, s32[8,256]{1,0:T(8,128)S(1)} %copy-done.10), custom_call_target="tpu_custom_call" | custom-call | tf_op jit(solution)/shard_map/add_fold/pallas_call | solution.py:476
  (23 shorter events, 0.0 us)
Async XLA Ops:
  0.0 36.5 %copy-start.10 = (s32[8,256]{1,0:T(8,128)S(1)}, s32[8,256]{1,0:T(8,128)}, u32[]{:S(2)}) copy-start(s32[8,256]{1,0:T(8,128)} %depth_ref.7) | copy-start | bytes 24580
  0.0 36.5 %copy-start.1 = (bf16[75,8,256]{2,1,0:T(8,128)(2,1)S(1)}, bf16[75,8,256]{2,1,0:T(8,128)(2,1)}, u32[]{:S(2)}) copy-start(bf16[75,8,256]{2,1,0:T(8,128)(2,1)} %mn_ref.5) | copy-start | bytes 921604
  0.0 36.5 %copy-start = (bf16[75,8,256]{2,1,0:T(8,128)(2,1)S(1)}, bf16[75,8,256]{2,1,0:T(8,128)(2,1)}, u32[]{:S(2)}) copy-start(bf16[75,8,256]{2,1,0:T(8,128)(2,1)} %sn_ref.5) | copy-start | bytes 921604
  0.0 36.5 %copy-start.3 = (bf16[75,8,256]{2,1,0:T(8,128)(2,1)S(1)}, bf16[75,8,256]{2,1,0:T(8,128)(2,1)}, u32[]{:S(2)}) copy-start(bf16[75,8,256]{2,1,0:T(8,128)(2,1)} %me_ref.3) | copy-start | bytes 921604
  0.0 36.5 %copy-start.2 = (bf16[75,8,256]{2,1,0:T(8,128)(2,1)S(1)}, bf16[75,8,256]{2,1,0:T(8,128)(2,1)}, u32[]{:S(2)}) copy-start(bf16[75,8,256]{2,1,0:T(8,128)(2,1)} %se_ref.3) | copy-start | bytes 921604
  0.0 31.4 %copy-start.11 = (s32[32]{0:T(128)S(1)}, s32[32]{0:T(128)}, u32[]{:S(2)}) copy-start(s32[32]{0:T(128)} %fold_ref.3) | copy-start | bytes 388
  11.7 19.7 %all-to-all-start = ((bf16[32,24,256]{2,1,0:T(8,128)(2,1)}), bf16[32,24,256]{2,1,0:T(8,128)(2,1)S(1)}, u32[]{:S(2)}, u32[]{:S(2)}) async-start(bf16[32,24,256]{2,1,0:T(8,128)(2,1)} %get-tuple-element.14), calls=%async_computation | async-start | bytes 786432 | tf_op jit(solution)/shard_map/all_to_all | solution.py:429
  21.5 15.0 %collective-permute-start = (bf16[3,19,8,256]{3,2,1,0:T(8,128)(2,1)}, bf16[3,19,8,256]{3,2,1,0:T(8,128)(2,1)S(1)}, u32[]{:S(2)}, u32[]{:S(2)}) collective-permute-start(bf16[3,19,8,256]{3,2,1,0:T(8,128)(2,1)} %get-tuple-element.15), channel_id=1, source_target_pairs={{0,1},{1,2},{2,3},{3,0},{4,5},{5,6},{6,7},{7,4},{8,9},{9,10},{10,1... | collective-permute-start | bytes 700424 | tf_op jit(solution)/shard_map/ppermute | solution.py:427
  24.9 11.6 %collective-permute-start.1 = (bf16[2,19,8,256]{3,2,1,0:T(8,128)(2,1)}, bf16[2,19,8,256]{3,2,1,0:T(8,128)(2,1)S(1)}, u32[]{:S(2)}, u32[]{:S(2)}) collective-permute-start(bf16[2,19,8,256]{3,2,1,0:T(8,128)(2,1)} %get-tuple-element.16), channel_id=1, source_target_pairs={{0,3},{1,0},{2,1},{3,2},{4,7},{5,4},{6,5},{7,6},{8,11},{9,8},{10,9... | collective-permute-start | bytes 466952 | tf_op jit(solution)/shard_map/ppermute | solution.py:428
  32.6 11.4 %all-to-all-start.1 = ((bf16[32,8,256]{2,1,0:T(8,128)(2,1)}), bf16[32,8,256]{2,1,0:T(8,128)(2,1)S(1)}, u32[]{:S(2)}, u32[]{:S(2)}) async-start(bf16[32,8,256]{2,1,0:T(8,128)(2,1)} %relay.2), calls=%async_computation.1 | async-start | bytes 262144 | tf_op jit(solution)/shard_map/all_to_all | solution.py:439
  36.6 1.1 %copy-start.4 = (f32[75,8,256]{2,1,0:T(8,128)S(1)}, f32[75,8,256]{2,1,0:T(8,128)}, u32[]{:S(2)}) copy-start(f32[75,8,256]{2,1,0:T(8,128)} %get-tuple-element.13.g_ref) | copy-start | bytes 1843204
  52.8 0.7 copy-start.9
  53.5 18.0 %all-to-all-start.2 = ((bf16[32,16,256]{2,1,0:T(8,128)(2,1)}), bf16[32,16,256]{2,1,0:T(8,128)(2,1)S(1)}, u32[]{:S(2)}, u32[]{:S(2)}) async-start(bf16[32,16,256]{2,1,0:T(8,128)(2,1)} %copy-done.9), calls=%async_computation.2 | async-start | bytes 524288 | tf_op jit(solution)/shard_map/all_to_all | solution.py:429
  59.7 7.7 %collective-permute-start.2 = (bf16[1,19,8,256]{3,2,1,0:T(8,128)(2,1)S(1)}, bf16[1,19,8,256]{3,2,1,0:T(8,128)(2,1)S(1)}, u32[]{:S(2)}, u32[]{:S(2)}) collective-permute-start(bf16[1,19,8,256]{3,2,1,0:T(8,128)(2,1)S(1)} %get-tuple-element.19), channel_id=1, source_target_pairs={{0,1},{1,2},{2,3},{3,0},{4,5},{5,6},{6,7},{7,4},{8,9},{9,10},{10,1... | collective-permute-start | bytes 233480 | tf_op jit(solution)/shard_map/ppermute | solution.py:427
  65.9 5.6 %collective-permute-start.3 = (bf16[1,19,8,256]{3,2,1,0:T(8,128)(2,1)S(1)}, bf16[1,19,8,256]{3,2,1,0:T(8,128)(2,1)S(1)}, u32[]{:S(2)}, u32[]{:S(2)}) collective-permute-start(bf16[1,19,8,256]{3,2,1,0:T(8,128)(2,1)S(1)} %get-tuple-element.20), channel_id=1, source_target_pairs={{0,3},{1,0},{2,1},{3,2},{4,7},{5,4},{6,5},{7,6},{8,11},{9,8},{10,9... | collective-permute-start | bytes 233480 | tf_op jit(solution)/shard_map/ppermute | solution.py:428
  67.4 12.6 %copy-start.5 = (bf16[1,19,8,256]{3,2,1,0:T(8,128)(2,1)}, bf16[1,19,8,256]{3,2,1,0:T(8,128)(2,1)S(1)}, u32[]{:S(2)}) copy-start(bf16[1,19,8,256]{3,2,1,0:T(8,128)(2,1)S(1)} %collective-permute-done.2.north_ref.rest_0_) | copy-start | bytes 233476
  71.5 8.5 %copy-start.7 = (bf16[1,19,8,256]{3,2,1,0:T(8,128)(2,1)}, bf16[1,19,8,256]{3,2,1,0:T(8,128)(2,1)S(1)}, u32[]{:S(2)}) copy-start(bf16[1,19,8,256]{3,2,1,0:T(8,128)(2,1)S(1)} %collective-permute-done.3.south_ref.rest_1_) | copy-start | bytes 233476
  72.8 14.8 %all-to-all-start.3 = ((bf16[32,8,256]{2,1,0:T(8,128)(2,1)}), bf16[32,8,256]{2,1,0:T(8,128)(2,1)}, u32[]{:S(2)}, u32[]{:S(2)}) async-start(bf16[32,8,256]{2,1,0:T(8,128)(2,1)} %relay.3), calls=%async_computation.3 | async-start | bytes 262144 | tf_op jit(solution)/shard_map/all_to_all | solution.py:439
  80.0 0.9 copy-start.6
  80.9 0.9 copy-start.8

commit v3 on v2

v3 whole, which is shorter than its diff:
```python
import jax
import jax.numpy as jnp
from jax import lax
from jax.experimental import pallas as pl
from jax.experimental.pallas import tpu as pltpu
from jax.sharding import PartitionSpec as P

F32 = jnp.float32
BF16 = jnp.bfloat16
LEV = 75
ROWS = 8
COLS = 256
HALF = 128
QUADS = 19
FULL_QUADS = 18
AHEAD = 4
TOGETHER = 3
NEAR = 8
EXT = LEV + 3
TAIL = LEV - 4 * FULL_QUADS


def lane_ids():
    return lax.broadcasted_iota(jnp.int32, (ROWS, HALF), 1)


def row_ids():
    return lax.broadcasted_iota(jnp.int32, (ROWS, HALF), 0)


def turn(tile, shift, axis):
    size = tile.shape[axis]
    if isinstance(shift, int):
        shift = shift % size
        if shift == 0:
            return tile
    return pltpu.roll(tile, shift, axis)


def halves(value):
    return [value[:, :HALF], value[:, HALF:]]


def for_quads(body):
    def step(quad, carry):
        body(quad, 4)
        return carry

    lax.fori_loop(0, FULL_QUADS, step, 0)
    body(FULL_QUADS, TAIL)


def vertical_sums(inverse_ref, weighted_ref, first_level, count):
    sums = [None] * count
    for k in range(LEV):
        weight = weighted_ref[k]
        for jj in range(count):
            term = inverse_ref[k, first_level + jj].astype(F32) * weight
            sums[jj] = term if k == 0 else sums[jj] + term
    return sums


def sum_quads(inverse_ref, weighted_ref, depth, g_ref, levels_copy, pack):
    def sum_one(quad, count):
        sums = vertical_sums(inverse_ref, weighted_ref, quad * 4, count)
        for l in range(count):
            g_ref[quad * 4 + l] = jnp.where(depth > quad * 4 + l, sums[l], 0.0)

    def step(quad, carry):
        start_ahead(quad, levels_copy)
        levels_copy(quad, 4).wait()
        pack(jnp.maximum(quad - 1, 0), 4, lambda: sum_one(quad, 4))
        return carry

    lax.fori_loop(0, FULL_QUADS, step, 0)
    levels_copy(FULL_QUADS, TAIL).wait()
    pack(FULL_QUADS - 1, 4, lambda: sum_one(FULL_QUADS, TAIL))
    pack(FULL_QUADS, TAIL, None)


def place_lanes(acc_ref, side, quad, tiles, from_lane, ahead):
    which = quad // 16
    first = lax.rem(quad, 16) * 4
    lane = lane_ids()
    total = acc_ref[side, which]
    for l, tile in enumerate(tiles):
        spot = first + l
        rolled = pltpu.roll(tile, lax.rem(2 * spot + ahead + (2 * HALF - from_lane), HALF), 1)
        total = jnp.where((lane // 2) == lax.rem(spot + ahead // 2, 64), rolled, total)
    acc_ref[side, which] = total


def pack_quad(quad, count, g_ref, sn_ref, mn_ref, se_ref, me_ref, north_ref, south_ref,
              fold_scr, lon_scr, lonc_scr, with_coefs, beside=None):
    row = row_ids()
    gs = [g_ref[quad * 4 + l] for l in range(count)]
    is_top = lax.axis_index("lat") == lax.axis_size("lat") - 1

    def gathered(tiles_of, shift, ahead=0):
        for c in range(2):
            value = jnp.zeros((ROWS, HALF), F32)
            for l in range(count):
                moved = turn(tiles_of(l)[c], 2 * l + 2 * ahead - shift, 0)
                value = jnp.where((row // 2) == (l + ahead) % 4, moved, value)
            yield slice(c * HALF, (c + 1) * HALF), value

    def level_of(ref):
        return lambda l: halves(ref[quad * 4 + l].astype(F32))

    for cols, value in gathered(lambda l: halves(gs[l]), 0, 1):
        south_ref[0, quad, :, cols] = value.astype(BF16)
    if with_coefs:
        for cols, value in gathered(level_of(sn_ref), 0, 1):
            south_ref[1, quad, :, cols] = value.astype(BF16)

    place_lanes(lon_scr, 0, quad, [g[:, HALF:] for g in gs], 126, 0)
    place_lanes(lon_scr, 1, quad, [g[:, :HALF] for g in gs], 0, 2)
    if with_coefs:
        se = [level_of(se_ref)(l) for l in range(count)]
        me = [level_of(me_ref)(l)[1] for l in range(count)]
        place_lanes(lonc_scr, 0, quad, [tile[1] for tile in se], 126, 0)
        place_lanes(lonc_scr, 2, quad, me, 126, 0)
        place_lanes(lonc_scr, 1, quad, [tile[0] for tile in se], 0, 2)
    if beside is not None:
        beside()

    @pl.when(jnp.logical_not(is_top))
    def _():
        for cols, value in gathered(lambda l: halves(gs[l]), 6):
            north_ref[0, quad, :, cols] = value.astype(BF16)
        if with_coefs:
            for cols, value in gathered(level_of(sn_ref), 6):
                north_ref[1, quad, :, cols] = value.astype(BF16)
            for cols, value in gathered(level_of(mn_ref), 6):
                north_ref[2, quad, :, cols] = value.astype(BF16)

    @pl.when(is_top)
    def _():
        def ghosts(l):
            g = halves(gs[l])
            s = level_of(sn_ref)(l)
            m = level_of(mn_ref)(l)
            result = []
            for c in range(2):
                slope = s[c] * (1.0 / 12.0)
                direct = g[c] * (m[c] - 7.0 * slope)
                inner = (g[c] - turn(g[c], -1, 0)) * slope
                result.append(jnp.where(row == 7, direct + turn(inner, 1, 0), turn(slope * g[c], -1, 0)))
            return result

        for cols, value in gathered(ghosts, 6):
            fold_scr[quad, :, cols] = value


def fill_sends(slots_hbm, fold_scr, lon_scr, lonc_scr, flipped_scr, rim_scr, slot_sem, rim_sem):
    near = lax.axis_index("near")
    is_top = lax.axis_index("lat") == lax.axis_size("lat") - 1
    parts = rim_scr.shape[1]
    folds = [pltpu.make_async_copy(flipped_scr, slots_hbm.at[i, pl.ds(0, QUADS)], slot_sem.at[i])
             for i in range(NEAR)]
    rims = [pltpu.make_async_copy(rim_scr.at[side], slots_hbm.at[slot, pl.ds(QUADS, parts)], rim_sem.at[side])
            for side, slot in enumerate((lax.rem(near + 1, NEAR), lax.rem(near + NEAR - 1, NEAR)))]
    for side in range(2):
        for part, (ref, which) in enumerate(((lon_scr, side), (lonc_scr, side), (lonc_scr, 2))[:parts]):
            rim_scr[side, part] = jnp.concatenate([ref[which, 0], ref[which, 1]], axis=1).astype(BF16)
        rims[side].start()

    @pl.when(is_top)
    def _():
        r = lax.broadcasted_iota(jnp.int32, (COLS, COLS), 0)
        q = lax.broadcasted_iota(jnp.int32, (COLS, COLS), 1)
        mirror = (r + q == COLS - 1).astype(F32).astype(BF16)
        flat = fold_scr[...].reshape(20 * ROWS, COLS).astype(BF16)
        flipped = jnp.dot(flat, mirror, preferred_element_type=F32).reshape(20, ROWS, COLS)
        flipped_scr[...] = flipped[:QUADS].astype(BF16)
        for copy in folds:
            copy.start()
        for copy in folds:
            copy.wait()

    for copy in rims:
        copy.wait()


def transposed_h(g_ref, se_ref, me_ref, sn_ref, mn_ref, depth_ref, north_ref, south_ref,
                 north_c_ref, south_c_ref, out_ref):
    row = row_ids()
    lane = lane_ids()
    lat = lax.axis_index("lat")
    has_south = lat > 0
    has_north = lat < lax.axis_size("lat") - 1

    def kept(value, condition):
        return halves(jnp.where(condition, value.astype(F32), 0.0))

    def quad_body(quad, levels):
        g_n = kept(north_ref[0, quad], has_south)
        s_n = kept(north_c_ref[1, quad], has_south)
        m_n = kept(north_c_ref[2, quad], has_south)
        g_s = kept(south_ref[0, quad], has_north)
        s_s = kept(south_c_ref[1, quad], has_north)
        ready = []
        for l in range(levels):
            j = quad * 4 + l
            depth = halves(depth_ref[...])
            g = halves(g_ref[j])
            se = halves(se_ref[j].astype(F32))
            me = halves(me_ref[j].astype(F32))
            sn = halves(sn_ref[j].astype(F32))
            mn = halves(mn_ref[j].astype(F32))
            nothing = jnp.zeros((ROWS, HALF), F32)
            tiles = [g[0], g[1], nothing]
            jump = [turn(jnp.where(lane == 0, tiles[c + 1], tiles[c]), -1, 1) - tiles[c] for c in range(2)]
            speeds = [se[0], se[1]]
            mixes = [me[0], me[1]]
            far = [speeds[c] * (jump[c] * (1.0 / 12.0)) for c in range(2)] + [nothing]
            seven = [7.0 * far[c] for c in range(2)]
            mixed = [mixes[c] * jump[c] for c in range(2)]
            high = [seven[c] - mixed[c] for c in range(2)] + [nothing]
            total = []
            for c in range(2):
                before = (c + 2) % 3
                after = c + 1
                value = g[c] + seven[c] + mixed[c]
                value = value + turn(jnp.where(lane == 127, high[before], high[c]), 1, 1)
                value = value - turn(jnp.where(lane == 0, far[after], far[c]), -1, 1)
                value = value - turn(jnp.where(lane >= 126, far[before], far[c]), 2, 1)
                total.append(value)
            for c in range(2):
                pair = (row // 2) == l
                rim = turn(jnp.where(pair, g_n[c], g_s[c]), 6 - 2 * l, 0)
                s_r = turn(jnp.where(pair, s_n[c], s_s[c]), 6 - 2 * l, 0)
                m_r = turn(m_n[c], 6 - 2 * l, 0)
                d = turn(jnp.where(row == 0, rim, g[c]), -1, 0) - g[c]
                d_r = turn(jnp.where(row == 0, g[c], rim), -1, 0) - rim
                fa = sn[c] * (d * (1.0 / 12.0))
                fa_r = s_r * (d_r * (1.0 / 12.0))
                seven_y = 7.0 * fa
                mixed_y = mn[c] * d
                hi = seven_y - mixed_y
                hi_r = 7.0 * fa_r - m_r * d_r
                value = total[c] + seven_y + mixed_y
                value = value + turn(jnp.where(row == 7, hi_r, hi), 1, 0)
                value = value - turn(jnp.where(row == 0, fa_r, fa), -1, 0)
                value = value - turn(jnp.where(row >= 6, fa_r, fa), 2, 0)
                ready.append((j, c, jnp.where(depth[c] > j, value, 0.0)))
        for j, c, value in ready:
            out_ref[j, :, c * HALF:(c + 1) * HALF] = value

    for_quads(quad_body)
    for part in range(LEV, EXT):
        out_ref[part] = g_ref[part]


def lon_rims(near_ref, far1_ref, far3_ref, part):
    near = lax.axis_index("near")
    west = near_ref[lax.rem(near + NEAR - 1, NEAR), QUADS + part].astype(F32)
    east = near_ref[lax.rem(near + 1, NEAR), QUADS + part].astype(F32)
    west = jnp.where(near == 0, far1_ref[QUADS + part].astype(F32), west)
    east = jnp.where(near == NEAR - 1, far3_ref[QUADS + part].astype(F32), east)
    return west, east


def lon_edges(west_g, east_g, west_s, west_m, east_s, own_ref):
    lane = lane_ids()
    west_edge, east_edge = [], []
    even = lane % 2 == 0

    for w, e, own, w_s, w_m, e_s, o_s, o_m in zip(*map(halves, (
            west_g, east_g, own_ref[LEV], west_s, west_m, east_s, own_ref[LEV + 1], own_ref[LEV + 2]))):
        jump_w = jnp.where(even, turn(w, -1, 1), turn(own, -1, 1)) - w
        far_w = w_s * (jump_w * (1.0 / 12.0))
        high_w = 7.0 * far_w - w_m * jump_w
        west_edge.append(turn(jnp.where(even, turn(high_w, -1, 1) - far_w, -far_w), 2, 1))
        next_e = turn(e, -1, 1)
        far_e = e_s * ((next_e - e) * (1.0 / 12.0))
        far_o = o_s * (next_e * (1.0 / 12.0))
        east_edge.append(jnp.where(even, -turn(far_o, -1, 1), 7.0 * far_o + o_m * next_e - turn(far_e, -1, 1)))
    return west_edge, east_edge


def place_of(block):
    return block // NEAR, lax.rem(block, NEAR)


def add_fold(pre_ref, fold_ref, near_ref, far_refs, rim_c, depth_ref, put, after=None):
    row = row_ids()
    lane = lane_ids()
    west_g, east_g = lon_rims(near_ref, far_refs[0], far_refs[2], 0)
    west_edge, east_edge = lon_edges(west_g, east_g, *rim_c, pre_ref)
    depth = halves(depth_ref[...])
    on_top = lax.axis_index("lat") == lax.axis_size("lat") - 1
    fars = lax.axis_size("far")
    my_far = lax.axis_index("far")
    far, near = place_of(fold_ref[my_far * NEAR + lax.axis_index("near")])
    steps = lax.rem(my_far - far + fars, fars)

    def quad_values(quad, levels):
        fold = near_ref[near, quad].astype(F32)
        for step, ref in enumerate(far_refs):
            fold = jnp.where(steps == step + 1, ref[quad].astype(F32), fold)
        fold = halves(fold)
        ready = []
        for l in range(levels):
            j = quad * 4 + l
            first = j < 64
            spot = lax.rem(j, 64)
            edge = jnp.where((lane // 2) == spot, jnp.where(first, east_edge[0], east_edge[1]),
                             jnp.where(first, west_edge[0], west_edge[1]))
            edge = pltpu.roll(edge, lax.rem(2 * HALF - 2 - 2 * spot, HALF), 1)
            for c in range(2):
                cols = slice(c * HALF, (c + 1) * HALF)
                at_edge = lane < 2 if c == 0 else lane >= 126
                more = jnp.where(at_edge, edge, 0.0)
                more = more + jnp.where(((row == 5) | (row == 6)) & on_top, turn(fold[c], 5 - 2 * l, 0), 0.0)
                ready.append((j, cols, pre_ref[j, :, cols] + jnp.where(depth[c] > j, more, 0.0)))
        return ready

    def several(step, carry):
        ready = []
        for part in range(TOGETHER):
            ready += quad_values(step * TOGETHER + part, 4)
        for j, cols, value in ready:
            put(j, cols, value)
        if after is not None:
            after(step * TOGETHER + TOGETHER - 1)
        return carry

    lax.fori_loop(0, FULL_QUADS // TOGETHER, several, 0)
    for j, cols, value in quad_values(FULL_QUADS, TAIL):
        put(j, cols, value)
    if after is not None:
        after(FULL_QUADS)


def start_ahead(quad, levels_copy):
    @pl.when(quad + AHEAD < FULL_QUADS)
    def _():
        levels_copy(quad + AHEAD, 4).start()

    @pl.when(quad + AHEAD == FULL_QUADS)
    def _():
        levels_copy(FULL_QUADS, TAIL).start()


def first_kernel(lam_hbm, inv_hbm, se_hbm, me_hbm, sn_hbm, mn_hbm, depth_hbm,
                 g_ref, slots_hbm, north_ref, south_ref,
                 lam, inverse, se, me, sn, mn, depth_ref, fold_scr, lon_scr, lonc_scr,
                 flipped_scr, rim_scr, small_sem, sem, slot_sem, rim_sem):
    small = [pltpu.make_async_copy(src, dst, small_sem.at[i])
             for i, (src, dst) in enumerate([(depth_hbm, depth_ref), (lam_hbm, lam), (sn_hbm, sn),
                                             (mn_hbm, mn), (se_hbm, se), (me_hbm, me)])]

    def levels_copy(quad, count):
        part = pl.ds(quad * 4, count)
        return pltpu.make_async_copy(inv_hbm.at[:, part], inverse.at[:, part], sem.at[quad])

    small[0].start()
    small[1].start()
    levels_copy(0, 4).start()
    levels_copy(1, 4).start()
    for copy in small[2:]:
        copy.start()
    for quad in range(2, AHEAD):
        levels_copy(quad, 4).start()
    small[0].wait()
    small[1].wait()
    depth = depth_ref[...]

    def mask(k, carry):
        lam[k] = jnp.where(depth > k, lam[k], 0.0)
        return carry

    lax.fori_loop(0, LEV, mask, 0, unroll=5)
    for copy in small[2:]:
        copy.wait()

    def pack(quad, count, beside):
        pack_quad(quad, count, g_ref, sn, mn, se, me, north_ref, south_ref, fold_scr, lon_scr, lonc_scr, True, beside)

    sum_quads(inverse, lam, depth, g_ref, levels_copy, pack)
    for part, (ref, side) in enumerate(((lon_scr, 1), (lonc_scr, 0), (lonc_scr, 2))):
        g_ref[LEV + part] = jnp.concatenate([ref[side, 0], ref[side, 1]], axis=1)
    fill_sends(slots_hbm, fold_scr, lon_scr, lonc_scr, flipped_scr, rim_scr, slot_sem, rim_sem)


def second_kernel(pre_ref, fold_ref, near_ref, far1_ref, far2_ref, far3_ref,
                  inv_hbm, sn_ref, mn_ref, depth_ref,
                  g_ref, slots_hbm, north_ref, south_ref, rim_c_ref,
                  lam, inverse, fold_scr, lon_scr, flipped_scr, rim_scr, sem, slot_sem, rim_sem):
    def levels_copy(quad, count):
        part = pl.ds(quad * 4, count)
        return pltpu.make_async_copy(inv_hbm.at[:, part], inverse.at[:, part], sem.at[quad])

    for quad in range(AHEAD):
        levels_copy(quad, 4).start()

    def put(j, cols, value):
        lam[j, :, cols] = value

    west_s, east_s = lon_rims(near_ref, far1_ref, far3_ref, 1)
    west_m, _ = lon_rims(near_ref, far1_ref, far3_ref, 2)
    for part, tile in enumerate((west_s, west_m, east_s)):
        rim_c_ref[part] = tile
    add_fold(pre_ref, fold_ref, near_ref, (far1_ref, far2_ref, far3_ref), (west_s, west_m, east_s), depth_ref, put)
    depth = depth_ref[...]

    def pack(quad, count, beside):
        pack_quad(quad, count, g_ref, sn_ref, mn_ref, None, None, north_ref, south_ref, fold_scr, lon_scr, None, False,
                  beside)

    sum_quads(inverse, lam, depth, g_ref, levels_copy, pack)
    g_ref[LEV] = jnp.concatenate([lon_scr[1, 0], lon_scr[1, 1]], axis=1)
    for part in range(LEV + 1, EXT):
        g_ref[part] = pre_ref[part]
    fill_sends(slots_hbm, fold_scr, lon_scr, None, flipped_scr, rim_scr, slot_sem, rim_sem)


def last_kernel(pre_ref, fold_ref, near_ref, far1_ref, far2_ref, far3_ref,
                rim_c_ref, depth_ref, out_hbm, total, sem):
    copies = [pltpu.make_async_copy(total.at[pl.ds(start, size)], out_hbm.at[pl.ds(start, size)], sem.at[i])
              for i, (start, size) in enumerate(((0, 24), (24, 24), (48, 27)))]

    def put(j, cols, value):
        total[j, :, cols] = value

    def after(quad):
        for i, last in enumerate((5, 11, FULL_QUADS)):
            @pl.when(quad == last)
            def _(copy=copies[i]):
                copy.start()

    add_fold(pre_ref, fold_ref, near_ref, (far1_ref, far2_ref, far3_ref),
             [rim_c_ref[part] for part in range(3)], depth_ref, put, after)
    for copy in copies:
        copy.wait()


def relay_kernel(fold_ref, near_ref, *refs):
    fars = lax.axis_size("far")
    my_far = lax.axis_index("far")
    my_near = lax.axis_index("near")
    far1_ref, _, far3_ref = refs[-3:]
    for ref, slot in ((far1_ref, lax.rem(my_near + NEAR - 1, NEAR)), (far3_ref, lax.rem(my_near + 1, NEAR))):
        for part in range(QUADS, ref.shape[0]):
            ref[part] = near_ref[slot, part]

    @pl.when(lax.axis_index("lat") == lax.axis_size("lat") - 1)
    def _():
        for step, out_ref in enumerate(refs[-3:]):
            target = lax.rem(my_far + step + 1, fars)
            _, near = place_of(fold_ref[target * NEAR + my_near])
            for quad in range(QUADS):
                out_ref[quad] = near_ref[near, quad]


def shaped(shape, dtype):
    return jax.ShapeDtypeStruct(shape, dtype)


def per_device(lam, inverse, se, me, sn, mn, depth, fold_block):
    field = (LEV, ROWS, COLS)
    extended = (EXT, ROWS, COLS)
    lats = lax.axis_size("lat")
    count = lax.axis_size("far") * NEAR
    lon = ("far", "near")
    vmem = pl.BlockSpec(memory_space=pltpu.VMEM)
    hbm = pl.BlockSpec(memory_space=pltpu.HBM)
    smem = pl.BlockSpec(memory_space=pltpu.SMEM)
    coefs = [se, me, sn, mn]
    lon_scr = pltpu.VMEM((2, 2, ROWS, HALF), F32)
    fold_scr = pltpu.VMEM((20, ROWS, COLS), F32)
    inverse_scr = pltpu.VMEM((LEV,) + field, BF16)
    quad_sems = pltpu.SemaphoreType.DMA((QUADS,))
    slot_sems = [pltpu.SemaphoreType.DMA((NEAR,)), pltpu.SemaphoreType.DMA((2,))]
    work = 2 * LEV * LEV * ROWS * COLS
    mib = 1024 * 1024
    block = (QUADS, ROWS, COLS)

    def cost(bytes_accessed):
        return pl.CostEstimate(flops=work, bytes_accessed=bytes_accessed, transcendentals=0)

    def limit(size):
        return pltpu.CompilerParams(vmem_limit_bytes=size * mib)

    def sends(north, south, parts):
        return [shaped((NEAR, QUADS + parts, ROWS, COLS), BF16), shaped((north,) + block, BF16),
                shaped((south,) + block, BF16)]

    def staging(parts):
        return [pltpu.VMEM(block, BF16), pltpu.VMEM((2, parts, ROWS, COLS), BF16)]

    g1, *sent1 = pl.pallas_call(
        first_kernel,
        in_specs=[hbm] * 7,
        out_specs=[vmem, hbm, vmem, vmem],
        out_shape=[shaped(extended, F32)] + sends(3, 2, 3),
        scratch_shapes=[pltpu.VMEM(field, F32), inverse_scr] + [pltpu.VMEM(field, BF16)] * 4
        + [pltpu.VMEM((ROWS, COLS), jnp.int32), fold_scr, lon_scr, pltpu.VMEM((3, 2, ROWS, HALF), F32)]
        + staging(3) + [pltpu.SemaphoreType.DMA((6,)), quad_sems] + slot_sems,
        compiler_params=limit(62),
        cost_estimate=cost(work),
        name="vertical_first",
    )(lam, inverse, *coefs, depth)

    def ring(size, shift):
        return [(i, (i + shift) % size) for i in range(size)]

    def exchange(slots, north, south):
        near = lax.all_to_all(slots, "near", 0, 0, tiled=True)
        rims = [lax.ppermute(north, "lat", ring(lats, 1)), lax.ppermute(south, "lat", ring(lats, -1))]
        parts = slots.shape[1]
        north, south, *fars = pl.pallas_call(
            relay_kernel,
            in_specs=[smem] + [vmem] * 3,
            out_specs=[vmem] * 5,
            out_shape=[shaped(rim.shape, BF16) for rim in rims]
            + [shaped((size, ROWS, COLS), BF16) for size in (parts, QUADS, parts)],
            input_output_aliases={2: 0, 3: 1},
            compiler_params=limit(4),
            cost_estimate=cost(work),
            name="relay",
        )(fold_block, near, *rims)
        far = [lax.ppermute(part, lon, ring(count, NEAR * (step + 1))) for step, part in enumerate(fars)]
        return (north, south), (near, *far)

    def stencil(g, rims, rims_c):
        return pl.pallas_call(
            transposed_h,
            in_specs=[vmem] * 10,
            out_specs=vmem,
            out_shape=shaped(extended, F32),
            compiler_params=limit(4),
            cost_estimate=cost(work),
            name="horizontal",
        )(g, *coefs, depth, *rims, *rims_c)

    rims1, folds1 = exchange(*sent1)
    pre1 = stencil(g1, rims1, rims1)

    g2, *sent2, rim_c = pl.pallas_call(
        second_kernel,
        in_specs=[vmem, smem] + [vmem] * 4 + [hbm] + [vmem] * 3,
        out_specs=[vmem, hbm, vmem, vmem, vmem],
        out_shape=[shaped(extended, F32)] + sends(1, 1, 1) + [shaped((3, ROWS, COLS), F32)],
        scratch_shapes=[pltpu.VMEM(field, F32), inverse_scr, fold_scr, lon_scr] + staging(1) + [quad_sems] + slot_sems,
        compiler_params=limit(44),
        cost_estimate=cost(work),
        name="vertical_second",
    )(pre1, fold_block, *folds1, inverse, sn, mn, depth)

    rims2, folds2 = exchange(*sent2)
    pre2 = stencil(g2, rims2, rims1)

    return pl.pallas_call(
        last_kernel,
        in_specs=[vmem, smem] + [vmem] * 6,
        out_specs=hbm,
        out_shape=shaped(field, F32),
        scratch_shapes=[pltpu.VMEM(field, F32), pltpu.SemaphoreType.DMA((3,))],
        compiler_params=limit(4),
        name="add_fold",
    )(pre2, fold_block, *folds2, rim_c, depth)


def solution(mesh):
    lons, lats = mesh.devices.shape
    split = jax.sharding.Mesh(mesh.devices.reshape(lons // NEAR, NEAR, lats), ("far", "near", "lat"))
    lon = ("far", "near")
    field = P(None, "lat", lon)
    return jax.shard_map(
        per_device,
        mesh=split,
        in_specs=(field, P(None, None, "lat", lon), field, field, field, field, P("lat", lon), P()),
        out_specs=field,
        check_vma=False,
    )
```

time: 90.1 us -> 82.5 us (0.916)
  the two profiles are of different devices: /device:TPU:1 before, /device:TPU:0 now
where the time goes in v3:
time: 82.5 us; the launch traced here: 82.2 us
  Pallas kernels  31.3 us (38%)
  starting transfers between devices  26.6 us (32%)
  waiting for transfers between devices  23.1 us (28%)
  local copies, waits for them, and re-layouts  1.1 us (1%)
    pallas_call x1, Pallas kernels, per_device(): pl.pallas_call(first_kernel, in_specs=[hbm] * 7, out_specs=[vmem, hbm, vm...  11.5 us
    all_to_all x2, starting transfers between devices, exchange(): near = lax.all_to_all(slots, 'near', 0, 0, tiled=True)  11 us
    ppermute x2, waiting for transfers between devices, exchange(): lax.ppermute(north, 'lat', ring(lats, 1))  10.1 us
    pallas_call x1, Pallas kernels, per_device(): pl.pallas_call(second_kernel, in_specs=[vmem, smem] + [vmem] * 4 + [hbm]...  9.68 us
    ppermute x6, starting transfers between devices, exchange(): lax.ppermute(part, lon, ring(count, NEAR * (step + 1)))  9.07 us
    ppermute x2, waiting for transfers between devices, exchange(): lax.ppermute(south, 'lat', ring(lats, -1))  8.9 us
    pallas_call x2, Pallas kernels, stencil(): pl.pallas_call(transposed_h, in_specs=[vmem] * 10, out_specs=vmem, out_sh...  6.74 us
    ppermute x2, starting transfers between devices, exchange(): lax.ppermute(south, 'lat', ring(lats, -1))  6.48 us
  transfers between devices with their start and end apart: 12, of which 5 were waited for; matrix products, arithmetic and copies ran while one was open for 0% of the time, Pallas kernels for 8%

profile of v3, /device:TPU:0, one launch (start us, length us, event | category | flops | bytes accessed | tf_op | source)
XLA Modules:
  0.0 82.2 jit_solution(704453532892088735)
XLA Ops:
  0.0 11.5 %vertical_first.1 = (f32[78,8,256]{2,1,0:T(8,128)}, bf16[8,22,8,256]{3,2,1,0:T(8,128)(2,1)}, bf16[3,19,8,256]{3,2,1,0:T(8,128)(2,1)}, bf16[2,19,8,256]{3,2,1,0:T(8,128)(2,1)}) custom-call(f32[75,8,256]{2,1,0:T(8,128)} %lam_hbm.1, bf16[75,75,8,256]{3,2,1,0:T(8,128)(2,1)} %inv_hbm.3, bf16[75,8,256]{2,1,0:T(8,128)(2,1)} %se_ref.3, bf16[75,8,256]{2,1,0:T(8,128)(2,1)} %me_ref.3, ...), custom_call_target="tpu_custom_call" | custom-call | flops 23040000 | bytes 23040000 | tf_op jit(solution)/shard_map/vertical_first/pallas_call | solution.py:493
  11.5 6.4 %all-to-all-start = ((bf16[8,22,8,256]{3,2,1,0:T(8,128)(2,1)}), bf16[8,22,8,256]{3,2,1,0:T(8,128)(2,1)S(1)}, u32[]{:S(2)}, u32[]{:S(2)}) async-start(bf16[8,22,8,256]{3,2,1,0:T(8,128)(2,1)} %get-tuple-element.25), calls=%async_computation | async-start | bytes 1441792 | tf_op jit(solution)/shard_map/all_to_all | solution.py:510
  17.9 0.0 collective-permute-start
  17.9 3.2 %collective-permute-start.1 = (bf16[2,19,8,256]{3,2,1,0:T(8,128)(2,1)}, bf16[2,19,8,256]{3,2,1,0:T(8,128)(2,1)S(1)}, u32[]{:S(2)}, u32[]{:S(2)}) collective-permute-start(bf16[2,19,8,256]{3,2,1,0:T(8,128)(2,1)} %get-tuple-element.27), channel_id=1, source_target_pairs={{0,3},{1,0},{2,1},{3,2},{4,7},{5,4},{6,5},{7,6},{8,11},{9,8},{10,9... | collective-permute-start | bytes 466952 | tf_op jit(solution)/shard_map/ppermute | solution.py:511
  21.1 8.9 %collective-permute-done.1.refs_1_ = bf16[2,19,8,256]{3,2,1,0:T(8,128)(2,1)S(1)} collective-permute-done((bf16[2,19,8,256]{3,2,1,0:T(8,128)(2,1)}, bf16[2,19,8,256]{3,2,1,0:T(8,128)(2,1)S(1)}, u32[]{:S(2)}, u32[]{:S(2)}) %collective-permute-start.1) | collective-permute-done | bytes 155680 | tf_op jit(solution)/shard_map/ppermute | solution.py:511
  30.0 3.6 %collective-permute-done.refs_0_ = bf16[3,19,8,256]{3,2,1,0:T(8,128)(2,1)S(1)} collective-permute-done((bf16[3,19,8,256]{3,2,1,0:T(8,128)(2,1)}, bf16[3,19,8,256]{3,2,1,0:T(8,128)(2,1)S(1)}, u32[]{:S(2)}, u32[]{:S(2)}) %collective-permute-start) | collective-permute-done | bytes 233504 | tf_op jit(solution)/shard_map/ppermute | solution.py:511
  33.6 0.6 relay.2
  34.2 1.6 %collective-permute-start.2 = (bf16[22,8,256]{2,1,0:T(8,128)(2,1)S(1)}, bf16[22,8,256]{2,1,0:T(8,128)(2,1)S(1)}, u32[]{:S(2)}, u32[]{:S(2)}) collective-permute-start(bf16[22,8,256]{2,1,0:T(8,128)(2,1)S(1)} %get-tuple-element.30), channel_id=1, source_target_pairs={{0,32},{4,36},{8,40},{12,44},{16,48},{20,52},{24,56},{28,60},{32,6... | collective-permute-start | bytes 270344 | tf_op jit(solution)/shard_map/ppermute | solution.py:524
  35.8 1.7 %collective-permute-start.4 = (bf16[22,8,256]{2,1,0:T(8,128)(2,1)S(1)}, bf16[22,8,256]{2,1,0:T(8,128)(2,1)S(1)}, u32[]{:S(2)}, u32[]{:S(2)}) collective-permute-start(bf16[22,8,256]{2,1,0:T(8,128)(2,1)S(1)} %get-tuple-element.32), channel_id=1, source_target_pairs={{0,96},{4,100},{8,104},{12,108},{16,112},{20,116},{24,120},{28,124... | collective-permute-start | bytes 270344 | tf_op jit(solution)/shard_map/ppermute | solution.py:524
  37.5 2.0 %collective-permute-start.3 = (bf16[19,8,256]{2,1,0:T(8,128)(2,1)S(1)}, bf16[19,8,256]{2,1,0:T(8,128)(2,1)S(1)}, u32[]{:S(2)}, u32[]{:S(2)}) collective-permute-start(bf16[19,8,256]{2,1,0:T(8,128)(2,1)S(1)} %get-tuple-element.31), channel_id=1, source_target_pairs={{0,64},{4,68},{8,72},{12,76},{16,80},{20,84},{24,88},{28,92},{32,9... | collective-permute-start | bytes 233480 | tf_op jit(solution)/shard_map/ppermute | solution.py:524
  39.5 1.1 %copy-done.4 = f32[78,8,256]{2,1,0:T(8,128)S(1)} copy-done((f32[78,8,256]{2,1,0:T(8,128)S(1)}, f32[78,8,256]{2,1,0:T(8,128)}, u32[]{:S(2)}) %copy-start.4) | copy-done | bytes 639000
  40.6 3.4 %horizontal.2.pre_ref = f32[78,8,256]{2,1,0:T(8,128)S(1)} custom-call(f32[78,8,256]{2,1,0:T(8,128)S(1)} %copy-done.4, bf16[75,8,256]{2,1,0:T(8,128)(2,1)S(1)} %copy-done.2, bf16[75,8,256]{2,1,0:T(8,128)(2,1)S(1)} %copy-done.3, bf16[75,8,256]{2,1,0:T(8,128)(2,1)S(1)} %copy-done, bf16[75,8,256]{2,1,0:T(8,128)(2,1)S(1)} %copy-done.1, s32[8,256]{1,0:T(8,128)S(1)} %copy-done.5, ...), custom_call_target="tpu_custom_call" | custom-call | flops 23040000 | bytes 23040000 | tf_op jit(solution)/shard_map/horizontal/pallas_call | solution.py:528
  44.0 9.7 %vertical_second.1 = (f32[78,8,256]{2,1,0:T(8,128)S(1)}, bf16[8,20,8,256]{3,2,1,0:T(8,128)(2,1)}, bf16[1,19,8,256]{3,2,1,0:T(8,128)(2,1)S(1)}, bf16[1,19,8,256]{3,2,1,0:T(8,128)(2,1)S(1)}, f32[3,8,256]{2,1,0:T(8,128)S(1)}) custom-call(f32[78,8,256]{2,1,0:T(8,128)S(1)} %horizontal.2.pre_ref, s32[32]{0:T(128)S(1)} %copy-done.6, ...), custom_call_target="tpu_custom_call" | custom-call | flops 23040000 | bytes 23040000 | tf_op jit(solution)/shard_map/vertical_second/pallas_call | solution.py:541
  53.7 4.7 %all-to-all-start.1 = ((bf16[8,20,8,256]{3,2,1,0:T(8,128)(2,1)}), bf16[8,20,8,256]{3,2,1,0:T(8,128)(2,1)S(1)}, u32[]{:S(2)}, u32[]{:S(2)}) async-start(bf16[8,20,8,256]{3,2,1,0:T(8,128)(2,1)} %get-tuple-element.34), calls=%async_computation.1 | async-start | bytes 1310720 | tf_op jit(solution)/shard_map/all_to_all | solution.py:510
  58.4 3.2 %collective-permute-start.6 = (bf16[1,19,8,256]{3,2,1,0:T(8,128)(2,1)S(1)}, bf16[1,19,8,256]{3,2,1,0:T(8,128)(2,1)S(1)}, u32[]{:S(2)}, u32[]{:S(2)}) collective-permute-start(bf16[1,19,8,256]{3,2,1,0:T(8,128)(2,1)S(1)} %get-tuple-element.36), channel_id=1, source_target_pairs={{0,3},{1,0},{2,1},{3,2},{4,7},{5,4},{6,5},{7,6},{8,11},{9,8},{10,9... | collective-permute-start | bytes 233480 | tf_op jit(solution)/shard_map/ppermute | solution.py:511
  61.6 6.5 %collective-permute-done.5.refs_0_ = bf16[1,19,8,256]{3,2,1,0:T(8,128)(2,1)S(1)} collective-permute-done((bf16[1,19,8,256]{3,2,1,0:T(8,128)(2,1)S(1)}, bf16[1,19,8,256]{3,2,1,0:T(8,128)(2,1)S(1)}, u32[]{:S(2)}, u32[]{:S(2)}) %collective-permute-start.5) | collective-permute-done | bytes 77856 | tf_op jit(solution)/shard_map/ppermute | solution.py:511
  68.1 2.0 %all-to-all-done.1.near_ref = bf16[8,20,8,256]{3,2,1,0:T(8,128)(2,1)S(1)} async-done(((bf16[8,20,8,256]{3,2,1,0:T(8,128)(2,1)}), bf16[8,20,8,256]{3,2,1,0:T(8,128)(2,1)S(1)}, u32[]{:S(2)}, u32[]{:S(2)}) %all-to-all-start.1) | async-done | bytes 655392 | tf_op jit(solution)/shard_map/all_to_all | solution.py:510
  70.1 0.6 relay.3
  70.7 0.7 collective-permute-start.7
  71.4 2.6 %collective-permute-start.9 = (bf16[20,8,256]{2,1,0:T(8,128)(2,1)S(1)}, bf16[20,8,256]{2,1,0:T(8,128)(2,1)S(1)}, u32[]{:S(2)}, u32[]{:S(2)}) collective-permute-start(bf16[20,8,256]{2,1,0:T(8,128)(2,1)S(1)} %get-tuple-element.41), channel_id=1, source_target_pairs={{0,96},{4,100},{8,104},{12,108},{16,112},{20,116},{24,120},{28,124... | collective-permute-start | bytes 245768 | tf_op jit(solution)/shard_map/ppermute | solution.py:524
  74.0 0.5 collective-permute-start.8
  74.5 3.4 %horizontal.3.pre_ref = f32[78,8,256]{2,1,0:T(8,128)S(1)} custom-call(f32[78,8,256]{2,1,0:T(8,128)S(1)} %get-tuple-element.33.g_ref, bf16[75,8,256]{2,1,0:T(8,128)(2,1)S(1)} %copy-done.2, bf16[75,8,256]{2,1,0:T(8,128)(2,1)S(1)} %copy-done.3, bf16[75,8,256]{2,1,0:T(8,128)(2,1)S(1)} %copy-done, bf16[75,8,256]{2,1,0:T(8,128)(2,1)S(1)} %copy-done.1, ...), custom_call_target="tpu_custom_call" | custom-call | flops 23040000 | bytes 23040000 | tf_op jit(solution)/shard_map/horizontal/pallas_call | solution.py:528
  77.8 2.0 %collective-permute-done.8.far2_ref = bf16[19,8,256]{2,1,0:T(8,128)(2,1)S(1)} collective-permute-done((bf16[19,8,256]{2,1,0:T(8,128)(2,1)S(1)}, bf16[19,8,256]{2,1,0:T(8,128)(2,1)S(1)}, u32[]{:S(2)}, u32[]{:S(2)}) %collective-permute-start.8) | collective-permute-done | bytes 77856 | tf_op jit(solution)/shard_map/ppermute | solution.py:524
  79.9 2.3 %add_fold.1 = f32[75,8,256]{2,1,0:T(8,128)} custom-call(f32[78,8,256]{2,1,0:T(8,128)S(1)} %horizontal.3.pre_ref, s32[32]{0:T(128)S(1)} %copy-done.6, bf16[8,20,8,256]{3,2,1,0:T(8,128)(2,1)S(1)} %all-to-all-done.1.near_ref, bf16[20,8,256]{2,1,0:T(8,128)(2,1)S(1)} %collective-permute-done.7.far1_ref, bf16[19,8,256]{2,1,0:T(8,128)(2,1)S(1)} %collective-permute-done.8.far2_ref, ...), custom_call_target="tpu_custom_call" | custom-call | tf_op jit(solution)/shard_map/add_fold/pallas_call | solution.py:555
  (21 shorter events, 0.0 us)
Async XLA Ops:
  0.0 39.5 %copy-start.5 = (s32[8,256]{1,0:T(8,128)S(1)}, s32[8,256]{1,0:T(8,128)}, u32[]{:S(2)}) copy-start(s32[8,256]{1,0:T(8,128)} %depth_ref.7) | copy-start | bytes 24580
  0.0 39.5 %copy-start.1 = (bf16[75,8,256]{2,1,0:T(8,128)(2,1)S(1)}, bf16[75,8,256]{2,1,0:T(8,128)(2,1)}, u32[]{:S(2)}) copy-start(bf16[75,8,256]{2,1,0:T(8,128)(2,1)} %mn_ref.5) | copy-start | bytes 921604
  0.0 39.5 %copy-start = (bf16[75,8,256]{2,1,0:T(8,128)(2,1)S(1)}, bf16[75,8,256]{2,1,0:T(8,128)(2,1)}, u32[]{:S(2)}) copy-start(bf16[75,8,256]{2,1,0:T(8,128)(2,1)} %sn_ref.5) | copy-start | bytes 921604
  0.0 39.5 %copy-start.3 = (bf16[75,8,256]{2,1,0:T(8,128)(2,1)S(1)}, bf16[75,8,256]{2,1,0:T(8,128)(2,1)}, u32[]{:S(2)}) copy-start(bf16[75,8,256]{2,1,0:T(8,128)(2,1)} %me_ref.3) | copy-start | bytes 921604
  0.0 39.5 %copy-start.2 = (bf16[75,8,256]{2,1,0:T(8,128)(2,1)S(1)}, bf16[75,8,256]{2,1,0:T(8,128)(2,1)}, u32[]{:S(2)}) copy-start(bf16[75,8,256]{2,1,0:T(8,128)(2,1)} %se_ref.3) | copy-start | bytes 921604
  0.0 33.6 %copy-start.6 = (s32[32]{0:T(128)S(1)}, s32[32]{0:T(128)}, u32[]{:S(2)}) copy-start(s32[32]{0:T(128)} %fold_ref.7) | copy-start | bytes 388
  11.5 22.1 %all-to-all-start = ((bf16[8,22,8,256]{3,2,1,0:T(8,128)(2,1)}), bf16[8,22,8,256]{3,2,1,0:T(8,128)(2,1)S(1)}, u32[]{:S(2)}, u32[]{:S(2)}) async-start(bf16[8,22,8,256]{3,2,1,0:T(8,128)(2,1)} %get-tuple-element.25), calls=%async_computation | async-start | bytes 1441792 | tf_op jit(solution)/shard_map/all_to_all | solution.py:510
  17.9 15.7 %collective-permute-start = (bf16[3,19,8,256]{3,2,1,0:T(8,128)(2,1)}, bf16[3,19,8,256]{3,2,1,0:T(8,128)(2,1)S(1)}, u32[]{:S(2)}, u32[]{:S(2)}) collective-permute-start(bf16[3,19,8,256]{3,2,1,0:T(8,128)(2,1)} %get-tuple-element.26), channel_id=1, source_target_pairs={{0,1},{1,2},{2,3},{3,0},{4,5},{5,6},{6,7},{7,4},{8,9},{9,10},{10,1... | collective-permute-start | bytes 700424 | tf_op jit(solution)/shard_map/ppermute | solution.py:511
  17.9 12.1 %collective-permute-start.1 = (bf16[2,19,8,256]{3,2,1,0:T(8,128)(2,1)}, bf16[2,19,8,256]{3,2,1,0:T(8,128)(2,1)S(1)}, u32[]{:S(2)}, u32[]{:S(2)}) collective-permute-start(bf16[2,19,8,256]{3,2,1,0:T(8,128)(2,1)} %get-tuple-element.27), channel_id=1, source_target_pairs={{0,3},{1,0},{2,1},{3,2},{4,7},{5,4},{6,5},{7,6},{8,11},{9,8},{10,9... | collective-permute-start | bytes 466952 | tf_op jit(solution)/shard_map/ppermute | solution.py:511
  34.2 9.8 %collective-permute-start.2 = (bf16[22,8,256]{2,1,0:T(8,128)(2,1)S(1)}, bf16[22,8,256]{2,1,0:T(8,128)(2,1)S(1)}, u32[]{:S(2)}, u32[]{:S(2)}) collective-permute-start(bf16[22,8,256]{2,1,0:T(8,128)(2,1)S(1)} %get-tuple-element.30), channel_id=1, source_target_pairs={{0,32},{4,36},{8,40},{12,44},{16,48},{20,52},{24,56},{28,60},{32,6... | collective-permute-start | bytes 270344 | tf_op jit(solution)/shard_map/ppermute | solution.py:524
  35.8 8.2 %collective-permute-start.4 = (bf16[22,8,256]{2,1,0:T(8,128)(2,1)S(1)}, bf16[22,8,256]{2,1,0:T(8,128)(2,1)S(1)}, u32[]{:S(2)}, u32[]{:S(2)}) collective-permute-start(bf16[22,8,256]{2,1,0:T(8,128)(2,1)S(1)} %get-tuple-element.32), channel_id=1, source_target_pairs={{0,96},{4,100},{8,104},{12,108},{16,112},{20,116},{24,120},{28,124... | collective-permute-start | bytes 270344 | tf_op jit(solution)/shard_map/ppermute | solution.py:524
  37.5 6.5 %collective-permute-start.3 = (bf16[19,8,256]{2,1,0:T(8,128)(2,1)S(1)}, bf16[19,8,256]{2,1,0:T(8,128)(2,1)S(1)}, u32[]{:S(2)}, u32[]{:S(2)}) collective-permute-start(bf16[19,8,256]{2,1,0:T(8,128)(2,1)S(1)} %get-tuple-element.31), channel_id=1, source_target_pairs={{0,64},{4,68},{8,72},{12,76},{16,80},{20,84},{24,88},{28,92},{32,9... | collective-permute-start | bytes 233480 | tf_op jit(solution)/shard_map/ppermute | solution.py:524
  39.5 1.1 %copy-start.4 = (f32[78,8,256]{2,1,0:T(8,128)S(1)}, f32[78,8,256]{2,1,0:T(8,128)}, u32[]{:S(2)}) copy-start(f32[78,8,256]{2,1,0:T(8,128)} %get-tuple-element.24.g_ref) | copy-start | bytes 1916932
  53.7 16.4 %all-to-all-start.1 = ((bf16[8,20,8,256]{3,2,1,0:T(8,128)(2,1)}), bf16[8,20,8,256]{3,2,1,0:T(8,128)(2,1)S(1)}, u32[]{:S(2)}, u32[]{:S(2)}) async-start(bf16[8,20,8,256]{3,2,1,0:T(8,128)(2,1)} %get-tuple-element.34), calls=%async_computation.1 | async-start | bytes 1310720 | tf_op jit(solution)/shard_map/all_to_all | solution.py:510
  58.4 9.8 %collective-permute-start.5 = (bf16[1,19,8,256]{3,2,1,0:T(8,128)(2,1)S(1)}, bf16[1,19,8,256]{3,2,1,0:T(8,128)(2,1)S(1)}, u32[]{:S(2)}, u32[]{:S(2)}) collective-permute-start(bf16[1,19,8,256]{3,2,1,0:T(8,128)(2,1)S(1)} %get-tuple-element.35), channel_id=1, source_target_pairs={{0,1},{1,2},{2,3},{3,0},{4,5},{5,6},{6,7},{7,4},{8,9},{9,10},{10,1... | collective-permute-start | bytes 233480 | tf_op jit(solution)/shard_map/ppermute | solution.py:511
  58.4 9.8 %collective-permute-start.6 = (bf16[1,19,8,256]{3,2,1,0:T(8,128)(2,1)S(1)}, bf16[1,19,8,256]{3,2,1,0:T(8,128)(2,1)S(1)}, u32[]{:S(2)}, u32[]{:S(2)}) collective-permute-start(bf16[1,19,8,256]{3,2,1,0:T(8,128)(2,1)S(1)} %get-tuple-element.36), channel_id=1, source_target_pairs={{0,3},{1,0},{2,1},{3,2},{4,7},{5,4},{6,5},{7,6},{8,11},{9,8},{10,9... | collective-permute-start | bytes 233480 | tf_op jit(solution)/shard_map/ppermute | solution.py:511
  70.7 9.2 %collective-permute-start.7 = (bf16[20,8,256]{2,1,0:T(8,128)(2,1)S(1)}, bf16[20,8,256]{2,1,0:T(8,128)(2,1)S(1)}, u32[]{:S(2)}, u32[]{:S(2)}) collective-permute-start(bf16[20,8,256]{2,1,0:T(8,128)(2,1)S(1)} %get-tuple-element.39), channel_id=1, source_target_pairs={{0,32},{4,36},{8,40},{12,44},{16,48},{20,52},{24,56},{28,60},{32,6... | collective-permute-start | bytes 245768 | tf_op jit(solution)/shard_map/ppermute | solution.py:524
  71.4 8.5 %collective-permute-start.9 = (bf16[20,8,256]{2,1,0:T(8,128)(2,1)S(1)}, bf16[20,8,256]{2,1,0:T(8,128)(2,1)S(1)}, u32[]{:S(2)}, u32[]{:S(2)}) collective-permute-start(bf16[20,8,256]{2,1,0:T(8,128)(2,1)S(1)} %get-tuple-element.41), channel_id=1, source_target_pairs={{0,96},{4,100},{8,104},{12,108},{16,112},{20,116},{24,120},{28,124... | collective-permute-start | bytes 245768 | tf_op jit(solution)/shard_map/ppermute | solution.py:524
  74.0 5.9 %collective-permute-start.8 = (bf16[19,8,256]{2,1,0:T(8,128)(2,1)S(1)}, bf16[19,8,256]{2,1,0:T(8,128)(2,1)S(1)}, u32[]{:S(2)}, u32[]{:S(2)}) collective-permute-start(bf16[19,8,256]{2,1,0:T(8,128)(2,1)S(1)} %get-tuple-element.40), channel_id=1, source_target_pairs={{0,64},{4,68},{8,72},{12,76},{16,80},{20,84},{24,88},{28,92},{32,9... | collective-permute-start | bytes 233480 | tf_op jit(solution)/shard_map/ppermute | solution.py:524

commit v4 on v3

--- a/solution.py
+++ b/solution.py
@@ -14,9 +14,10 @@
 QUADS = 19
 FULL_QUADS = 18
 AHEAD = 4
-TOGETHER = 3
+TOGETHER = 6
 NEAR = 8
-EXT = LEV + 3
+OWN = LEV + 3
+EXT = LEV + 6
 TAIL = LEV - 4 * FULL_QUADS
 
 
@@ -107,12 +108,21 @@
     def level_of(ref):
         return lambda l: halves(ref[quad * 4 + l].astype(F32))
 
-    for cols, value in gathered(lambda l: halves(gs[l]), 0, 1):
+    def far_of(l, c):
+        g = halves(gs[l])[c]
+        return level_of(sn_ref)(l)[c] * ((turn(g, -1, 0) - g) * (1.0 / 12.0))
+
+    def south_rows(l):
+        return [jnp.where(row == 0, halves(gs[l])[c], turn(far_of(l, c), 1, 0)) for c in range(2)]
+
+    def north_rows(l):
+        return [jnp.where(row == 7, halves(gs[l])[c], far_of(l, c)) for c in range(2)]
+
+    def north_coefs(l):
+        return [jnp.where(row == 7, level_of(sn_ref)(l)[c], turn(level_of(mn_ref)(l)[c], -1, 0)) for c in range(2)]
+
+    for cols, value in gathered(south_rows, 0, 1):
         south_ref[0, quad, :, cols] = value.astype(BF16)
-    if with_coefs:
-        for cols, value in gathered(level_of(sn_ref), 0, 1):
-            south_ref[1, quad, :, cols] = value.astype(BF16)
-
     place_lanes(lon_scr, 0, quad, [g[:, HALF:] for g in gs], 126, 0)
     place_lanes(lon_scr, 1, quad, [g[:, :HALF] for g in gs], 0, 2)
     if with_coefs:
@@ -126,13 +136,11 @@
 
     @pl.when(jnp.logical_not(is_top))
     def _():
-        for cols, value in gathered(lambda l: halves(gs[l]), 6):
+        for cols, value in gathered(north_rows, 6):
             north_ref[0, quad, :, cols] = value.astype(BF16)
         if with_coefs:
-            for cols, value in gathered(level_of(sn_ref), 6):
+            for cols, value in gathered(north_coefs, 6):
                 north_ref[1, quad, :, cols] = value.astype(BF16)
-            for cols, value in gathered(level_of(mn_ref), 6):
-                north_ref[2, quad, :, cols] = value.astype(BF16)
 
     @pl.when(is_top)
     def _():
@@ -183,7 +191,7 @@
 
 
 def transposed_h(g_ref, se_ref, me_ref, sn_ref, mn_ref, depth_ref, north_ref, south_ref,
-                 north_c_ref, south_c_ref, out_ref):
+                 north_c_ref, out_ref):
     row = row_ids()
     lane = lane_ids()
     lat = lax.axis_index("lat")
@@ -195,10 +203,8 @@
 
     def quad_body(quad, levels):
         g_n = kept(north_ref[0, quad], has_south)
-        s_n = kept(north_c_ref[1, quad], has_south)
-        m_n = kept(north_c_ref[2, quad], has_south)
+        c_n = kept(north_c_ref[1, quad], has_south)
         g_s = kept(south_ref[0, quad], has_north)
-        s_s = kept(south_c_ref[1, quad], has_north)
         ready = []
         for l in range(levels):
             j = quad * 4 + l
@@ -229,12 +235,12 @@
             for c in range(2):
                 pair = (row // 2) == l
                 rim = turn(jnp.where(pair, g_n[c], g_s[c]), 6 - 2 * l, 0)
-                s_r = turn(jnp.where(pair, s_n[c], s_s[c]), 6 - 2 * l, 0)
-                m_r = turn(m_n[c], 6 - 2 * l, 0)
+                s_r = turn(c_n[c], 6 - 2 * l, 0)
+                m_r = turn(s_r, 1, 0)
                 d = turn(jnp.where(row == 0, rim, g[c]), -1, 0) - g[c]
                 d_r = turn(jnp.where(row == 0, g[c], rim), -1, 0) - rim
                 fa = sn[c] * (d * (1.0 / 12.0))
-                fa_r = s_r * (d_r * (1.0 / 12.0))
+                fa_r = jnp.where(row == 7, s_r * (d_r * (1.0 / 12.0)), jnp.where(row == 6, rim, turn(rim, -1, 0)))
                 seven_y = 7.0 * fa
                 mixed_y = mn[c] * d
                 hi = seven_y - mixed_y
@@ -386,7 +392,7 @@
 
 def second_kernel(pre_ref, fold_ref, near_ref, far1_ref, far2_ref, far3_ref,
                   inv_hbm, sn_ref, mn_ref, depth_ref,
-                  g_ref, slots_hbm, north_ref, south_ref, rim_c_ref,
+                  g_ref, slots_hbm, north_ref, south_ref,
                   lam, inverse, fold_scr, lon_scr, flipped_scr, rim_scr, sem, slot_sem, rim_sem):
     def levels_copy(quad, count):
         part = pl.ds(quad * 4, count)
@@ -401,7 +407,7 @@
     west_s, east_s = lon_rims(near_ref, far1_ref, far3_ref, 1)
     west_m, _ = lon_rims(near_ref, far1_ref, far3_ref, 2)
     for part, tile in enumerate((west_s, west_m, east_s)):
-        rim_c_ref[part] = tile
+        g_ref[OWN + part] = tile
     add_fold(pre_ref, fold_ref, near_ref, (far1_ref, far2_ref, far3_ref), (west_s, west_m, east_s), depth_ref, put)
     depth = depth_ref[...]
 
@@ -411,13 +417,13 @@
 
     sum_quads(inverse, lam, depth, g_ref, levels_copy, pack)
     g_ref[LEV] = jnp.concatenate([lon_scr[1, 0], lon_scr[1, 1]], axis=1)
-    for part in range(LEV + 1, EXT):
+    for part in range(LEV + 1, OWN):
         g_ref[part] = pre_ref[part]
     fill_sends(slots_hbm, fold_scr, lon_scr, None, flipped_scr, rim_scr, slot_sem, rim_sem)
 
 
 def last_kernel(pre_ref, fold_ref, near_ref, far1_ref, far2_ref, far3_ref,
-                rim_c_ref, depth_ref, out_hbm, total, sem):
+                depth_ref, out_hbm, total, sem):
     copies = [pltpu.make_async_copy(total.at[pl.ds(start, size)], out_hbm.at[pl.ds(start, size)], sem.at[i])
               for i, (start, size) in enumerate(((0, 24), (24, 24), (48, 27)))]
 
@@ -431,7 +437,7 @@
                 copy.start()
 
     add_fold(pre_ref, fold_ref, near_ref, (far1_ref, far2_ref, far3_ref),
-             [rim_c_ref[part] for part in range(3)], depth_ref, put, after)
+             [pre_ref[part] for part in range(OWN, EXT)], depth_ref, put, after)
     for copy in copies:
         copy.wait()
 
@@ -494,7 +500,7 @@
         first_kernel,
         in_specs=[hbm] * 7,
         out_specs=[vmem, hbm, vmem, vmem],
-        out_shape=[shaped(extended, F32)] + sends(3, 2, 3),
+        out_shape=[shaped(extended, F32)] + sends(2, 1, 3),
         scratch_shapes=[pltpu.VMEM(field, F32), inverse_scr] + [pltpu.VMEM(field, BF16)] * 4
         + [pltpu.VMEM((ROWS, COLS), jnp.int32), fold_scr, lon_scr, pltpu.VMEM((3, 2, ROWS, HALF), F32)]
         + staging(3) + [pltpu.SemaphoreType.DMA((6,)), quad_sems] + slot_sems,
@@ -506,61 +512,63 @@
     def ring(size, shift):
         return [(i, (i + shift) % size) for i in range(size)]
 
-    def exchange(slots, north, south):
+    def exchange(g, slots, north, south, *carried):
         near = lax.all_to_all(slots, "near", 0, 0, tiled=True)
         rims = [lax.ppermute(north, "lat", ring(lats, 1)), lax.ppermute(south, "lat", ring(lats, -1))]
         parts = slots.shape[1]
-        north, south, *fars = pl.pallas_call(
+        held = len(carried)
+        g, north, south, *rest = pl.pallas_call(
             relay_kernel,
-            in_specs=[smem] + [vmem] * 3,
-            out_specs=[vmem] * 5,
-            out_shape=[shaped(rim.shape, BF16) for rim in rims]
+            in_specs=[smem] + [vmem] * (4 + held),
+            out_specs=[vmem] * (6 + held),
+            out_shape=[shaped(extended, F32)] + [shaped(part.shape, BF16) for part in (*rims, *carried)]
             + [shaped((size, ROWS, COLS), BF16) for size in (parts, QUADS, parts)],
-            input_output_aliases={2: 0, 3: 1},
+            input_output_aliases={2 + i: i for i in range(3 + held)},
             compiler_params=limit(4),
             cost_estimate=cost(work),
             name="relay",
-        )(fold_block, near, *rims)
+        )(fold_block, near, g, *rims, *carried)
+        carried, fars = rest[:held], rest[held:]
         far = [lax.ppermute(part, lon, ring(count, NEAR * (step + 1))) for step, part in enumerate(fars)]
-        return (north, south), (near, *far)
-
-    def stencil(g, rims, rims_c):
+        return g, (north, south), (near, *far), carried
+
+    def stencil(g, rims, north_c):
         return pl.pallas_call(
             transposed_h,
-            in_specs=[vmem] * 10,
+            in_specs=[vmem] * 9,
             out_specs=vmem,
             out_shape=shaped(extended, F32),
             compiler_params=limit(4),
             cost_estimate=cost(work),
             name="horizontal",
-        )(g, *coefs, depth, *rims, *rims_c)
-
-    rims1, folds1 = exchange(*sent1)
-    pre1 = stencil(g1, rims1, rims1)
-
-    g2, *sent2, rim_c = pl.pallas_call(
+        )(g, *coefs, depth, *rims, north_c)
+
+    g1, rims1, folds1, _ = exchange(g1, *sent1)
+    pre1 = stencil(g1, rims1, rims1[0])
+
+    g2, *sent2 = pl.pallas_call(
         second_kernel,
         in_specs=[vmem, smem] + [vmem] * 4 + [hbm] + [vmem] * 3,
-        out_specs=[vmem, hbm, vmem, vmem, vmem],
-        out_shape=[shaped(extended, F32)] + sends(1, 1, 1) + [shaped((3, ROWS, COLS), F32)],
+        out_specs=[vmem, hbm, vmem, vmem],
+        out_shape=[shaped(extended, F32)] + sends(1, 1, 1),
         scratch_shapes=[pltpu.VMEM(field, F32), inverse_scr, fold_scr, lon_scr] + staging(1) + [quad_sems] + slot_sems,
-        compiler_params=limit(44),
+        compiler_params=limit(36),
         cost_estimate=cost(work),
         name="vertical_second",
     )(pre1, fold_block, *folds1, inverse, sn, mn, depth)
 
-    rims2, folds2 = exchange(*sent2)
-    pre2 = stencil(g2, rims2, rims1)
+    g2, rims2, folds2, (north_c,) = exchange(g2, *sent2, rims1[0])
+    pre2 = stencil(g2, rims2, north_c)
 
     return pl.pallas_call(
         last_kernel,
-        in_specs=[vmem, smem] + [vmem] * 6,
+        in_specs=[vmem, smem] + [vmem] * 5,
         out_specs=hbm,
         out_shape=shaped(field, F32),
         scratch_shapes=[pltpu.VMEM(field, F32), pltpu.SemaphoreType.DMA((3,))],
         compiler_params=limit(4),
         name="add_fold",
-    )(pre2, fold_block, *folds2, rim_c, depth)
+    )(pre2, fold_block, *folds2, depth)
 
 
 def solution(mesh):

time: 82.5 us -> 80.7 us (0.978)
  waiting for transfers between devices: 23.1 us -> 21.4 us
    ppermute x2, waiting for transfers between devices: 8.9 us -> 7.24 us  [exchange(): lax.ppermute(south, 'lat', ring(lats, -1))]
    ppermute x2, waiting for transfers between devices: 10.1 us -> 8.93 us  [exchange(): lax.ppermute(north, 'lat', ring(lats, 1))]
  transfers between devices with their start and end apart: 12 -> 12, of which waited for: 5 -> 6; matrix products, arithmetic and copies ran while one was open for 0% -> 0% of each run, Pallas kernels for 8% -> 8%
where the time goes in v4:
time: 80.7 us; the launch traced here: 80.4 us
  Pallas kernels  31.1 us (39%)
  starting transfers between devices  26.6 us (33%)
  waiting for transfers between devices  21.4 us (27%)
  local copies, waits for them, and re-layouts  1.11 us (1%)
    pallas_call x1, Pallas kernels, per_device(): pl.pallas_call(first_kernel, in_specs=[hbm] * 7, out_specs=[vmem, hbm, vm...  11.5 us
    all_to_all x2, starting transfers between devices, exchange(): near = lax.all_to_all(slots, 'near', 0, 0, tiled=True)  11 us
    pallas_call x1, Pallas kernels, per_device(): pl.pallas_call(second_kernel, in_specs=[vmem, smem] + [vmem] * 4 + [hbm]...  9.7 us
    ppermute x6, starting transfers between devices, exchange(): lax.ppermute(part, lon, ring(count, NEAR * (step + 1)))  9.07 us
    ppermute x2, waiting for transfers between devices, exchange(): lax.ppermute(north, 'lat', ring(lats, 1))  8.93 us
    ppermute x2, waiting for transfers between devices, exchange(): lax.ppermute(south, 'lat', ring(lats, -1))  7.24 us
    pallas_call x2, Pallas kernels, stencil(): pl.pallas_call(transposed_h, in_specs=[vmem] * 9, out_specs=vmem, out_sha...  6.71 us
    ppermute x2, starting transfers between devices, exchange(): lax.ppermute(south, 'lat', ring(lats, -1))  6.48 us
  transfers between devices with their start and end apart: 12, of which 6 were waited for; matrix products, arithmetic and copies ran while one was open for 0% of the time, Pallas kernels for 8%

profile of v4, /device:TPU:0, one launch (start us, length us, event | category | flops | bytes accessed | tf_op | source)
XLA Modules:
  0.0 80.4 jit_solution(17407958681423243145)
XLA Ops:
  0.0 11.5 %vertical_first.1 = (f32[81,8,256]{2,1,0:T(8,128)}, bf16[8,22,8,256]{3,2,1,0:T(8,128)(2,1)}, bf16[2,19,8,256]{3,2,1,0:T(8,128)(2,1)}, bf16[1,19,8,256]{3,2,1,0:T(8,128)(2,1)}) custom-call(f32[75,8,256]{2,1,0:T(8,128)} %lam_hbm.1, bf16[75,75,8,256]{3,2,1,0:T(8,128)(2,1)} %inv_hbm.3, bf16[75,8,256]{2,1,0:T(8,128)(2,1)} %se_ref.3, bf16[75,8,256]{2,1,0:T(8,128)(2,1)} %me_ref.3, ...), custom_call_target="tpu_custom_call" | custom-call | flops 23040000 | bytes 23040000 | tf_op jit(solution)/shard_map/vertical_first/pallas_call | solution.py:499
  11.5 6.4 %all-to-all-start = ((bf16[8,22,8,256]{3,2,1,0:T(8,128)(2,1)}), bf16[8,22,8,256]{3,2,1,0:T(8,128)(2,1)S(1)}, u32[]{:S(2)}, u32[]{:S(2)}) async-start(bf16[8,22,8,256]{3,2,1,0:T(8,128)(2,1)} %get-tuple-element.26), calls=%async_computation | async-start | bytes 1441792 | tf_op jit(solution)/shard_map/all_to_all | solution.py:516
  17.9 3.2 %collective-permute-start.1 = (bf16[1,19,8,256]{3,2,1,0:T(8,128)(2,1)}, bf16[1,19,8,256]{3,2,1,0:T(8,128)(2,1)S(1)}, u32[]{:S(2)}, u32[]{:S(2)}) collective-permute-start(bf16[1,19,8,256]{3,2,1,0:T(8,128)(2,1)} %get-tuple-element.29), channel_id=1, source_target_pairs={{0,3},{1,0},{2,1},{3,2},{4,7},{5,4},{6,5},{7,6},{8,11},{9,8},{10,9... | collective-permute-start | bytes 233480 | tf_op jit(solution)/shard_map/ppermute | solution.py:517
  21.1 7.2 %collective-permute-done.1.refs_2_ = bf16[1,19,8,256]{3,2,1,0:T(8,128)(2,1)S(1)} collective-permute-done((bf16[1,19,8,256]{3,2,1,0:T(8,128)(2,1)}, bf16[1,19,8,256]{3,2,1,0:T(8,128)(2,1)S(1)}, u32[]{:S(2)}, u32[]{:S(2)}) %collective-permute-start.1) | collective-permute-done | bytes 77856 | tf_op jit(solution)/shard_map/ppermute | solution.py:517
  28.3 3.6 %collective-permute-done.refs_1_ = bf16[2,19,8,256]{3,2,1,0:T(8,128)(2,1)S(1)} collective-permute-done((bf16[2,19,8,256]{3,2,1,0:T(8,128)(2,1)}, bf16[2,19,8,256]{3,2,1,0:T(8,128)(2,1)S(1)}, u32[]{:S(2)}, u32[]{:S(2)}) %collective-permute-start) | collective-permute-done | bytes 155680 | tf_op jit(solution)/shard_map/ppermute | solution.py:517
  31.9 1.1 %copy-done.4 = f32[81,8,256]{2,1,0:T(8,128)S(1)} copy-done((f32[81,8,256]{2,1,0:T(8,128)S(1)}, f32[81,8,256]{2,1,0:T(8,128)}, u32[]{:S(2)}) %copy-start.4) | copy-done | bytes 663576
  33.0 0.6 relay.2
  33.6 1.6 %collective-permute-start.2 = (bf16[22,8,256]{2,1,0:T(8,128)(2,1)S(1)}, bf16[22,8,256]{2,1,0:T(8,128)(2,1)S(1)}, u32[]{:S(2)}, u32[]{:S(2)}) collective-permute-start(bf16[22,8,256]{2,1,0:T(8,128)(2,1)S(1)} %get-tuple-element.33), channel_id=1, source_target_pairs={{0,32},{4,36},{8,40},{12,44},{16,48},{20,52},{24,56},{28,60},{32,6... | collective-permute-start | bytes 270344 | tf_op jit(solution)/shard_map/ppermute | solution.py:532
  35.2 1.7 %collective-permute-start.4 = (bf16[22,8,256]{2,1,0:T(8,128)(2,1)S(1)}, bf16[22,8,256]{2,1,0:T(8,128)(2,1)S(1)}, u32[]{:S(2)}, u32[]{:S(2)}) collective-permute-start(bf16[22,8,256]{2,1,0:T(8,128)(2,1)S(1)} %get-tuple-element.35), channel_id=1, source_target_pairs={{0,96},{4,100},{8,104},{12,108},{16,112},{20,116},{24,120},{28,124... | collective-permute-start | bytes 270344 | tf_op jit(solution)/shard_map/ppermute | solution.py:532
  36.9 2.0 %collective-permute-start.3 = (bf16[19,8,256]{2,1,0:T(8,128)(2,1)S(1)}, bf16[19,8,256]{2,1,0:T(8,128)(2,1)S(1)}, u32[]{:S(2)}, u32[]{:S(2)}) collective-permute-start(bf16[19,8,256]{2,1,0:T(8,128)(2,1)S(1)} %get-tuple-element.34), channel_id=1, source_target_pairs={{0,64},{4,68},{8,72},{12,76},{16,80},{20,84},{24,88},{28,92},{32,9... | collective-permute-start | bytes 233480 | tf_op jit(solution)/shard_map/ppermute | solution.py:532
  38.9 3.4 %horizontal.2.pre_ref = f32[81,8,256]{2,1,0:T(8,128)S(1)} custom-call(f32[81,8,256]{2,1,0:T(8,128)S(1)} %get-tuple-element.30.g_ref, bf16[75,8,256]{2,1,0:T(8,128)(2,1)S(1)} %copy-done.2, bf16[75,8,256]{2,1,0:T(8,128)(2,1)S(1)} %copy-done.3, bf16[75,8,256]{2,1,0:T(8,128)(2,1)S(1)} %copy-done, bf16[75,8,256]{2,1,0:T(8,128)(2,1)S(1)} %copy-done.1, ...), custom_call_target="tpu_custom_call" | custom-call | flops 23040000 | bytes 23040000 | tf_op jit(solution)/shard_map/horizontal/pallas_call | solution.py:536
  42.3 0.5 collective-permute-done.3.far2_ref
  42.8 9.7 %vertical_second.1 = (f32[81,8,256]{2,1,0:T(8,128)S(1)}, bf16[8,20,8,256]{3,2,1,0:T(8,128)(2,1)}, bf16[1,19,8,256]{3,2,1,0:T(8,128)(2,1)S(1)}, bf16[1,19,8,256]{3,2,1,0:T(8,128)(2,1)S(1)}) custom-call(f32[81,8,256]{2,1,0:T(8,128)S(1)} %horizontal.2.pre_ref, s32[32]{0:T(128)S(1)} %copy-done.6, bf16[8,22,8,256]{3,2,1,0:T(8,128)(2,1)S(1)} %all-to-all-done.near_ref, ...), custom_call_target="tpu_custom_call" | custom-call | flops 23040000 | bytes 23040000 | tf_op jit(solution)/shard_map/vertical_second/pallas_call | solution.py:549
  52.5 4.7 %all-to-all-start.1 = ((bf16[8,20,8,256]{3,2,1,0:T(8,128)(2,1)}), bf16[8,20,8,256]{3,2,1,0:T(8,128)(2,1)S(1)}, u32[]{:S(2)}, u32[]{:S(2)}) async-start(bf16[8,20,8,256]{3,2,1,0:T(8,128)(2,1)} %get-tuple-element.36), calls=%async_computation.1 | async-start | bytes 1310720 | tf_op jit(solution)/shard_map/all_to_all | solution.py:516
  57.2 3.2 %collective-permute-start.6 = (bf16[1,19,8,256]{3,2,1,0:T(8,128)(2,1)S(1)}, bf16[1,19,8,256]{3,2,1,0:T(8,128)(2,1)S(1)}, u32[]{:S(2)}, u32[]{:S(2)}) collective-permute-start(bf16[1,19,8,256]{3,2,1,0:T(8,128)(2,1)S(1)} %get-tuple-element.39), channel_id=1, source_target_pairs={{0,3},{1,0},{2,1},{3,2},{4,7},{5,4},{6,5},{7,6},{8,11},{9,8},{10,9... | collective-permute-start | bytes 233480 | tf_op jit(solution)/shard_map/ppermute | solution.py:517
  60.4 5.3 %collective-permute-done.5.refs_1_ = bf16[1,19,8,256]{3,2,1,0:T(8,128)(2,1)S(1)} collective-permute-done((bf16[1,19,8,256]{3,2,1,0:T(8,128)(2,1)S(1)}, bf16[1,19,8,256]{3,2,1,0:T(8,128)(2,1)S(1)}, u32[]{:S(2)}, u32[]{:S(2)}) %collective-permute-start.5) | collective-permute-done | bytes 77856 | tf_op jit(solution)/shard_map/ppermute | solution.py:517
  65.8 2.7 %all-to-all-done.1.near_ref = bf16[8,20,8,256]{3,2,1,0:T(8,128)(2,1)S(1)} async-done(((bf16[8,20,8,256]{3,2,1,0:T(8,128)(2,1)}), bf16[8,20,8,256]{3,2,1,0:T(8,128)(2,1)S(1)}, u32[]{:S(2)}, u32[]{:S(2)}) %all-to-all-start.1) | async-done | bytes 655392 | tf_op jit(solution)/shard_map/all_to_all | solution.py:516
  68.5 0.6 relay.3
  69.0 0.7 collective-permute-start.7
  69.8 2.6 %collective-permute-start.9 = (bf16[20,8,256]{2,1,0:T(8,128)(2,1)S(1)}, bf16[20,8,256]{2,1,0:T(8,128)(2,1)S(1)}, u32[]{:S(2)}, u32[]{:S(2)}) collective-permute-start(bf16[20,8,256]{2,1,0:T(8,128)(2,1)S(1)} %get-tuple-element.46), channel_id=1, source_target_pairs={{0,96},{4,100},{8,104},{12,108},{16,112},{20,116},{24,120},{28,124... | collective-permute-start | bytes 245768 | tf_op jit(solution)/shard_map/ppermute | solution.py:532
  72.3 0.5 collective-permute-start.8
  72.8 3.4 %horizontal.3.pre_ref = f32[81,8,256]{2,1,0:T(8,128)S(1)} custom-call(f32[81,8,256]{2,1,0:T(8,128)S(1)} %get-tuple-element.40.g_ref, bf16[75,8,256]{2,1,0:T(8,128)(2,1)S(1)} %copy-done.2, bf16[75,8,256]{2,1,0:T(8,128)(2,1)S(1)} %copy-done.3, bf16[75,8,256]{2,1,0:T(8,128)(2,1)S(1)} %copy-done, bf16[75,8,256]{2,1,0:T(8,128)(2,1)S(1)} %copy-done.1, ...), custom_call_target="tpu_custom_call" | custom-call | flops 23040000 | bytes 23040000 | tf_op jit(solution)/shard_map/horizontal/pallas_call | solution.py:536
  76.2 2.1 %collective-permute-done.8.far2_ref = bf16[19,8,256]{2,1,0:T(8,128)(2,1)S(1)} collective-permute-done((bf16[19,8,256]{2,1,0:T(8,128)(2,1)S(1)}, bf16[19,8,256]{2,1,0:T(8,128)(2,1)S(1)}, u32[]{:S(2)}, u32[]{:S(2)}) %collective-permute-start.8) | collective-permute-done | bytes 77856 | tf_op jit(solution)/shard_map/ppermute | solution.py:532
  78.2 2.1 %add_fold.1 = f32[75,8,256]{2,1,0:T(8,128)} custom-call(f32[81,8,256]{2,1,0:T(8,128)S(1)} %horizontal.3.pre_ref, s32[32]{0:T(128)S(1)} %copy-done.6, bf16[8,20,8,256]{3,2,1,0:T(8,128)(2,1)S(1)} %all-to-all-done.1.near_ref, bf16[20,8,256]{2,1,0:T(8,128)(2,1)S(1)} %collective-permute-done.7.far1_ref, bf16[19,8,256]{2,1,0:T(8,128)(2,1)S(1)} %collective-permute-done.8.far2_ref, ...), custom_call_target="tpu_custom_call" | custom-call | tf_op jit(solution)/shard_map/add_fold/pallas_call | solution.py:563
  (21 shorter events, 0.0 us)
Async XLA Ops:
  0.0 38.9 %copy-start.5 = (s32[8,256]{1,0:T(8,128)S(1)}, s32[8,256]{1,0:T(8,128)}, u32[]{:S(2)}) copy-start(s32[8,256]{1,0:T(8,128)} %depth_ref.7) | copy-start | bytes 24580
  0.0 38.9 %copy-start.1 = (bf16[75,8,256]{2,1,0:T(8,128)(2,1)S(1)}, bf16[75,8,256]{2,1,0:T(8,128)(2,1)}, u32[]{:S(2)}) copy-start(bf16[75,8,256]{2,1,0:T(8,128)(2,1)} %mn_ref.5) | copy-start | bytes 921604
  0.0 38.9 %copy-start = (bf16[75,8,256]{2,1,0:T(8,128)(2,1)S(1)}, bf16[75,8,256]{2,1,0:T(8,128)(2,1)}, u32[]{:S(2)}) copy-start(bf16[75,8,256]{2,1,0:T(8,128)(2,1)} %sn_ref.5) | copy-start | bytes 921604
  0.0 38.9 %copy-start.3 = (bf16[75,8,256]{2,1,0:T(8,128)(2,1)S(1)}, bf16[75,8,256]{2,1,0:T(8,128)(2,1)}, u32[]{:S(2)}) copy-start(bf16[75,8,256]{2,1,0:T(8,128)(2,1)} %me_ref.3) | copy-start | bytes 921604
  0.0 38.9 %copy-start.2 = (bf16[75,8,256]{2,1,0:T(8,128)(2,1)S(1)}, bf16[75,8,256]{2,1,0:T(8,128)(2,1)}, u32[]{:S(2)}) copy-start(bf16[75,8,256]{2,1,0:T(8,128)(2,1)} %se_ref.3) | copy-start | bytes 921604
  0.0 31.9 %copy-start.6 = (s32[32]{0:T(128)S(1)}, s32[32]{0:T(128)}, u32[]{:S(2)}) copy-start(s32[32]{0:T(128)} %fold_ref.7) | copy-start | bytes 388
  11.5 20.4 %all-to-all-start = ((bf16[8,22,8,256]{3,2,1,0:T(8,128)(2,1)}), bf16[8,22,8,256]{3,2,1,0:T(8,128)(2,1)S(1)}, u32[]{:S(2)}, u32[]{:S(2)}) async-start(bf16[8,22,8,256]{3,2,1,0:T(8,128)(2,1)} %get-tuple-element.26), calls=%async_computation | async-start | bytes 1441792 | tf_op jit(solution)/shard_map/all_to_all | solution.py:516
  17.9 14.1 %collective-permute-start = (bf16[2,19,8,256]{3,2,1,0:T(8,128)(2,1)}, bf16[2,19,8,256]{3,2,1,0:T(8,128)(2,1)S(1)}, u32[]{:S(2)}, u32[]{:S(2)}) collective-permute-start(bf16[2,19,8,256]{3,2,1,0:T(8,128)(2,1)} %get-tuple-element.28), channel_id=1, source_target_pairs={{0,1},{1,2},{2,3},{3,0},{4,5},{5,6},{6,7},{7,4},{8,9},{9,10},{10,1... | collective-permute-start | bytes 466952 | tf_op jit(solution)/shard_map/ppermute | solution.py:517
  17.9 10.5 %collective-permute-start.1 = (bf16[1,19,8,256]{3,2,1,0:T(8,128)(2,1)}, bf16[1,19,8,256]{3,2,1,0:T(8,128)(2,1)S(1)}, u32[]{:S(2)}, u32[]{:S(2)}) collective-permute-start(bf16[1,19,8,256]{3,2,1,0:T(8,128)(2,1)} %get-tuple-element.29), channel_id=1, source_target_pairs={{0,3},{1,0},{2,1},{3,2},{4,7},{5,4},{6,5},{7,6},{8,11},{9,8},{10,9... | collective-permute-start | bytes 233480 | tf_op jit(solution)/shard_map/ppermute | solution.py:517
  31.9 1.1 %copy-start.4 = (f32[81,8,256]{2,1,0:T(8,128)S(1)}, f32[81,8,256]{2,1,0:T(8,128)}, u32[]{:S(2)}) copy-start(f32[81,8,256]{2,1,0:T(8,128)} %get-tuple-element.27.refs_0_) | copy-start | bytes 1990660
  33.6 9.2 %collective-permute-start.2 = (bf16[22,8,256]{2,1,0:T(8,128)(2,1)S(1)}, bf16[22,8,256]{2,1,0:T(8,128)(2,1)S(1)}, u32[]{:S(2)}, u32[]{:S(2)}) collective-permute-start(bf16[22,8,256]{2,1,0:T(8,128)(2,1)S(1)} %get-tuple-element.33), channel_id=1, source_target_pairs={{0,32},{4,36},{8,40},{12,44},{16,48},{20,52},{24,56},{28,60},{32,6... | collective-permute-start | bytes 270344 | tf_op jit(solution)/shard_map/ppermute | solution.py:532
  35.2 7.6 %collective-permute-start.4 = (bf16[22,8,256]{2,1,0:T(8,128)(2,1)S(1)}, bf16[22,8,256]{2,1,0:T(8,128)(2,1)S(1)}, u32[]{:S(2)}, u32[]{:S(2)}) collective-permute-start(bf16[22,8,256]{2,1,0:T(8,128)(2,1)S(1)} %get-tuple-element.35), channel_id=1, source_target_pairs={{0,96},{4,100},{8,104},{12,108},{16,112},{20,116},{24,120},{28,124... | collective-permute-start | bytes 270344 | tf_op jit(solution)/shard_map/ppermute | solution.py:532
  36.9 5.9 %collective-permute-start.3 = (bf16[19,8,256]{2,1,0:T(8,128)(2,1)S(1)}, bf16[19,8,256]{2,1,0:T(8,128)(2,1)S(1)}, u32[]{:S(2)}, u32[]{:S(2)}) collective-permute-start(bf16[19,8,256]{2,1,0:T(8,128)(2,1)S(1)} %get-tuple-element.34), channel_id=1, source_target_pairs={{0,64},{4,68},{8,72},{12,76},{16,80},{20,84},{24,88},{28,92},{32,9... | collective-permute-start | bytes 233480 | tf_op jit(solution)/shard_map/ppermute | solution.py:532
  52.5 15.9 %all-to-all-start.1 = ((bf16[8,20,8,256]{3,2,1,0:T(8,128)(2,1)}), bf16[8,20,8,256]{3,2,1,0:T(8,128)(2,1)S(1)}, u32[]{:S(2)}, u32[]{:S(2)}) async-start(bf16[8,20,8,256]{3,2,1,0:T(8,128)(2,1)} %get-tuple-element.36), calls=%async_computation.1 | async-start | bytes 1310720 | tf_op jit(solution)/shard_map/all_to_all | solution.py:516
  57.2 8.6 %collective-permute-start.5 = (bf16[1,19,8,256]{3,2,1,0:T(8,128)(2,1)S(1)}, bf16[1,19,8,256]{3,2,1,0:T(8,128)(2,1)S(1)}, u32[]{:S(2)}, u32[]{:S(2)}) collective-permute-start(bf16[1,19,8,256]{3,2,1,0:T(8,128)(2,1)S(1)} %get-tuple-element.38), channel_id=1, source_target_pairs={{0,1},{1,2},{2,3},{3,0},{4,5},{5,6},{6,7},{7,4},{8,9},{9,10},{10,1... | collective-permute-start | bytes 233480 | tf_op jit(solution)/shard_map/ppermute | solution.py:517
  57.2 8.6 %collective-permute-start.6 = (bf16[1,19,8,256]{3,2,1,0:T(8,128)(2,1)S(1)}, bf16[1,19,8,256]{3,2,1,0:T(8,128)(2,1)S(1)}, u32[]{:S(2)}, u32[]{:S(2)}) collective-permute-start(bf16[1,19,8,256]{3,2,1,0:T(8,128)(2,1)S(1)} %get-tuple-element.39), channel_id=1, source_target_pairs={{0,3},{1,0},{2,1},{3,2},{4,7},{5,4},{6,5},{7,6},{8,11},{9,8},{10,9... | collective-permute-start | bytes 233480 | tf_op jit(solution)/shard_map/ppermute | solution.py:517
  69.0 9.2 %collective-permute-start.7 = (bf16[20,8,256]{2,1,0:T(8,128)(2,1)S(1)}, bf16[20,8,256]{2,1,0:T(8,128)(2,1)S(1)}, u32[]{:S(2)}, u32[]{:S(2)}) collective-permute-start(bf16[20,8,256]{2,1,0:T(8,128)(2,1)S(1)} %get-tuple-element.44), channel_id=1, source_target_pairs={{0,32},{4,36},{8,40},{12,44},{16,48},{20,52},{24,56},{28,60},{32,6... | collective-permute-start | bytes 245768 | tf_op jit(solution)/shard_map/ppermute | solution.py:532
  69.8 8.5 %collective-permute-start.9 = (bf16[20,8,256]{2,1,0:T(8,128)(2,1)S(1)}, bf16[20,8,256]{2,1,0:T(8,128)(2,1)S(1)}, u32[]{:S(2)}, u32[]{:S(2)}) collective-permute-start(bf16[20,8,256]{2,1,0:T(8,128)(2,1)S(1)} %get-tuple-element.46), channel_id=1, source_target_pairs={{0,96},{4,100},{8,104},{12,108},{16,112},{20,116},{24,120},{28,124... | collective-permute-start | bytes 245768 | tf_op jit(solution)/shard_map/ppermute | solution.py:532
  72.3 5.9 %collective-permute-start.8 = (bf16[19,8,256]{2,1,0:T(8,128)(2,1)S(1)}, bf16[19,8,256]{2,1,0:T(8,128)(2,1)S(1)}, u32[]{:S(2)}, u32[]{:S(2)}) collective-permute-start(bf16[19,8,256]{2,1,0:T(8,128)(2,1)S(1)} %get-tuple-element.45), channel_id=1, source_target_pairs={{0,64},{4,68},{8,72},{12,76},{16,80},{20,84},{24,88},{28,92},{32,9... | collective-permute-start | bytes 233480 | tf_op jit(solution)/shard_map/ppermute | solution.py:532

commit v5 on v4

--- a/solution.py
+++ b/solution.py
@@ -13,7 +13,7 @@
 HALF = 128
 QUADS = 19
 FULL_QUADS = 18
-AHEAD = 4
+AHEAD = 5
 TOGETHER = 6
 NEAR = 8
 OWN = LEV + 3

time: 80.7 us -> 80.5 us (level)
  no operation moved by 1% of the time
where the time goes in v5:
time: 80.5 us; the launch traced here: 80.2 us
  Pallas kernels  31 us (39%)
  starting transfers between devices  26.6 us (33%)
  waiting for transfers between devices  21.4 us (27%)
  local copies, waits for them, and re-layouts  1.11 us (1%)
    pallas_call x1, Pallas kernels, per_device(): pl.pallas_call(first_kernel, in_specs=[hbm] * 7, out_specs=[vmem, hbm, vm...  11.4 us
    all_to_all x2, starting transfers between devices, exchange(): near = lax.all_to_all(slots, 'near', 0, 0, tiled=True)  11 us
    pallas_call x1, Pallas kernels, per_device(): pl.pallas_call(second_kernel, in_specs=[vmem, smem] + [vmem] * 4 + [hbm]...  9.63 us
    ppermute x6, starting transfers between devices, exchange(): lax.ppermute(part, lon, ring(count, NEAR * (step + 1)))  9.07 us
    ppermute x2, waiting for transfers between devices, exchange(): lax.ppermute(north, 'lat', ring(lats, 1))  8.91 us
    ppermute x2, waiting for transfers between devices, exchange(): lax.ppermute(south, 'lat', ring(lats, -1))  7.24 us
    pallas_call x2, Pallas kernels, stencil(): pl.pallas_call(transposed_h, in_specs=[vmem] * 9, out_specs=vmem, out_sha...  6.71 us
    ppermute x2, starting transfers between devices, exchange(): lax.ppermute(south, 'lat', ring(lats, -1))  6.48 us
  transfers between devices with their start and end apart: 12, of which 6 were waited for; matrix products, arithmetic and copies ran while one was open for 0% of the time, Pallas kernels for 8%

profile of v5, /device:TPU:0, one launch (start us, length us, event | category | flops | bytes accessed | tf_op | source)
XLA Modules:
  0.0 80.2 jit_solution(8850598652496352105)
XLA Ops:
  0.0 11.4 %vertical_first.1 = (f32[81,8,256]{2,1,0:T(8,128)}, bf16[8,22,8,256]{3,2,1,0:T(8,128)(2,1)}, bf16[2,19,8,256]{3,2,1,0:T(8,128)(2,1)}, bf16[1,19,8,256]{3,2,1,0:T(8,128)(2,1)}) custom-call(f32[75,8,256]{2,1,0:T(8,128)} %lam_hbm.1, bf16[75,75,8,256]{3,2,1,0:T(8,128)(2,1)} %inv_hbm.3, bf16[75,8,256]{2,1,0:T(8,128)(2,1)} %se_ref.3, bf16[75,8,256]{2,1,0:T(8,128)(2,1)} %me_ref.3, ...), custom_call_target="tpu_custom_call" | custom-call | flops 23040000 | bytes 23040000 | tf_op jit(solution)/shard_map/vertical_first/pallas_call | solution.py:499
  11.4 6.4 %all-to-all-start = ((bf16[8,22,8,256]{3,2,1,0:T(8,128)(2,1)}), bf16[8,22,8,256]{3,2,1,0:T(8,128)(2,1)S(1)}, u32[]{:S(2)}, u32[]{:S(2)}) async-start(bf16[8,22,8,256]{3,2,1,0:T(8,128)(2,1)} %get-tuple-element.26), calls=%async_computation | async-start | bytes 1441792 | tf_op jit(solution)/shard_map/all_to_all | solution.py:516
  17.8 3.2 %collective-permute-start.1 = (bf16[1,19,8,256]{3,2,1,0:T(8,128)(2,1)}, bf16[1,19,8,256]{3,2,1,0:T(8,128)(2,1)S(1)}, u32[]{:S(2)}, u32[]{:S(2)}) collective-permute-start(bf16[1,19,8,256]{3,2,1,0:T(8,128)(2,1)} %get-tuple-element.29), channel_id=1, source_target_pairs={{0,3},{1,0},{2,1},{3,2},{4,7},{5,4},{6,5},{7,6},{8,11},{9,8},{10,9... | collective-permute-start | bytes 233480 | tf_op jit(solution)/shard_map/ppermute | solution.py:517
  21.0 7.2 %collective-permute-done.1.refs_2_ = bf16[1,19,8,256]{3,2,1,0:T(8,128)(2,1)S(1)} collective-permute-done((bf16[1,19,8,256]{3,2,1,0:T(8,128)(2,1)}, bf16[1,19,8,256]{3,2,1,0:T(8,128)(2,1)S(1)}, u32[]{:S(2)}, u32[]{:S(2)}) %collective-permute-start.1) | collective-permute-done | bytes 77856 | tf_op jit(solution)/shard_map/ppermute | solution.py:517
  28.2 3.6 %collective-permute-done.refs_1_ = bf16[2,19,8,256]{3,2,1,0:T(8,128)(2,1)S(1)} collective-permute-done((bf16[2,19,8,256]{3,2,1,0:T(8,128)(2,1)}, bf16[2,19,8,256]{3,2,1,0:T(8,128)(2,1)S(1)}, u32[]{:S(2)}, u32[]{:S(2)}) %collective-permute-start) | collective-permute-done | bytes 155680 | tf_op jit(solution)/shard_map/ppermute | solution.py:517
  31.8 1.1 %copy-done.4 = f32[81,8,256]{2,1,0:T(8,128)S(1)} copy-done((f32[81,8,256]{2,1,0:T(8,128)S(1)}, f32[81,8,256]{2,1,0:T(8,128)}, u32[]{:S(2)}) %copy-start.4) | copy-done | bytes 663576
  32.9 0.6 relay.2
  33.5 1.6 %collective-permute-start.2 = (bf16[22,8,256]{2,1,0:T(8,128)(2,1)S(1)}, bf16[22,8,256]{2,1,0:T(8,128)(2,1)S(1)}, u32[]{:S(2)}, u32[]{:S(2)}) collective-permute-start(bf16[22,8,256]{2,1,0:T(8,128)(2,1)S(1)} %get-tuple-element.33), channel_id=1, source_target_pairs={{0,32},{4,36},{8,40},{12,44},{16,48},{20,52},{24,56},{28,60},{32,6... | collective-permute-start | bytes 270344 | tf_op jit(solution)/shard_map/ppermute | solution.py:532
  35.1 1.7 %collective-permute-start.4 = (bf16[22,8,256]{2,1,0:T(8,128)(2,1)S(1)}, bf16[22,8,256]{2,1,0:T(8,128)(2,1)S(1)}, u32[]{:S(2)}, u32[]{:S(2)}) collective-permute-start(bf16[22,8,256]{2,1,0:T(8,128)(2,1)S(1)} %get-tuple-element.35), channel_id=1, source_target_pairs={{0,96},{4,100},{8,104},{12,108},{16,112},{20,116},{24,120},{28,124... | collective-permute-start | bytes 270344 | tf_op jit(solution)/shard_map/ppermute | solution.py:532
  36.8 2.0 %collective-permute-start.3 = (bf16[19,8,256]{2,1,0:T(8,128)(2,1)S(1)}, bf16[19,8,256]{2,1,0:T(8,128)(2,1)S(1)}, u32[]{:S(2)}, u32[]{:S(2)}) collective-permute-start(bf16[19,8,256]{2,1,0:T(8,128)(2,1)S(1)} %get-tuple-element.34), channel_id=1, source_target_pairs={{0,64},{4,68},{8,72},{12,76},{16,80},{20,84},{24,88},{28,92},{32,9... | collective-permute-start | bytes 233480 | tf_op jit(solution)/shard_map/ppermute | solution.py:532
  38.8 3.4 %horizontal.2.pre_ref = f32[81,8,256]{2,1,0:T(8,128)S(1)} custom-call(f32[81,8,256]{2,1,0:T(8,128)S(1)} %get-tuple-element.30.g_ref, bf16[75,8,256]{2,1,0:T(8,128)(2,1)S(1)} %copy-done.2, bf16[75,8,256]{2,1,0:T(8,128)(2,1)S(1)} %copy-done.3, bf16[75,8,256]{2,1,0:T(8,128)(2,1)S(1)} %copy-done, bf16[75,8,256]{2,1,0:T(8,128)(2,1)S(1)} %copy-done.1, ...), custom_call_target="tpu_custom_call" | custom-call | flops 23040000 | bytes 23040000 | tf_op jit(solution)/shard_map/horizontal/pallas_call | solution.py:536
  42.2 0.5 collective-permute-done.3.far2_ref
  42.7 9.6 %vertical_second.1 = (f32[81,8,256]{2,1,0:T(8,128)S(1)}, bf16[8,20,8,256]{3,2,1,0:T(8,128)(2,1)}, bf16[1,19,8,256]{3,2,1,0:T(8,128)(2,1)S(1)}, bf16[1,19,8,256]{3,2,1,0:T(8,128)(2,1)S(1)}) custom-call(f32[81,8,256]{2,1,0:T(8,128)S(1)} %horizontal.2.pre_ref, s32[32]{0:T(128)S(1)} %copy-done.6, bf16[8,22,8,256]{3,2,1,0:T(8,128)(2,1)S(1)} %all-to-all-done.near_ref, ...), custom_call_target="tpu_custom_call" | custom-call | flops 23040000 | bytes 23040000 | tf_op jit(solution)/shard_map/vertical_second/pallas_call | solution.py:549
  52.3 4.7 %all-to-all-start.1 = ((bf16[8,20,8,256]{3,2,1,0:T(8,128)(2,1)}), bf16[8,20,8,256]{3,2,1,0:T(8,128)(2,1)S(1)}, u32[]{:S(2)}, u32[]{:S(2)}) async-start(bf16[8,20,8,256]{3,2,1,0:T(8,128)(2,1)} %get-tuple-element.36), calls=%async_computation.1 | async-start | bytes 1310720 | tf_op jit(solution)/shard_map/all_to_all | solution.py:516
  57.0 3.2 %collective-permute-start.6 = (bf16[1,19,8,256]{3,2,1,0:T(8,128)(2,1)S(1)}, bf16[1,19,8,256]{3,2,1,0:T(8,128)(2,1)S(1)}, u32[]{:S(2)}, u32[]{:S(2)}) collective-permute-start(bf16[1,19,8,256]{3,2,1,0:T(8,128)(2,1)S(1)} %get-tuple-element.39), channel_id=1, source_target_pairs={{0,3},{1,0},{2,1},{3,2},{4,7},{5,4},{6,5},{7,6},{8,11},{9,8},{10,9... | collective-permute-start | bytes 233480 | tf_op jit(solution)/shard_map/ppermute | solution.py:517
  60.3 5.3 %collective-permute-done.5.refs_1_ = bf16[1,19,8,256]{3,2,1,0:T(8,128)(2,1)S(1)} collective-permute-done((bf16[1,19,8,256]{3,2,1,0:T(8,128)(2,1)S(1)}, bf16[1,19,8,256]{3,2,1,0:T(8,128)(2,1)S(1)}, u32[]{:S(2)}, u32[]{:S(2)}) %collective-permute-start.5) | collective-permute-done | bytes 77856 | tf_op jit(solution)/shard_map/ppermute | solution.py:517
  65.6 2.7 %all-to-all-done.1.near_ref = bf16[8,20,8,256]{3,2,1,0:T(8,128)(2,1)S(1)} async-done(((bf16[8,20,8,256]{3,2,1,0:T(8,128)(2,1)}), bf16[8,20,8,256]{3,2,1,0:T(8,128)(2,1)S(1)}, u32[]{:S(2)}, u32[]{:S(2)}) %all-to-all-start.1) | async-done | bytes 655392 | tf_op jit(solution)/shard_map/all_to_all | solution.py:516
  68.3 0.6 relay.3
  68.8 0.7 collective-permute-start.7
  69.6 2.6 %collective-permute-start.9 = (bf16[20,8,256]{2,1,0:T(8,128)(2,1)S(1)}, bf16[20,8,256]{2,1,0:T(8,128)(2,1)S(1)}, u32[]{:S(2)}, u32[]{:S(2)}) collective-permute-start(bf16[20,8,256]{2,1,0:T(8,128)(2,1)S(1)} %get-tuple-element.46), channel_id=1, source_target_pairs={{0,96},{4,100},{8,104},{12,108},{16,112},{20,116},{24,120},{28,124... | collective-permute-start | bytes 245768 | tf_op jit(solution)/shard_map/ppermute | solution.py:532
  72.1 0.5 collective-permute-start.8
  72.6 3.4 %horizontal.3.pre_ref = f32[81,8,256]{2,1,0:T(8,128)S(1)} custom-call(f32[81,8,256]{2,1,0:T(8,128)S(1)} %get-tuple-element.40.g_ref, bf16[75,8,256]{2,1,0:T(8,128)(2,1)S(1)} %copy-done.2, bf16[75,8,256]{2,1,0:T(8,128)(2,1)S(1)} %copy-done.3, bf16[75,8,256]{2,1,0:T(8,128)(2,1)S(1)} %copy-done, bf16[75,8,256]{2,1,0:T(8,128)(2,1)S(1)} %copy-done.1, ...), custom_call_target="tpu_custom_call" | custom-call | flops 23040000 | bytes 23040000 | tf_op jit(solution)/shard_map/horizontal/pallas_call | solution.py:536
  76.0 2.1 %collective-permute-done.8.far2_ref = bf16[19,8,256]{2,1,0:T(8,128)(2,1)S(1)} collective-permute-done((bf16[19,8,256]{2,1,0:T(8,128)(2,1)S(1)}, bf16[19,8,256]{2,1,0:T(8,128)(2,1)S(1)}, u32[]{:S(2)}, u32[]{:S(2)}) %collective-permute-start.8) | collective-permute-done | bytes 77856 | tf_op jit(solution)/shard_map/ppermute | solution.py:532
  78.1 2.1 %add_fold.1 = f32[75,8,256]{2,1,0:T(8,128)} custom-call(f32[81,8,256]{2,1,0:T(8,128)S(1)} %horizontal.3.pre_ref, s32[32]{0:T(128)S(1)} %copy-done.6, bf16[8,20,8,256]{3,2,1,0:T(8,128)(2,1)S(1)} %all-to-all-done.1.near_ref, bf16[20,8,256]{2,1,0:T(8,128)(2,1)S(1)} %collective-permute-done.7.far1_ref, bf16[19,8,256]{2,1,0:T(8,128)(2,1)S(1)} %collective-permute-done.8.far2_ref, ...), custom_call_target="tpu_custom_call" | custom-call | tf_op jit(solution)/shard_map/add_fold/pallas_call | solution.py:563
  (21 shorter events, 0.0 us)
Async XLA Ops:
  0.0 38.8 %copy-start.5 = (s32[8,256]{1,0:T(8,128)S(1)}, s32[8,256]{1,0:T(8,128)}, u32[]{:S(2)}) copy-start(s32[8,256]{1,0:T(8,128)} %depth_ref.7) | copy-start | bytes 24580
  0.0 38.8 %copy-start.1 = (bf16[75,8,256]{2,1,0:T(8,128)(2,1)S(1)}, bf16[75,8,256]{2,1,0:T(8,128)(2,1)}, u32[]{:S(2)}) copy-start(bf16[75,8,256]{2,1,0:T(8,128)(2,1)} %mn_ref.5) | copy-start | bytes 921604
  0.0 38.8 %copy-start = (bf16[75,8,256]{2,1,0:T(8,128)(2,1)S(1)}, bf16[75,8,256]{2,1,0:T(8,128)(2,1)}, u32[]{:S(2)}) copy-start(bf16[75,8,256]{2,1,0:T(8,128)(2,1)} %sn_ref.5) | copy-start | bytes 921604
  0.0 38.8 %copy-start.3 = (bf16[75,8,256]{2,1,0:T(8,128)(2,1)S(1)}, bf16[75,8,256]{2,1,0:T(8,128)(2,1)}, u32[]{:S(2)}) copy-start(bf16[75,8,256]{2,1,0:T(8,128)(2,1)} %me_ref.3) | copy-start | bytes 921604
  0.0 38.8 %copy-start.2 = (bf16[75,8,256]{2,1,0:T(8,128)(2,1)S(1)}, bf16[75,8,256]{2,1,0:T(8,128)(2,1)}, u32[]{:S(2)}) copy-start(bf16[75,8,256]{2,1,0:T(8,128)(2,1)} %se_ref.3) | copy-start | bytes 921604
  0.0 31.8 %copy-start.6 = (s32[32]{0:T(128)S(1)}, s32[32]{0:T(128)}, u32[]{:S(2)}) copy-start(s32[32]{0:T(128)} %fold_ref.7) | copy-start | bytes 388
  11.4 20.4 %all-to-all-start = ((bf16[8,22,8,256]{3,2,1,0:T(8,128)(2,1)}), bf16[8,22,8,256]{3,2,1,0:T(8,128)(2,1)S(1)}, u32[]{:S(2)}, u32[]{:S(2)}) async-start(bf16[8,22,8,256]{3,2,1,0:T(8,128)(2,1)} %get-tuple-element.26), calls=%async_computation | async-start | bytes 1441792 | tf_op jit(solution)/shard_map/all_to_all | solution.py:516
  17.8 14.1 %collective-permute-start = (bf16[2,19,8,256]{3,2,1,0:T(8,128)(2,1)}, bf16[2,19,8,256]{3,2,1,0:T(8,128)(2,1)S(1)}, u32[]{:S(2)}, u32[]{:S(2)}) collective-permute-start(bf16[2,19,8,256]{3,2,1,0:T(8,128)(2,1)} %get-tuple-element.28), channel_id=1, source_target_pairs={{0,1},{1,2},{2,3},{3,0},{4,5},{5,6},{6,7},{7,4},{8,9},{9,10},{10,1... | collective-permute-start | bytes 466952 | tf_op jit(solution)/shard_map/ppermute | solution.py:517
  17.8 10.5 %collective-permute-start.1 = (bf16[1,19,8,256]{3,2,1,0:T(8,128)(2,1)}, bf16[1,19,8,256]{3,2,1,0:T(8,128)(2,1)S(1)}, u32[]{:S(2)}, u32[]{:S(2)}) collective-permute-start(bf16[1,19,8,256]{3,2,1,0:T(8,128)(2,1)} %get-tuple-element.29), channel_id=1, source_target_pairs={{0,3},{1,0},{2,1},{3,2},{4,7},{5,4},{6,5},{7,6},{8,11},{9,8},{10,9... | collective-permute-start | bytes 233480 | tf_op jit(solution)/shard_map/ppermute | solution.py:517
  31.8 1.1 %copy-start.4 = (f32[81,8,256]{2,1,0:T(8,128)S(1)}, f32[81,8,256]{2,1,0:T(8,128)}, u32[]{:S(2)}) copy-start(f32[81,8,256]{2,1,0:T(8,128)} %get-tuple-element.27.refs_0_) | copy-start | bytes 1990660
  33.5 9.2 %collective-permute-start.2 = (bf16[22,8,256]{2,1,0:T(8,128)(2,1)S(1)}, bf16[22,8,256]{2,1,0:T(8,128)(2,1)S(1)}, u32[]{:S(2)}, u32[]{:S(2)}) collective-permute-start(bf16[22,8,256]{2,1,0:T(8,128)(2,1)S(1)} %get-tuple-element.33), channel_id=1, source_target_pairs={{0,32},{4,36},{8,40},{12,44},{16,48},{20,52},{24,56},{28,60},{32,6... | collective-permute-start | bytes 270344 | tf_op jit(solution)/shard_map/ppermute | solution.py:532
  35.1 7.6 %collective-permute-start.4 = (bf16[22,8,256]{2,1,0:T(8,128)(2,1)S(1)}, bf16[22,8,256]{2,1,0:T(8,128)(2,1)S(1)}, u32[]{:S(2)}, u32[]{:S(2)}) collective-permute-start(bf16[22,8,256]{2,1,0:T(8,128)(2,1)S(1)} %get-tuple-element.35), channel_id=1, source_target_pairs={{0,96},{4,100},{8,104},{12,108},{16,112},{20,116},{24,120},{28,124... | collective-permute-start | bytes 270344 | tf_op jit(solution)/shard_map/ppermute | solution.py:532
  36.8 5.9 %collective-permute-start.3 = (bf16[19,8,256]{2,1,0:T(8,128)(2,1)S(1)}, bf16[19,8,256]{2,1,0:T(8,128)(2,1)S(1)}, u32[]{:S(2)}, u32[]{:S(2)}) collective-permute-start(bf16[19,8,256]{2,1,0:T(8,128)(2,1)S(1)} %get-tuple-element.34), channel_id=1, source_target_pairs={{0,64},{4,68},{8,72},{12,76},{16,80},{20,84},{24,88},{28,92},{32,9... | collective-permute-start | bytes 233480 | tf_op jit(solution)/shard_map/ppermute | solution.py:532
  52.3 15.9 %all-to-all-start.1 = ((bf16[8,20,8,256]{3,2,1,0:T(8,128)(2,1)}), bf16[8,20,8,256]{3,2,1,0:T(8,128)(2,1)S(1)}, u32[]{:S(2)}, u32[]{:S(2)}) async-start(bf16[8,20,8,256]{3,2,1,0:T(8,128)(2,1)} %get-tuple-element.36), calls=%async_computation.1 | async-start | bytes 1310720 | tf_op jit(solution)/shard_map/all_to_all | solution.py:516
  57.0 8.6 %collective-permute-start.5 = (bf16[1,19,8,256]{3,2,1,0:T(8,128)(2,1)S(1)}, bf16[1,19,8,256]{3,2,1,0:T(8,128)(2,1)S(1)}, u32[]{:S(2)}, u32[]{:S(2)}) collective-permute-start(bf16[1,19,8,256]{3,2,1,0:T(8,128)(2,1)S(1)} %get-tuple-element.38), channel_id=1, source_target_pairs={{0,1},{1,2},{2,3},{3,0},{4,5},{5,6},{6,7},{7,4},{8,9},{9,10},{10,1... | collective-permute-start | bytes 233480 | tf_op jit(solution)/shard_map/ppermute | solution.py:517
  57.0 8.6 %collective-permute-start.6 = (bf16[1,19,8,256]{3,2,1,0:T(8,128)(2,1)S(1)}, bf16[1,19,8,256]{3,2,1,0:T(8,128)(2,1)S(1)}, u32[]{:S(2)}, u32[]{:S(2)}) collective-permute-start(bf16[1,19,8,256]{3,2,1,0:T(8,128)(2,1)S(1)} %get-tuple-element.39), channel_id=1, source_target_pairs={{0,3},{1,0},{2,1},{3,2},{4,7},{5,4},{6,5},{7,6},{8,11},{9,8},{10,9... | collective-permute-start | bytes 233480 | tf_op jit(solution)/shard_map/ppermute | solution.py:517
  68.8 9.2 %collective-permute-start.7 = (bf16[20,8,256]{2,1,0:T(8,128)(2,1)S(1)}, bf16[20,8,256]{2,1,0:T(8,128)(2,1)S(1)}, u32[]{:S(2)}, u32[]{:S(2)}) collective-permute-start(bf16[20,8,256]{2,1,0:T(8,128)(2,1)S(1)} %get-tuple-element.44), channel_id=1, source_target_pairs={{0,32},{4,36},{8,40},{12,44},{16,48},{20,52},{24,56},{28,60},{32,6... | collective-permute-start | bytes 245768 | tf_op jit(solution)/shard_map/ppermute | solution.py:532
  69.6 8.5 %collective-permute-start.9 = (bf16[20,8,256]{2,1,0:T(8,128)(2,1)S(1)}, bf16[20,8,256]{2,1,0:T(8,128)(2,1)S(1)}, u32[]{:S(2)}, u32[]{:S(2)}) collective-permute-start(bf16[20,8,256]{2,1,0:T(8,128)(2,1)S(1)} %get-tuple-element.46), channel_id=1, source_target_pairs={{0,96},{4,100},{8,104},{12,108},{16,112},{20,116},{24,120},{28,124... | collective-permute-start | bytes 245768 | tf_op jit(solution)/shard_map/ppermute | solution.py:532
  72.1 5.9 %collective-permute-start.8 = (bf16[19,8,256]{2,1,0:T(8,128)(2,1)S(1)}, bf16[19,8,256]{2,1,0:T(8,128)(2,1)S(1)}, u32[]{:S(2)}, u32[]{:S(2)}) collective-permute-start(bf16[19,8,256]{2,1,0:T(8,128)(2,1)S(1)} %get-tuple-element.45), channel_id=1, source_target_pairs={{0,64},{4,68},{8,72},{12,76},{16,80},{20,84},{24,88},{28,92},{32,9... | collective-permute-start | bytes 233480 | tf_op jit(solution)/shard_map/ppermute | solution.py:532
